TPU v7x, 32 devices: a whole 2x2x4 slice. The times are simulated.
32 devices in a mesh: slab: 8 (over z, x), col: 4 (over y, core).
Axes of the slice: x: 2, y: 2, z: 4, core: 2. Of those that a mesh axis runs over, the one named last changes fastest.
Arguments:
- order_params: float32 [16, 64, 32, 256], P(None, 'slab', 'col'), may hold values from 0 to 0.5
- layer_mask: int32 [64, 32, 256], P('slab', 'col'), may hold values 0 or 1
- coarse_temp: float32 [48, 16, 128], P('slab', 'col'), may hold values from 0.5 to 1.5, as said below
- coarse_rows: int32 [8], replicated, may hold values from 2 to 6, as said below
- grain_ids: int32 [8, 4, 16], replicated, may hold values from 0 to 303, as said below
- energy: float32 [304], replicated, may hold values from 0.5 to 6
Outputs:
- evolved: float32 [16, 64, 32, 256], P(None, 'slab', 'col')
Inputs may be any that keep to these rules, and one draw needn't show every extreme that they name: coarse_rows sums to 32; the s-th block of coarse planes begins within 1 planes of s * 4; some entry equals 6. `coarse_temp`: rows of one index of slab past its entry of coarse_rows are not part of the field. `grain_ids`: the 16 ids of a block are distinct; a block shares exactly 4 ids with each block beside it along slab and along col and none with any other block.
All inputs are finite; a program needn't handle non-finite values. No bound on the sum of `layer_mask` on one device may be relied on, other than what follows from the above.
Results may differ from a plain program's by a relative error of at most 0.0001.
Values sent between devices are 32-bit elements; how exact they have to be, the bound alone decides.
No kernel may reach another device: no remote copies, remote signals or barrier semaphores. Data moves between devices by JAX's collectives and lax.ppermute only.
A program may use at most 64 MiB of HBM per device.

v0:
```python
import jax
import jax.numpy as jnp
from jax import lax
from jax.sharding import PartitionSpec as P

SHARE = 4
STEPS = 4


FULL_ACCURACY = lax.Precision.HIGHEST
TIME_STEP = 0.05
COUPLING = 1.5


def padded(cells, sides, width):
    for axis, dim in sides:
        count = lax.axis_size(axis)
        ends = count - 1
        head = lax.slice_in_dim(cells, 0, width, axis=dim)
        tail = lax.slice_in_dim(cells, cells.shape[dim] - width, cells.shape[dim], axis=dim)
        cells = jnp.concatenate(
            [
                lax.ppermute(tail, axis, [(i, (i + 1) % count) for i in range(ends)]),
                cells,
                lax.ppermute(head, axis, [((i + 1) % count, i) for i in range(ends)]),
            ],
            axis=dim,
        )
    return cells


def passed_along(array, axis, by):
    peers = lax.axis_size(axis)
    pairs = [(i, i + by) for i in range(peers) if 0 <= i + by < peers]
    return lax.ppermute(array, axis, pairs)


def node_weights(fine_index, coarse_count):
    lower_index = (2 * fine_index - 1) // 4
    weight = (2 * fine_index - 1 - 4 * lower_index).astype(jnp.float32) / 4.0
    lower_node = jnp.clip(lower_index, 0, coarse_count - 1)
    upper_node = jnp.clip(lower_index + 1, 0, coarse_count - 1)
    return (lower_node, upper_node, weight)


def interpolation_matrix(lower_node, upper_node, weight, column_count):
    columns = jnp.arange(column_count, dtype=jnp.int32)
    lower_hit = (columns[None, :] == lower_node[:, None]).astype(jnp.float32)
    upper_hit = (columns[None, :] == upper_node[:, None]).astype(jnp.float32)
    return (1.0 - weight)[:, None] * lower_hit + weight[:, None] * upper_hit


def pick_entry(values, slab_iota, position):
    return jnp.sum(jnp.where(slab_iota == position, values, 0))


def block_ids(grain_ids, slab_pos, col_pos):
    slab_row = lax.dynamic_index_in_dim(grain_ids, slab_pos, 0, keepdims=False)
    return lax.dynamic_index_in_dim(slab_row, col_pos, 0, keepdims=False)


def slot_match(mine, theirs):
    return (mine[:, None] == theirs[None, :]).astype(jnp.float32)


def packing(sender, receiver):
    shared = jnp.any(sender[:, None] == receiver[None, :], axis=1)
    placed = jnp.cumsum(shared.astype(jnp.int32)) - 1
    targets = jnp.arange(SHARE, dtype=jnp.int32)
    return ((placed[None, :] == targets[:, None]) & shared[None, :]).astype(jnp.float32)


def unpacking(sender, receiver):
    return jnp.dot(
        slot_match(receiver, sender), packing(sender, receiver).T, precision=FULL_ACCURACY
    )


def apply_slots(matrix, face_cells):
    return jnp.einsum("qr,ryz->qyz", matrix, face_cells, precision=FULL_ACCURACY)


def rates(fields, laplace, grain_mobility, slot_energy):
    squares = jnp.sum(fields * fields, axis=0)
    force = (
        -fields
        + fields * fields * fields
        + 2.0 * COUPLING * fields * (squares - fields * fields)
        - laplace
        - slot_energy * fields * (1.0 - fields)
    )
    return -grain_mobility * force


def total_rate(local_rate):
    return lax.psum(local_rate, ("slab", "col"))


def per_device(order_params, layer_mask, coarse_temp, coarse_rows, grain_ids, energy):
    slot_count, cells_x, cells_y, cells_z = order_params.shape
    slab_count = lax.axis_size("slab")
    col_count = lax.axis_size("col")
    slab_at = lax.axis_index("slab")
    col_at = lax.axis_index("col")
    capacity = coarse_temp.shape[0]
    coarse_y = coarse_temp.shape[1]
    coarse_z = coarse_temp.shape[2]
    extended = padded(coarse_temp, (("col", 1),), 1)
    block_ends = jnp.cumsum(coarse_rows)
    block_starts = block_ends - coarse_rows
    slab_iota = jnp.arange(slab_count, dtype=jnp.int32)
    start_own = pick_entry(block_starts, slab_iota, slab_at)
    end_own = pick_entry(block_ends, slab_iota, slab_at)
    start_prev = pick_entry(block_starts, slab_iota, slab_at - 1)
    fine_x = slab_at * cells_x + jnp.arange(cells_x, dtype=jnp.int32)
    lower_x, upper_x, weight_x = node_weights(fine_x, slab_count * (cells_x // 2))
    source = padded(extended, (("slab", 0),), capacity)

    def locate(plane):
        return jnp.where(
            plane < start_own,
            plane - start_prev,
            jnp.where(
                plane < end_own, capacity + plane - start_own, 2 * capacity + plane - end_own
            ),
        )

    along_x = interpolation_matrix(locate(lower_x), locate(upper_x), weight_x, source.shape[0])
    coarse_slab = jnp.einsum("ir,ryz->iyz", along_x, source, precision=FULL_ACCURACY)
    fine_y = col_at * cells_y + jnp.arange(cells_y, dtype=jnp.int32)
    lower_y, upper_y, weight_y = node_weights(fine_y, col_count * coarse_y)
    y_offset = col_at * coarse_y - 1
    along_y = interpolation_matrix(lower_y - y_offset, upper_y - y_offset, weight_y, coarse_y + 2)
    coarse_columns = jnp.einsum("jy,iyz->ijz", along_y, coarse_slab, precision=FULL_ACCURACY)
    lower_z, upper_z, weight_z = node_weights(jnp.arange(cells_z, dtype=jnp.int32), coarse_z)
    vertical_direction = interpolation_matrix(lower_z, upper_z, weight_z, coarse_z)
    thermal_profile = jnp.einsum(
        "au,hwu->hwa", vertical_direction, coarse_columns, precision=FULL_ACCURACY
    )
    grain_mobility = jnp.exp(2.0 * (thermal_profile - 1.0))
    deposited = layer_mask.astype(jnp.float32)
    local_mobility = jnp.sum(deposited * grain_mobility)
    mobility_sum = jnp.float32(1.0)
    mobility_sum = lax.psum(local_mobility, ("slab", "col")) * slot_count
    own_ids = block_ids(grain_ids, slab_at, col_at)
    prev_slab_ids = block_ids(grain_ids, jnp.maximum(slab_at - 1, 0), col_at)
    next_slab_ids = block_ids(grain_ids, jnp.minimum(slab_at + 1, slab_count - 1), col_at)
    prev_col_ids = block_ids(grain_ids, slab_at, jnp.maximum(col_at - 1, 0))
    next_col_ids = block_ids(grain_ids, slab_at, jnp.minimum(col_at + 1, col_count - 1))
    grain_iota = jnp.arange(energy.shape[0], dtype=jnp.int32)
    slot_energy = jnp.sum(
        jnp.where(own_ids[:, None] == grain_iota[None, :], energy[None, :], 0.0), axis=1
    )[:, None, None, None]
    pack_up_slab = packing(own_ids, next_slab_ids)
    pack_down_slab = packing(own_ids, prev_slab_ids)
    pack_up_col = packing(own_ids, next_col_ids)
    pack_down_col = packing(own_ids, prev_col_ids)
    below_map = unpacking(prev_slab_ids, own_ids)
    above_map = unpacking(next_slab_ids, own_ids)
    left_map = unpacking(prev_col_ids, own_ids)
    right_map = unpacking(next_col_ids, own_ids)
    fields = order_params
    zero_plane = jnp.zeros((slot_count, cells_x, cells_y, 1), jnp.float32)
    for step_index in range(STEPS):
        from_lower = passed_along(apply_slots(pack_up_slab, fields[:, -1]), "slab", 1)
        from_upper = passed_along(apply_slots(pack_down_slab, fields[:, 0]), "slab", -1)
        from_left = passed_along(apply_slots(pack_up_col, fields[:, :, -1]), "col", 1)
        from_right = passed_along(apply_slots(pack_down_col, fields[:, :, 0]), "col", -1)
        below = apply_slots(below_map, from_lower)
        above = apply_slots(above_map, from_upper)
        left_side = apply_slots(left_map, from_left)
        right_side = apply_slots(right_map, from_right)
        x_low = jnp.concatenate([below[:, None], fields[:, :-1]], axis=1)
        x_high = jnp.concatenate([fields[:, 1:], above[:, None]], axis=1)
        y_low = jnp.concatenate([left_side[:, :, None], fields[:, :, :-1]], axis=2)
        y_high = jnp.concatenate([fields[:, :, 1:], right_side[:, :, None]], axis=2)
        z_low = jnp.concatenate([zero_plane, fields[..., :-1]], axis=3)
        z_high = jnp.concatenate([fields[..., 1:], zero_plane], axis=3)
        laplace = x_low + x_high + y_low + y_high + z_low + z_high - 6.0 * fields
        rate = rates(fields, laplace, grain_mobility, slot_energy)
        local_rate = jnp.sum(deposited * jnp.sum(rate, axis=0))
        rate_sum = total_rate(local_rate)
        multiplier = rate_sum / mobility_sum
        fields = fields + TIME_STEP * deposited * (rate - grain_mobility * multiplier)
    return fields


def solution(mesh):
    in_specs = (
        P(None, "slab", "col", None),
        P("slab", "col", None),
        P("slab", "col", None),
        P(),
        P(),
        P(),
    )
    out_specs = P(None, "slab", "col", None)
    return jax.shard_map(
        per_device, mesh=mesh, in_specs=in_specs, out_specs=out_specs, check_vma=False
    )
```

profile of v0, /device:TPU:0, one launch (start us, length us, event | category | flops | bytes accessed | tf_op | source)
XLA Modules:
  0.0 277.5 jit_solution(7139101808587439099)
XLA Ops:
  0.8 2.4 collective-permute-start
  3.2 1.3 collective-permute-start.1
  5.9 1.8 fusion.212
  7.9 5.2 %collective-permute-start.6 = (f32[4,8,256]{2,0,1:T(4,128)S(1)}, f32[4,8,256]{2,0,1:T(4,128)S(1)}, u32[]{:S(2)}, u32[]{:S(2)}) collective-permute-start(f32[4,8,256]{2,0,1:T(4,128)S(1)} %fusion.115), channel_id=1, source_target_pairs={{0,1},{1,2},{2,3},{4,5},{5,6},{6,7},{8,9},{9,10},{10,11},{12,13},{... | collective-permute-start | bytes 98312 | tf_op jit(solution)/shard_map/ppermute | solution.py:35
  15.9 1.3 collective-permute-start.5
  17.3 1.5 fusion.213
  18.8 1.5 fusion.211
  20.3 1.4 fusion.210
  25.6 1.3 collective-permute-start.3
  26.9 5.2 %collective-permute-start.2 = (f32[6,6,128]{2,0,1:T(8,128)S(1)}, f32[6,6,128]{2,0,1:T(8,128)S(1)}, u32[]{:S(2)}, u32[]{:S(2)}) collective-permute-start(f32[6,6,128]{2,0,1:T(8,128)S(1)} %constant_dynamic-update-slice_fusion), channel_id=1, source_target_pairs={{0,4},{4,8},{8,12},{12,16},{16,20},{20,24},{24,28},{1,5},{5,9},{9,... | collective-permute-start | bytes 55304 | tf_op jit(solution)/shard_map/ppermute | solution.py:23
  32.1 1.9 compare_select_fusion.1
  34.0 4.8 %collective-permute-start.4 = (f32[4,8,256]{2,0,1:T(4,128)S(1)}, f32[4,8,256]{2,0,1:T(4,128)S(1)}, u32[]{:S(2)}, u32[]{:S(2)}) collective-permute-start(f32[4,8,256]{2,0,1:T(4,128)S(1)} %fusion.111), channel_id=1, source_target_pairs={{0,4},{4,8},{8,12},{12,16},{16,20},{20,24},{24,28},{1,5},{5,9},{9,... | collective-permute-start | bytes 98312 | tf_op jit(solution)/shard_map/ppermute | solution.py:35
  41.3 3.4 %fusion.216 = (f32[8,8,256]{2,1,0:T(8,128)S(1)}, f32[16,8,8,256]{3,0,2,1:T(8,128)S(1)}) fusion(f32[16]{0:T(128)S(1)} %select_reduce_fusion, f32[16,8,8,255]{3,0,2,1:T(8,128)S(1)} %copy-done.2, f32[16,8,8,255]{3,0,2,1:T(8,128)S(1)} %get-tuple-element.44, f32[16,8,1,256]{3,0,2,1:T(8,128)S(1)} %convolution_bitcast_fusion.12, ...), kind=kOutput, calls=%fused_computation.315 | output fusion | flops 7077903 | bytes 8511552 | tf_op jit(solution)/shard_map/sub | solution.py:88
  45.5 43.9 %all-reduce.8 = (f32[]{:T(128)}, f32[]{:T(128)}) all-reduce(f32[]{:T(128)} %get-tuple-element.6, f32[]{:T(128)} %get-tuple-element.5), channel_id=1, replica_groups=mesh['slab'=8,'col'=4] {'slab','col'}, use_global_device_ids=true, to_apply=%region_24.25 | all-reduce | flops 2 | bytes 16 | tf_op jit(solution)/shard_map/psum | solution.py:96
  92.7 1.3 collective-permute-start.10
  94.2 1.3 collective-permute-start.11
  95.5 4.2 %collective-permute-start.8 = (f32[4,8,256]{2,0,1:T(4,128)S(1)}, f32[4,8,256]{2,0,1:T(4,128)S(1)}, u32[]{:S(2)}, u32[]{:S(2)}) collective-permute-start(f32[4,8,256]{2,0,1:T(4,128)S(1)} %fusion.109), channel_id=1, source_target_pairs={{0,4},{4,8},{8,12},{12,16},{16,20},{20,24},{24,28},{1,5},{5,9},{9,... | collective-permute-start | bytes 98312 | tf_op jit(solution)/shard_map/ppermute | solution.py:35
  99.7 1.3 collective-permute-start.9
  101.3 4.1 %collective-permute-done.9 = f32[4,8,256]{2,0,1:T(4,128)S(1)} collective-permute-done((f32[4,8,256]{2,0,1:T(4,128)S(1)}, f32[4,8,256]{2,0,1:T(4,128)S(1)}, u32[]{:S(2)}, u32[]{:S(2)}) %collective-permute-start.9) | collective-permute-done | bytes 32800 | tf_op jit(solution)/shard_map/ppermute | solution.py:35
  108.3 44.0 %psum.37 = f32[]{:T(128)} all-reduce(f32[]{:T(128)} %multiply_reduce_fusion.6), channel_id=1, replica_groups=mesh['slab'=8,'col'=4] {'slab','col'}, use_global_device_ids=true, to_apply=%region_30.31 | all-reduce | flops 1 | bytes 8 | tf_op jit(solution)/shard_map/psum | solution.py:96
  154.8 1.3 collective-permute-start.14
  156.2 1.3 collective-permute-start.15
  157.5 4.2 %collective-permute-start.12 = (f32[4,8,256]{2,0,1:T(4,128)S(1)}, f32[4,8,256]{2,0,1:T(4,128)S(1)}, u32[]{:S(2)}, u32[]{:S(2)}) collective-permute-start(f32[4,8,256]{2,0,1:T(4,128)S(1)} %fusion.105), channel_id=1, source_target_pairs={{0,4},{4,8},{8,12},{12,16},{16,20},{20,24},{24,28},{1,5},{5,9},{9,... | collective-permute-start | bytes 98312 | tf_op jit(solution)/shard_map/ppermute | solution.py:35
  161.7 1.3 collective-permute-start.13
  163.4 4.1 %collective-permute-done.13 = f32[4,8,256]{2,0,1:T(4,128)S(1)} collective-permute-done((f32[4,8,256]{2,0,1:T(4,128)S(1)}, f32[4,8,256]{2,0,1:T(4,128)S(1)}, u32[]{:S(2)}, u32[]{:S(2)}) %collective-permute-start.13) | collective-permute-done | bytes 32800 | tf_op jit(solution)/shard_map/ppermute | solution.py:35
  170.4 43.0 %psum.38 = f32[]{:T(128)} all-reduce(f32[]{:T(128)} %multiply_reduce_fusion.5), channel_id=1, replica_groups=mesh['slab'=8,'col'=4] {'slab','col'}, use_global_device_ids=true, to_apply=%region_34.35 | all-reduce | flops 1 | bytes 8 | tf_op jit(solution)/shard_map/psum | solution.py:96
  217.3 1.3 collective-permute-start.19
  218.6 4.2 %collective-permute-start.16 = (f32[4,8,256]{2,0,1:T(4,128)S(1)}, f32[4,8,256]{2,0,1:T(4,128)S(1)}, u32[]{:S(2)}, u32[]{:S(2)}) collective-permute-start(f32[4,8,256]{2,0,1:T(4,128)S(1)} %fusion.101), channel_id=1, source_target_pairs={{0,4},{4,8},{8,12},{12,16},{16,20},{20,24},{24,28},{1,5},{5,9},{9,... | collective-permute-start | bytes 98312 | tf_op jit(solution)/shard_map/ppermute | solution.py:35
  222.8 1.3 collective-permute-start.17
  224.4 4.1 %collective-permute-done.17 = f32[4,8,256]{2,0,1:T(4,128)S(1)} collective-permute-done((f32[4,8,256]{2,0,1:T(4,128)S(1)}, f32[4,8,256]{2,0,1:T(4,128)S(1)}, u32[]{:S(2)}, u32[]{:S(2)}) %collective-permute-start.17) | collective-permute-done | bytes 32800 | tf_op jit(solution)/shard_map/ppermute | solution.py:35
  231.5 43.4 %psum.39 = f32[]{:T(128)} all-reduce(f32[]{:T(128)} %multiply_reduce_fusion.4), channel_id=1, replica_groups=mesh['slab'=8,'col'=4] {'slab','col'}, use_global_device_ids=true, to_apply=%region_38.39 | all-reduce | flops 1 | bytes 8 | tf_op jit(solution)/shard_map/psum | solution.py:96
  275.9 1.6 copy.190
  (145 shorter events, 29.4 us)
Async XLA Ops:
  0.0 14.8 %copy-start = (f32[16,8,8,256]{3,2,1,0:T(8,128)S(1)}, f32[16,8,8,256]{3,2,1,0:T(8,128)}, u32[]{:S(2)}) copy-start(f32[16,8,8,256]{3,2,1,0:T(8,128)} %param.6) | copy-start | bytes 3145732
  0.8 24.8 %collective-permute-start = (f32[6,1,128]{2,0,1:T(8,128)S(1)}, f32[6,1,128]{2,0,1:T(8,128)S(1)}, u32[]{:S(2)}, u32[]{:S(2)}) collective-permute-start(f32[6,1,128]{2,0,1:T(8,128)S(1)} %copy.222), channel_id=1, source_target_pairs={{0,1},{1,2},{2,3},{4,5},{5,6},{6,7},{8,9},{9,10},{10,11},{12,13},{... | collective-permute-start | bytes 9224 | tf_op jit(solution)/shard_map/ppermute | solution.py:23
  3.2 22.4 %collective-permute-start.1 = (f32[6,1,128]{2,0,1:T(8,128)S(1)}, f32[6,1,128]{2,0,1:T(8,128)S(1)}, u32[]{:S(2)}, u32[]{:S(2)}) collective-permute-start(f32[6,1,128]{2,0,1:T(8,128)S(1)} %copy.223), channel_id=1, source_target_pairs={{1,0},{2,1},{3,2},{5,4},{6,5},{7,6},{9,8},{10,9},{11,10},{13,12},{... | collective-permute-start | bytes 9224 | tf_op jit(solution)/shard_map/ppermute | solution.py:25
  7.9 32.3 %collective-permute-start.6 = (f32[4,8,256]{2,0,1:T(4,128)S(1)}, f32[4,8,256]{2,0,1:T(4,128)S(1)}, u32[]{:S(2)}, u32[]{:S(2)}) collective-permute-start(f32[4,8,256]{2,0,1:T(4,128)S(1)} %fusion.115), channel_id=1, source_target_pairs={{0,1},{1,2},{2,3},{4,5},{5,6},{6,7},{8,9},{9,10},{10,11},{12,13},{... | collective-permute-start | bytes 98312 | tf_op jit(solution)/shard_map/ppermute | solution.py:35
  13.5 26.3 %collective-permute-start.7 = (f32[4,8,256]{2,0,1:T(4,128)S(1)}, f32[4,8,256]{2,0,1:T(4,128)S(1)}, u32[]{:S(2)}, u32[]{:S(2)}) collective-permute-start(f32[4,8,256]{2,0,1:T(4,128)S(1)} %fusion.112), channel_id=1, source_target_pairs={{1,0},{2,1},{3,2},{5,4},{6,5},{7,6},{9,8},{10,9},{11,10},{13,12},{... | collective-permute-start | bytes 98312 | tf_op jit(solution)/shard_map/ppermute | solution.py:35
  15.9 25.0 %collective-permute-start.5 = (f32[4,8,256]{2,0,1:T(4,128)S(1)}, f32[4,8,256]{2,0,1:T(4,128)S(1)}, u32[]{:S(2)}, u32[]{:S(2)}) collective-permute-start(f32[4,8,256]{2,0,1:T(4,128)S(1)} %fusion.110), channel_id=1, source_target_pairs={{4,0},{8,4},{12,8},{16,12},{20,16},{24,20},{28,24},{5,1},{9,5},{13... | collective-permute-start | bytes 98312 | tf_op jit(solution)/shard_map/ppermute | solution.py:35
  20.3 1.4 copy-start.4
  21.8 0.7 copy-start.5
  24.3 1.3 copy-start.3
  25.1 16.2 %copy-start.2 = (f32[16,8,8,255]{3,0,2,1:T(8,128)S(1)}, f32[16,8,8,255]{3,0,2,1:T(8,128)}, u32[]{:S(2)}) copy-start(f32[16,8,8,255]{3,0,2,1:T(8,128)} %get-tuple-element.45) | copy-start | bytes 3133444
  25.6 8.4 %collective-permute-start.3 = (f32[6,6,128]{2,0,1:T(8,128)S(1)}, f32[6,6,128]{2,0,1:T(8,128)S(1)}, u32[]{:S(2)}, u32[]{:S(2)}) collective-permute-start(f32[6,6,128]{2,0,1:T(8,128)S(1)} %constant_dynamic-update-slice_fusion), channel_id=1, source_target_pairs={{4,0},{8,4},{12,8},{16,12},{20,16},{24,20},{28,24},{5,1},{9,5},{13... | collective-permute-start | bytes 55304 | tf_op jit(solution)/shard_map/ppermute | solution.py:25
  26.9 11.9 %collective-permute-start.2 = (f32[6,6,128]{2,0,1:T(8,128)S(1)}, f32[6,6,128]{2,0,1:T(8,128)S(1)}, u32[]{:S(2)}, u32[]{:S(2)}) collective-permute-start(f32[6,6,128]{2,0,1:T(8,128)S(1)} %constant_dynamic-update-slice_fusion), channel_id=1, source_target_pairs={{0,4},{4,8},{8,12},{12,16},{16,20},{20,24},{24,28},{1,5},{5,9},{9,... | collective-permute-start | bytes 55304 | tf_op jit(solution)/shard_map/ppermute | solution.py:23
  34.0 6.5 %collective-permute-start.4 = (f32[4,8,256]{2,0,1:T(4,128)S(1)}, f32[4,8,256]{2,0,1:T(4,128)S(1)}, u32[]{:S(2)}, u32[]{:S(2)}) collective-permute-start(f32[4,8,256]{2,0,1:T(4,128)S(1)} %fusion.111), channel_id=1, source_target_pairs={{0,4},{4,8},{8,12},{12,16},{16,20},{20,24},{24,28},{1,5},{5,9},{9,... | collective-permute-start | bytes 98312 | tf_op jit(solution)/shard_map/ppermute | solution.py:35
  41.3 3.5 %copy-start.1 = (s32[8,8,256]{2,1,0:T(8,128)S(1)}, s32[8,8,256]{2,1,0:T(8,128)}, u32[]{:S(2)}) copy-start(s32[8,8,256]{2,1,0:T(8,128)} %param.7) | copy-start | bytes 196612
  92.7 8.3 %collective-permute-start.10 = (f32[4,8,256]{2,0,1:T(4,128)S(1)}, f32[4,8,256]{2,0,1:T(4,128)S(1)}, u32[]{:S(2)}, u32[]{:S(2)}) collective-permute-start(f32[4,8,256]{2,0,1:T(4,128)S(1)} %fusion.107), channel_id=1, source_target_pairs={{0,1},{1,2},{2,3},{4,5},{5,6},{6,7},{8,9},{9,10},{10,11},{12,13},{... | collective-permute-start | bytes 98312 | tf_op jit(solution)/shard_map/ppermute | solution.py:35
  94.2 12.0 %collective-permute-start.11 = (f32[4,8,256]{2,0,1:T(4,128)S(1)}, f32[4,8,256]{2,0,1:T(4,128)S(1)}, u32[]{:S(2)}, u32[]{:S(2)}) collective-permute-start(f32[4,8,256]{2,0,1:T(4,128)S(1)} %fusion.106), channel_id=1, source_target_pairs={{1,0},{2,1},{3,2},{5,4},{6,5},{7,6},{9,8},{10,9},{11,10},{13,12},{... | collective-permute-start | bytes 98312 | tf_op jit(solution)/shard_map/ppermute | solution.py:35
  95.5 10.4 %collective-permute-start.8 = (f32[4,8,256]{2,0,1:T(4,128)S(1)}, f32[4,8,256]{2,0,1:T(4,128)S(1)}, u32[]{:S(2)}, u32[]{:S(2)}) collective-permute-start(f32[4,8,256]{2,0,1:T(4,128)S(1)} %fusion.109), channel_id=1, source_target_pairs={{0,4},{4,8},{8,12},{12,16},{16,20},{20,24},{24,28},{1,5},{5,9},{9,... | collective-permute-start | bytes 98312 | tf_op jit(solution)/shard_map/ppermute | solution.py:35
  99.7 5.8 %collective-permute-start.9 = (f32[4,8,256]{2,0,1:T(4,128)S(1)}, f32[4,8,256]{2,0,1:T(4,128)S(1)}, u32[]{:S(2)}, u32[]{:S(2)}) collective-permute-start(f32[4,8,256]{2,0,1:T(4,128)S(1)} %fusion.108), channel_id=1, source_target_pairs={{4,0},{8,4},{12,8},{16,12},{20,16},{24,20},{28,24},{5,1},{9,5},{13... | collective-permute-start | bytes 98312 | tf_op jit(solution)/shard_map/ppermute | solution.py:35
  154.8 8.3 %collective-permute-start.14 = (f32[4,8,256]{2,0,1:T(4,128)S(1)}, f32[4,8,256]{2,0,1:T(4,128)S(1)}, u32[]{:S(2)}, u32[]{:S(2)}) collective-permute-start(f32[4,8,256]{2,0,1:T(4,128)S(1)} %fusion.103), channel_id=1, source_target_pairs={{0,1},{1,2},{2,3},{4,5},{5,6},{6,7},{8,9},{9,10},{10,11},{12,13},{... | collective-permute-start | bytes 98312 | tf_op jit(solution)/shard_map/ppermute | solution.py:35
  156.2 12.0 %collective-permute-start.15 = (f32[4,8,256]{2,0,1:T(4,128)S(1)}, f32[4,8,256]{2,0,1:T(4,128)S(1)}, u32[]{:S(2)}, u32[]{:S(2)}) collective-permute-start(f32[4,8,256]{2,0,1:T(4,128)S(1)} %fusion.102), channel_id=1, source_target_pairs={{1,0},{2,1},{3,2},{5,4},{6,5},{7,6},{9,8},{10,9},{11,10},{13,12},{... | collective-permute-start | bytes 98312 | tf_op jit(solution)/shard_map/ppermute | solution.py:35
  157.5 10.4 %collective-permute-start.12 = (f32[4,8,256]{2,0,1:T(4,128)S(1)}, f32[4,8,256]{2,0,1:T(4,128)S(1)}, u32[]{:S(2)}, u32[]{:S(2)}) collective-permute-start(f32[4,8,256]{2,0,1:T(4,128)S(1)} %fusion.105), channel_id=1, source_target_pairs={{0,4},{4,8},{8,12},{12,16},{16,20},{20,24},{24,28},{1,5},{5,9},{9,... | collective-permute-start | bytes 98312 | tf_op jit(solution)/shard_map/ppermute | solution.py:35
  161.7 5.8 %collective-permute-start.13 = (f32[4,8,256]{2,0,1:T(4,128)S(1)}, f32[4,8,256]{2,0,1:T(4,128)S(1)}, u32[]{:S(2)}, u32[]{:S(2)}) collective-permute-start(f32[4,8,256]{2,0,1:T(4,128)S(1)} %fusion.104), channel_id=1, source_target_pairs={{4,0},{8,4},{12,8},{16,12},{20,16},{24,20},{28,24},{5,1},{9,5},{13... | collective-permute-start | bytes 98312 | tf_op jit(solution)/shard_map/ppermute | solution.py:35
  215.8 8.3 %collective-permute-start.18 = (f32[4,8,256]{2,0,1:T(4,128)S(1)}, f32[4,8,256]{2,0,1:T(4,128)S(1)}, u32[]{:S(2)}, u32[]{:S(2)}) collective-permute-start(f32[4,8,256]{2,0,1:T(4,128)S(1)} %fusion.99), channel_id=1, source_target_pairs={{0,1},{1,2},{2,3},{4,5},{5,6},{6,7},{8,9},{9,10},{10,11},{12,13},{... | collective-permute-start | bytes 98312 | tf_op jit(solution)/shard_map/ppermute | solution.py:35
  217.3 12.0 %collective-permute-start.19 = (f32[4,8,256]{2,0,1:T(4,128)S(1)}, f32[4,8,256]{2,0,1:T(4,128)S(1)}, u32[]{:S(2)}, u32[]{:S(2)}) collective-permute-start(f32[4,8,256]{2,0,1:T(4,128)S(1)} %fusion.98), channel_id=1, source_target_pairs={{1,0},{2,1},{3,2},{5,4},{6,5},{7,6},{9,8},{10,9},{11,10},{13,12},{... | collective-permute-start | bytes 98312 | tf_op jit(solution)/shard_map/ppermute | solution.py:35
  218.6 10.4 %collective-permute-start.16 = (f32[4,8,256]{2,0,1:T(4,128)S(1)}, f32[4,8,256]{2,0,1:T(4,128)S(1)}, u32[]{:S(2)}, u32[]{:S(2)}) collective-permute-start(f32[4,8,256]{2,0,1:T(4,128)S(1)} %fusion.101), channel_id=1, source_target_pairs={{0,4},{4,8},{8,12},{12,16},{16,20},{20,24},{24,28},{1,5},{5,9},{9,... | collective-permute-start | bytes 98312 | tf_op jit(solution)/shard_map/ppermute | solution.py:35
  222.8 5.8 %collective-permute-start.17 = (f32[4,8,256]{2,0,1:T(4,128)S(1)}, f32[4,8,256]{2,0,1:T(4,128)S(1)}, u32[]{:S(2)}, u32[]{:S(2)}) collective-permute-start(f32[4,8,256]{2,0,1:T(4,128)S(1)} %fusion.100), channel_id=1, source_target_pairs={{4,0},{8,4},{12,8},{16,12},{20,16},{24,20},{28,24},{5,1},{9,5},{13... | collective-permute-start | bytes 98312 | tf_op jit(solution)/shard_map/ppermute | solution.py:35
where the time goes:
time: 279 us; the launch traced here: 277 us
  blocking collectives  174 us (62%)
  starting transfers between devices  46.9 us (17%)
  other arithmetic  15.9 us (6%)
  local copies, waits for them, and re-layouts  13.9 us (5%)
  waiting for transfers between devices  12.5 us (4%)
  matrix products  10 us (4%)
  between operations  4.05 us (1%)
    psum x4, blocking collectives, total_rate(): return lax.psum(local_rate, ('slab', 'col'))  174 us
    ppermute x16, starting transfers between devices, passed_along(): return lax.ppermute(array, axis, pairs)  36.7 us
    ppermute x16, waiting for transfers between devices, passed_along(): return lax.ppermute(array, axis, pairs)  12.4 us
    dot_general x32, matrix products, apply_slots(): jnp.einsum('qr,ryz->qyz', matrix, face_cells, precision=FULL_ACCURACY)  8.33 us
    ppermute x2, starting transfers between devices, padded(): lax.ppermute(tail, axis, [(i, (i + 1) % count) for i in range(ends)])  7.53 us
    sub x4, other arithmetic, rates(): squares - fields * fields  6.9 us
  transfers between devices with their start and end apart: 20, of which 3 were waited for; matrix products, arithmetic and copies ran while one was open for 7% of the time, Pallas kernels for 0%

commit v1 on v0

--- a/solution.py
+++ b/solution.py
@@ -92,8 +92,12 @@
     return -grain_mobility * force
 
 
-def total_rate(local_rate):
-    return lax.psum(local_rate, ("slab", "col"))
+def total(parts):
+    devices = lax.axis_size("slab") * lax.axis_size("col")
+    row = jnp.pad(jnp.stack(parts), (0, 128 - len(parts)))
+    sent = jnp.broadcast_to(row, (devices, 1, 128))
+    got = lax.all_to_all(sent, ("slab", "col"), 0, 0)
+    return jnp.sum(got, axis=(0, 1))
 
 
 def per_device(order_params, layer_mask, coarse_temp, coarse_rows, grain_ids, energy):
@@ -140,8 +144,6 @@
     grain_mobility = jnp.exp(2.0 * (thermal_profile - 1.0))
     deposited = layer_mask.astype(jnp.float32)
     local_mobility = jnp.sum(deposited * grain_mobility)
-    mobility_sum = jnp.float32(1.0)
-    mobility_sum = lax.psum(local_mobility, ("slab", "col")) * slot_count
     own_ids = block_ids(grain_ids, slab_at, col_at)
     prev_slab_ids = block_ids(grain_ids, jnp.maximum(slab_at - 1, 0), col_at)
     next_slab_ids = block_ids(grain_ids, jnp.minimum(slab_at + 1, slab_count - 1), col_at)
@@ -179,8 +181,12 @@
         laplace = x_low + x_high + y_low + y_high + z_low + z_high - 6.0 * fields
         rate = rates(fields, laplace, grain_mobility, slot_energy)
         local_rate = jnp.sum(deposited * jnp.sum(rate, axis=0))
-        rate_sum = total_rate(local_rate)
-        multiplier = rate_sum / mobility_sum
+        if step_index == 0:
+            sums = total([local_rate, local_mobility])
+            mobility_sum = sums[1] * slot_count
+        else:
+            sums = total([local_rate])
+        multiplier = sums[0] / mobility_sum
         fields = fields + TIME_STEP * deposited * (rate - grain_mobility * multiplier)
     return fields
 

time: 279 us -> 155 us (0.56)
  blocking collectives: 174 us -> 52.4 us
  starting transfers between devices: 46.9 us -> 43.2 us
    psum x4 -> x0, blocking collectives: 174 us -> none  [total_rate(): return lax.psum(local_rate, ('slab', 'col'))]
    all_to_all x0 -> x4, blocking collectives: none -> 52.4 us  [total(): got = lax.all_to_all(sent, ('slab', 'col'), 0, 0)]
    ppermute x16, starting transfers between devices: 36.7 us -> 33.1 us  [passed_along(): return lax.ppermute(array, axis, pairs)]
  transfers between devices with their start and end apart: 20 -> 20, of which waited for: 3 -> 3; matrix products, arithmetic and copies ran while one was open for 7% -> 13% of each run, Pallas kernels for 0% -> 0%
where the time goes in v1:
time: 155 us; the launch traced here: 154 us
  blocking collectives  52.4 us (34%)
  starting transfers between devices  43.2 us (28%)
  other arithmetic  17.4 us (11%)
  local copies, waits for them, and re-layouts  16.6 us (11%)
  waiting for transfers between devices  12.5 us (8%)
  matrix products  9.98 us (6%)
  between operations  2.41 us (2%)
    all_to_all x4, blocking collectives, total(): got = lax.all_to_all(sent, ('slab', 'col'), 0, 0)  52.4 us
    ppermute x16, starting transfers between devices, passed_along(): return lax.ppermute(array, axis, pairs)  33.1 us
    ppermute x16, waiting for transfers between devices, passed_along(): return lax.ppermute(array, axis, pairs)  12.4 us
    dot_general x32, matrix products, apply_slots(): jnp.einsum('qr,ryz->qyz', matrix, face_cells, precision=FULL_ACCURACY)  8.31 us
    ppermute x2, starting transfers between devices, padded(): lax.ppermute(tail, axis, [(i, (i + 1) % count) for i in range(ends)])  7.53 us
    sub x4, other arithmetic, rates(): squares - fields * fields  6.9 us
  transfers between devices with their start and end apart: 20, of which 3 were waited for; matrix products, arithmetic and copies ran while one was open for 13% of the time, Pallas kernels for 0%

profile of v1, /device:TPU:0, one launch (start us, length us, event | category | flops | bytes accessed | tf_op | source)
XLA Modules:
  0.0 154.4 jit_solution(18301763186646596815)
XLA Ops:
  0.8 2.4 %collective-permute-start = (f32[6,1,128]{2,0,1:T(8,128)S(1)}, f32[6,1,128]{2,0,1:T(8,128)S(1)}, u32[]{:S(2)}, u32[]{:S(2)}) collective-permute-start(f32[6,1,128]{2,0,1:T(8,128)S(1)} %copy.282), channel_id=1, source_target_pairs={{0,1},{1,2},{2,3},{4,5},{5,6},{6,7},{8,9},{9,10},{10,11},{12,13},{... | collective-permute-start | bytes 9224 | tf_op jit(solution)/shard_map/ppermute | solution.py:23
  3.2 1.3 collective-permute-start.1
  5.9 1.9 %fusion.213 = (f32[16,8,1,256]{3,2,1,0:T(1,128)S(1)}, f32[16,8,1,256]{3,2,1,0:T(1,128)S(1)}) fusion(f32[16,8,8,256]{3,2,1,0:T(8,128)} %param.6), kind=kLoop, calls=%fused_computation.314 | loop fusion | bytes 524288 | tf_op jit(solution)/shard_map/slice | solution.py:170
  8.0 5.2 %collective-permute-start.6 = (f32[4,8,256]{2,0,1:T(4,128)S(1)}, f32[4,8,256]{2,0,1:T(4,128)S(1)}, u32[]{:S(2)}, u32[]{:S(2)}) collective-permute-start(f32[4,8,256]{2,0,1:T(4,128)S(1)} %fusion.115), channel_id=1, source_target_pairs={{0,1},{1,2},{2,3},{4,5},{5,6},{6,7},{8,9},{9,10},{10,11},{12,13},{... | collective-permute-start | bytes 98312 | tf_op jit(solution)/shard_map/ppermute | solution.py:35
  16.0 1.3 collective-permute-start.5
  17.4 1.5 fusion.214
  18.9 1.5 fusion.212
  20.4 1.4 fusion.211
  25.8 1.3 collective-permute-start.3
  27.1 5.2 %collective-permute-start.2 = (f32[6,6,128]{2,0,1:T(8,128)S(1)}, f32[6,6,128]{2,0,1:T(8,128)S(1)}, u32[]{:S(2)}, u32[]{:S(2)}) collective-permute-start(f32[6,6,128]{2,0,1:T(8,128)S(1)} %constant_dynamic-update-slice_fusion), channel_id=1, source_target_pairs={{0,4},{4,8},{8,12},{12,16},{16,20},{20,24},{24,28},{1,5},{5,9},{9,... | collective-permute-start | bytes 55304 | tf_op jit(solution)/shard_map/ppermute | solution.py:23
  32.2 1.9 %compare_select_fusion.1 = (s32[8]{0:T(128)S(1)}, s32[8]{0:T(128)S(1)}) fusion(s32[]{:T(128)} %get-tuple-element.17, s32[]{:T(128)} %get-tuple-element.8, s32[]{:T(128)} %get-tuple-element.7, s32[]{:T(128)S(6)} %mul.354), kind=kLoop, calls=%fused_computation.236 | loop fusion | flops 312 | bytes 80 | tf_op jit(solution)/shard_map/jit(_where)/select_n | solution.py:124
  34.2 4.8 %collective-permute-start.4 = (f32[4,8,256]{2,0,1:T(4,128)S(1)}, f32[4,8,256]{2,0,1:T(4,128)S(1)}, u32[]{:S(2)}, u32[]{:S(2)}) collective-permute-start(f32[4,8,256]{2,0,1:T(4,128)S(1)} %fusion.111), channel_id=1, source_target_pairs={{0,4},{4,8},{8,12},{12,16},{16,20},{20,24},{24,28},{1,5},{5,9},{9,... | collective-permute-start | bytes 98312 | tf_op jit(solution)/shard_map/ppermute | solution.py:35
  41.4 3.4 %fusion.218 = (f32[8,8,256]{2,1,0:T(8,128)S(1)}, f32[16,8,8,256]{3,0,2,1:T(8,128)S(1)}) fusion(f32[16]{0:T(128)S(1)} %select_reduce_fusion, f32[16,8,8,255]{3,0,2,1:T(8,128)S(1)} %copy-done.2, f32[16,8,8,255]{3,0,2,1:T(8,128)S(1)} %get-tuple-element.42, f32[16,8,1,256]{3,0,2,1:T(8,128)S(1)} %convolution_bitcast_fusion.12, ...), kind=kOutput, calls=%fused_computation.319 | output fusion | flops 7077903 | bytes 8511552 | tf_op jit(solution)/shard_map/sub | solution.py:88
  45.6 1.4 fusion.193
  47.0 15.9 %all_to_all.20 = f32[32,1,128]{2,1,0:T(1,128)S(1)} all-to-all(f32[32,1,128]{2,1,0:T(1,128)S(1)} %broadcast_in_dim.62), channel_id=1, replica_groups=mesh['slab'=8,'col'=4] {'slab','col'}, dimensions={0} | all-to-all | bytes 32768 | tf_op jit(solution)/shard_map/all_to_all | solution.py:99
  67.0 1.8 %collective-permute-start.10 = (f32[4,8,256]{2,0,1:T(4,128)S(1)}, f32[4,8,256]{2,0,1:T(4,128)S(1)}, u32[]{:S(2)}, u32[]{:S(2)}) collective-permute-start(f32[4,8,256]{2,0,1:T(4,128)S(1)} %fusion.107), channel_id=1, source_target_pairs={{0,1},{1,2},{2,3},{4,5},{5,6},{6,7},{8,9},{9,10},{10,11},{12,13},{... | collective-permute-start | bytes 98312 | tf_op jit(solution)/shard_map/ppermute | solution.py:35
  68.9 1.3 collective-permute-start.11
  70.2 2.4 %collective-permute-start.8 = (f32[4,8,256]{2,0,1:T(4,128)S(1)}, f32[4,8,256]{2,0,1:T(4,128)S(1)}, u32[]{:S(2)}, u32[]{:S(2)}) collective-permute-start(f32[4,8,256]{2,0,1:T(4,128)S(1)} %fusion.109), channel_id=1, source_target_pairs={{0,4},{4,8},{8,12},{12,16},{16,20},{20,24},{24,28},{1,5},{5,9},{9,... | collective-permute-start | bytes 98312 | tf_op jit(solution)/shard_map/ppermute | solution.py:35
  72.7 1.3 collective-permute-start.9
  74.3 4.2 %collective-permute-done.9 = f32[4,8,256]{2,0,1:T(4,128)S(1)} collective-permute-done((f32[4,8,256]{2,0,1:T(4,128)S(1)}, f32[4,8,256]{2,0,1:T(4,128)S(1)}, u32[]{:S(2)}, u32[]{:S(2)}) %collective-permute-start.9) | collective-permute-done | bytes 32800 | tf_op jit(solution)/shard_map/ppermute | solution.py:35
  82.1 12.2 %all_to_all.21 = f32[32,1,128]{2,1,0:T(1,128)S(1)} all-to-all(f32[32,1,128]{2,1,0:T(1,128)S(1)} %broadcast_in_dim.67), channel_id=1, replica_groups=mesh['slab'=8,'col'=4] {'slab','col'}, dimensions={0} | all-to-all | bytes 32768 | tf_op jit(solution)/shard_map/all_to_all | solution.py:99
  96.1 1.8 %collective-permute-start.14 = (f32[4,8,256]{2,0,1:T(4,128)S(1)}, f32[4,8,256]{2,0,1:T(4,128)S(1)}, u32[]{:S(2)}, u32[]{:S(2)}) collective-permute-start(f32[4,8,256]{2,0,1:T(4,128)S(1)} %fusion.103), channel_id=1, source_target_pairs={{0,1},{1,2},{2,3},{4,5},{5,6},{6,7},{8,9},{9,10},{10,11},{12,13},{... | collective-permute-start | bytes 98312 | tf_op jit(solution)/shard_map/ppermute | solution.py:35
  99.3 2.4 %collective-permute-start.12 = (f32[4,8,256]{2,0,1:T(4,128)S(1)}, f32[4,8,256]{2,0,1:T(4,128)S(1)}, u32[]{:S(2)}, u32[]{:S(2)}) collective-permute-start(f32[4,8,256]{2,0,1:T(4,128)S(1)} %fusion.105), channel_id=1, source_target_pairs={{0,4},{4,8},{8,12},{12,16},{16,20},{20,24},{24,28},{1,5},{5,9},{9,... | collective-permute-start | bytes 98312 | tf_op jit(solution)/shard_map/ppermute | solution.py:35
  101.7 1.5 collective-permute-start.13
  103.6 4.0 %collective-permute-done.13 = f32[4,8,256]{2,0,1:T(4,128)S(1)} collective-permute-done((f32[4,8,256]{2,0,1:T(4,128)S(1)}, f32[4,8,256]{2,0,1:T(4,128)S(1)}, u32[]{:S(2)}, u32[]{:S(2)}) %collective-permute-start.13) | collective-permute-done | bytes 32800 | tf_op jit(solution)/shard_map/ppermute | solution.py:35
  111.1 12.2 %all_to_all.22 = f32[32,1,128]{2,1,0:T(1,128)S(1)} all-to-all(f32[32,1,128]{2,1,0:T(1,128)S(1)} %broadcast_in_dim.72), channel_id=1, replica_groups=mesh['slab'=8,'col'=4] {'slab','col'}, dimensions={0} | all-to-all | bytes 32768 | tf_op jit(solution)/shard_map/all_to_all | solution.py:99
  125.2 1.8 %collective-permute-start.18 = (f32[4,8,256]{2,0,1:T(4,128)S(1)}, f32[4,8,256]{2,0,1:T(4,128)S(1)}, u32[]{:S(2)}, u32[]{:S(2)}) collective-permute-start(f32[4,8,256]{2,0,1:T(4,128)S(1)} %fusion.99), channel_id=1, source_target_pairs={{0,1},{1,2},{2,3},{4,5},{5,6},{6,7},{8,9},{9,10},{10,11},{12,13},{... | collective-permute-start | bytes 98312 | tf_op jit(solution)/shard_map/ppermute | solution.py:35
  127.1 1.3 collective-permute-start.19
  128.4 2.4 %collective-permute-start.16 = (f32[4,8,256]{2,0,1:T(4,128)S(1)}, f32[4,8,256]{2,0,1:T(4,128)S(1)}, u32[]{:S(2)}, u32[]{:S(2)}) collective-permute-start(f32[4,8,256]{2,0,1:T(4,128)S(1)} %fusion.101), channel_id=1, source_target_pairs={{0,4},{4,8},{8,12},{12,16},{16,20},{20,24},{24,28},{1,5},{5,9},{9,... | collective-permute-start | bytes 98312 | tf_op jit(solution)/shard_map/ppermute | solution.py:35
  132.5 4.2 %collective-permute-done.17 = f32[4,8,256]{2,0,1:T(4,128)S(1)} collective-permute-done((f32[4,8,256]{2,0,1:T(4,128)S(1)}, f32[4,8,256]{2,0,1:T(4,128)S(1)}, u32[]{:S(2)}, u32[]{:S(2)}) %collective-permute-start.17) | collective-permute-done | bytes 32800 | tf_op jit(solution)/shard_map/ppermute | solution.py:35
  140.2 12.2 %all_to_all.23 = f32[32,1,128]{2,1,0:T(1,128)S(1)} all-to-all(f32[32,1,128]{2,1,0:T(1,128)S(1)} %broadcast_in_dim.77), channel_id=1, replica_groups=mesh['slab'=8,'col'=4] {'slab','col'}, dimensions={0} | all-to-all | bytes 32768 | tf_op jit(solution)/shard_map/all_to_all | solution.py:99
  152.8 1.6 %copy.250 = f32[16,8,8,256]{3,2,1,0:T(8,128)} copy(f32[16,8,8,256]{3,0,2,1:T(8,128)S(1)} %multiply_add_fusion) | data formatting | bytes 2097152 | tf_op jit(solution)/shard_map/add | solution.py:190
  (158 shorter events, 33.4 us)
Async XLA Ops:
  0.0 15.0 %copy-start = (f32[16,8,8,256]{3,2,1,0:T(8,128)S(1)}, f32[16,8,8,256]{3,2,1,0:T(8,128)}, u32[]{:S(2)}) copy-start(f32[16,8,8,256]{3,2,1,0:T(8,128)} %param.6) | copy-start | bytes 3145732
  0.8 24.9 %collective-permute-start = (f32[6,1,128]{2,0,1:T(8,128)S(1)}, f32[6,1,128]{2,0,1:T(8,128)S(1)}, u32[]{:S(2)}, u32[]{:S(2)}) collective-permute-start(f32[6,1,128]{2,0,1:T(8,128)S(1)} %copy.282), channel_id=1, source_target_pairs={{0,1},{1,2},{2,3},{4,5},{5,6},{6,7},{8,9},{9,10},{10,11},{12,13},{... | collective-permute-start | bytes 9224 | tf_op jit(solution)/shard_map/ppermute | solution.py:23
  3.2 22.5 %collective-permute-start.1 = (f32[6,1,128]{2,0,1:T(8,128)S(1)}, f32[6,1,128]{2,0,1:T(8,128)S(1)}, u32[]{:S(2)}, u32[]{:S(2)}) collective-permute-start(f32[6,1,128]{2,0,1:T(8,128)S(1)} %copy.283), channel_id=1, source_target_pairs={{1,0},{2,1},{3,2},{5,4},{6,5},{7,6},{9,8},{10,9},{11,10},{13,12},{... | collective-permute-start | bytes 9224 | tf_op jit(solution)/shard_map/ppermute | solution.py:25
  8.0 32.3 %collective-permute-start.6 = (f32[4,8,256]{2,0,1:T(4,128)S(1)}, f32[4,8,256]{2,0,1:T(4,128)S(1)}, u32[]{:S(2)}, u32[]{:S(2)}) collective-permute-start(f32[4,8,256]{2,0,1:T(4,128)S(1)} %fusion.115), channel_id=1, source_target_pairs={{0,1},{1,2},{2,3},{4,5},{5,6},{6,7},{8,9},{9,10},{10,11},{12,13},{... | collective-permute-start | bytes 98312 | tf_op jit(solution)/shard_map/ppermute | solution.py:35
  13.7 26.3 %collective-permute-start.7 = (f32[4,8,256]{2,0,1:T(4,128)S(1)}, f32[4,8,256]{2,0,1:T(4,128)S(1)}, u32[]{:S(2)}, u32[]{:S(2)}) collective-permute-start(f32[4,8,256]{2,0,1:T(4,128)S(1)} %fusion.112), channel_id=1, source_target_pairs={{1,0},{2,1},{3,2},{5,4},{6,5},{7,6},{9,8},{10,9},{11,10},{13,12},{... | collective-permute-start | bytes 98312 | tf_op jit(solution)/shard_map/ppermute | solution.py:35
  16.0 25.0 %collective-permute-start.5 = (f32[4,8,256]{2,0,1:T(4,128)S(1)}, f32[4,8,256]{2,0,1:T(4,128)S(1)}, u32[]{:S(2)}, u32[]{:S(2)}) collective-permute-start(f32[4,8,256]{2,0,1:T(4,128)S(1)} %fusion.110), channel_id=1, source_target_pairs={{4,0},{8,4},{12,8},{16,12},{20,16},{24,20},{28,24},{5,1},{9,5},{13... | collective-permute-start | bytes 98312 | tf_op jit(solution)/shard_map/ppermute | solution.py:35
  20.4 1.4 copy-start.4
  21.9 0.7 copy-start.5
  24.4 1.3 copy-start.3
  25.2 16.2 %copy-start.2 = (f32[16,8,8,255]{3,0,2,1:T(8,128)S(1)}, f32[16,8,8,255]{3,0,2,1:T(8,128)}, u32[]{:S(2)}) copy-start(f32[16,8,8,255]{3,0,2,1:T(8,128)} %get-tuple-element.43) | copy-start | bytes 3133444
  25.8 8.4 %collective-permute-start.3 = (f32[6,6,128]{2,0,1:T(8,128)S(1)}, f32[6,6,128]{2,0,1:T(8,128)S(1)}, u32[]{:S(2)}, u32[]{:S(2)}) collective-permute-start(f32[6,6,128]{2,0,1:T(8,128)S(1)} %constant_dynamic-update-slice_fusion), channel_id=1, source_target_pairs={{4,0},{8,4},{12,8},{16,12},{20,16},{24,20},{28,24},{5,1},{9,5},{13... | collective-permute-start | bytes 55304 | tf_op jit(solution)/shard_map/ppermute | solution.py:25
  27.1 11.9 %collective-permute-start.2 = (f32[6,6,128]{2,0,1:T(8,128)S(1)}, f32[6,6,128]{2,0,1:T(8,128)S(1)}, u32[]{:S(2)}, u32[]{:S(2)}) collective-permute-start(f32[6,6,128]{2,0,1:T(8,128)S(1)} %constant_dynamic-update-slice_fusion), channel_id=1, source_target_pairs={{0,4},{4,8},{8,12},{12,16},{16,20},{20,24},{24,28},{1,5},{5,9},{9,... | collective-permute-start | bytes 55304 | tf_op jit(solution)/shard_map/ppermute | solution.py:23
  34.2 6.5 %collective-permute-start.4 = (f32[4,8,256]{2,0,1:T(4,128)S(1)}, f32[4,8,256]{2,0,1:T(4,128)S(1)}, u32[]{:S(2)}, u32[]{:S(2)}) collective-permute-start(f32[4,8,256]{2,0,1:T(4,128)S(1)} %fusion.111), channel_id=1, source_target_pairs={{0,4},{4,8},{8,12},{12,16},{16,20},{20,24},{24,28},{1,5},{5,9},{9,... | collective-permute-start | bytes 98312 | tf_op jit(solution)/shard_map/ppermute | solution.py:35
  41.4 3.5 %copy-start.1 = (s32[8,8,256]{2,1,0:T(8,128)S(1)}, s32[8,8,256]{2,1,0:T(8,128)}, u32[]{:S(2)}) copy-start(s32[8,8,256]{2,1,0:T(8,128)} %param.7) | copy-start | bytes 196612
  67.0 7.0 %collective-permute-start.10 = (f32[4,8,256]{2,0,1:T(4,128)S(1)}, f32[4,8,256]{2,0,1:T(4,128)S(1)}, u32[]{:S(2)}, u32[]{:S(2)}) collective-permute-start(f32[4,8,256]{2,0,1:T(4,128)S(1)} %fusion.107), channel_id=1, source_target_pairs={{0,1},{1,2},{2,3},{4,5},{5,6},{6,7},{8,9},{9,10},{10,11},{12,13},{... | collective-permute-start | bytes 98312 | tf_op jit(solution)/shard_map/ppermute | solution.py:35
  68.9 10.3 %collective-permute-start.11 = (f32[4,8,256]{2,0,1:T(4,128)S(1)}, f32[4,8,256]{2,0,1:T(4,128)S(1)}, u32[]{:S(2)}, u32[]{:S(2)}) collective-permute-start(f32[4,8,256]{2,0,1:T(4,128)S(1)} %fusion.106), channel_id=1, source_target_pairs={{1,0},{2,1},{3,2},{5,4},{6,5},{7,6},{9,8},{10,9},{11,10},{13,12},{... | collective-permute-start | bytes 98312 | tf_op jit(solution)/shard_map/ppermute | solution.py:35
  70.2 8.6 %collective-permute-start.8 = (f32[4,8,256]{2,0,1:T(4,128)S(1)}, f32[4,8,256]{2,0,1:T(4,128)S(1)}, u32[]{:S(2)}, u32[]{:S(2)}) collective-permute-start(f32[4,8,256]{2,0,1:T(4,128)S(1)} %fusion.109), channel_id=1, source_target_pairs={{0,4},{4,8},{8,12},{12,16},{16,20},{20,24},{24,28},{1,5},{5,9},{9,... | collective-permute-start | bytes 98312 | tf_op jit(solution)/shard_map/ppermute | solution.py:35
  72.7 5.9 %collective-permute-start.9 = (f32[4,8,256]{2,0,1:T(4,128)S(1)}, f32[4,8,256]{2,0,1:T(4,128)S(1)}, u32[]{:S(2)}, u32[]{:S(2)}) collective-permute-start(f32[4,8,256]{2,0,1:T(4,128)S(1)} %fusion.108), channel_id=1, source_target_pairs={{4,0},{8,4},{12,8},{16,12},{20,16},{24,20},{28,24},{5,1},{9,5},{13... | collective-permute-start | bytes 98312 | tf_op jit(solution)/shard_map/ppermute | solution.py:35
  96.1 7.2 %collective-permute-start.14 = (f32[4,8,256]{2,0,1:T(4,128)S(1)}, f32[4,8,256]{2,0,1:T(4,128)S(1)}, u32[]{:S(2)}, u32[]{:S(2)}) collective-permute-start(f32[4,8,256]{2,0,1:T(4,128)S(1)} %fusion.103), channel_id=1, source_target_pairs={{0,1},{1,2},{2,3},{4,5},{5,6},{6,7},{8,9},{9,10},{10,11},{12,13},{... | collective-permute-start | bytes 98312 | tf_op jit(solution)/shard_map/ppermute | solution.py:35
  98.0 10.3 %collective-permute-start.15 = (f32[4,8,256]{2,0,1:T(4,128)S(1)}, f32[4,8,256]{2,0,1:T(4,128)S(1)}, u32[]{:S(2)}, u32[]{:S(2)}) collective-permute-start(f32[4,8,256]{2,0,1:T(4,128)S(1)} %fusion.102), channel_id=1, source_target_pairs={{1,0},{2,1},{3,2},{5,4},{6,5},{7,6},{9,8},{10,9},{11,10},{13,12},{... | collective-permute-start | bytes 98312 | tf_op jit(solution)/shard_map/ppermute | solution.py:35
  99.3 8.6 %collective-permute-start.12 = (f32[4,8,256]{2,0,1:T(4,128)S(1)}, f32[4,8,256]{2,0,1:T(4,128)S(1)}, u32[]{:S(2)}, u32[]{:S(2)}) collective-permute-start(f32[4,8,256]{2,0,1:T(4,128)S(1)} %fusion.105), channel_id=1, source_target_pairs={{0,4},{4,8},{8,12},{12,16},{16,20},{20,24},{24,28},{1,5},{5,9},{9,... | collective-permute-start | bytes 98312 | tf_op jit(solution)/shard_map/ppermute | solution.py:35
  101.7 5.9 %collective-permute-start.13 = (f32[4,8,256]{2,0,1:T(4,128)S(1)}, f32[4,8,256]{2,0,1:T(4,128)S(1)}, u32[]{:S(2)}, u32[]{:S(2)}) collective-permute-start(f32[4,8,256]{2,0,1:T(4,128)S(1)} %fusion.104), channel_id=1, source_target_pairs={{4,0},{8,4},{12,8},{16,12},{20,16},{24,20},{28,24},{5,1},{9,5},{13... | collective-permute-start | bytes 98312 | tf_op jit(solution)/shard_map/ppermute | solution.py:35
  125.2 7.0 %collective-permute-start.18 = (f32[4,8,256]{2,0,1:T(4,128)S(1)}, f32[4,8,256]{2,0,1:T(4,128)S(1)}, u32[]{:S(2)}, u32[]{:S(2)}) collective-permute-start(f32[4,8,256]{2,0,1:T(4,128)S(1)} %fusion.99), channel_id=1, source_target_pairs={{0,1},{1,2},{2,3},{4,5},{5,6},{6,7},{8,9},{9,10},{10,11},{12,13},{... | collective-permute-start | bytes 98312 | tf_op jit(solution)/shard_map/ppermute | solution.py:35
  127.1 10.3 %collective-permute-start.19 = (f32[4,8,256]{2,0,1:T(4,128)S(1)}, f32[4,8,256]{2,0,1:T(4,128)S(1)}, u32[]{:S(2)}, u32[]{:S(2)}) collective-permute-start(f32[4,8,256]{2,0,1:T(4,128)S(1)} %fusion.98), channel_id=1, source_target_pairs={{1,0},{2,1},{3,2},{5,4},{6,5},{7,6},{9,8},{10,9},{11,10},{13,12},{... | collective-permute-start | bytes 98312 | tf_op jit(solution)/shard_map/ppermute | solution.py:35
  128.4 8.6 %collective-permute-start.16 = (f32[4,8,256]{2,0,1:T(4,128)S(1)}, f32[4,8,256]{2,0,1:T(4,128)S(1)}, u32[]{:S(2)}, u32[]{:S(2)}) collective-permute-start(f32[4,8,256]{2,0,1:T(4,128)S(1)} %fusion.101), channel_id=1, source_target_pairs={{0,4},{4,8},{8,12},{12,16},{16,20},{20,24},{24,28},{1,5},{5,9},{9,... | collective-permute-start | bytes 98312 | tf_op jit(solution)/shard_map/ppermute | solution.py:35
  130.8 5.9 %collective-permute-start.17 = (f32[4,8,256]{2,0,1:T(4,128)S(1)}, f32[4,8,256]{2,0,1:T(4,128)S(1)}, u32[]{:S(2)}, u32[]{:S(2)}) collective-permute-start(f32[4,8,256]{2,0,1:T(4,128)S(1)} %fusion.100), channel_id=1, source_target_pairs={{4,0},{8,4},{12,8},{16,12},{20,16},{24,20},{28,24},{5,1},{9,5},{13... | collective-permute-start | bytes 98312 | tf_op jit(solution)/shard_map/ppermute | solution.py:35

commit v2 on v0

v2 whole, which is shorter than its diff:
```python
import functools

import jax
import jax.numpy as jnp
import numpy as np
from jax import lax
from jax.experimental import pallas as pl
from jax.experimental.pallas import tpu as pltpu
from jax.sharding import PartitionSpec as P

SHARE = 4
STEPS = 4
TIME_STEP = 0.05
COUPLING = 1.5
BELOW, ABOVE, LEFT, RIGHT = range(4)
FACES = 4
LANES = 128
ROWS = 8
HIGHEST = lax.Precision.HIGHEST

VMEM = pl.BlockSpec(memory_space=pltpu.VMEM)
SMEM = pl.BlockSpec(memory_space=pltpu.SMEM)


def call(body, out_shape, in_specs, out_specs, scratch=(), flops=1000, size=1000):
    return pl.pallas_call(
        body,
        out_shape=out_shape,
        in_specs=in_specs,
        out_specs=out_specs,
        scratch_shapes=list(scratch),
        compiler_params=pltpu.CompilerParams(vmem_limit_bytes=20 << 20),
        cost_estimate=pl.CostEstimate(flops=flops, bytes_accessed=size, transcendentals=0),
    )


def f32(*shape):
    return jax.ShapeDtypeStruct(shape, jnp.float32)


def present(slabs, cols):
    s, c = lax.axis_index("slab"), lax.axis_index("col")
    return (s > 0, s < slabs - 1, c > 0, c < cols - 1)


def beside(slabs, cols):
    s, c = lax.axis_index("slab"), lax.axis_index("col")
    return (
        (jnp.maximum(s - 1, 0), c),
        (jnp.minimum(s + 1, slabs - 1), c),
        (s, jnp.maximum(c - 1, 0)),
        (s, jnp.minimum(c + 1, cols - 1)),
    )


def order_body(slabs, cols, slots, ids_ref, ids_smem, energy_ref, slots_ref, energy_out):
    s, c = lax.axis_index("slab"), lax.axis_index("col")
    sub = lax.broadcasted_iota(jnp.int32, (slots, LANES), 0)
    lane = lax.broadcasted_iota(jnp.int32, (slots, LANES), 1)
    own = jnp.zeros((slots, LANES), jnp.int32)
    own_energy = jnp.zeros((slots, LANES), jnp.float32)
    for q in range(slots):
        grain = ids_smem[s, c, q]
        own = jnp.where(sub == q, grain, own)
        own_energy = jnp.where(sub == q, energy_ref[grain], own_energy)
    one, zero = jnp.float32(1.0), jnp.float32(0.0)
    have = present(slabs, cols)
    matches, ranks = [], []
    for k, (ns, nc) in enumerate(beside(slabs, cols)):
        row = ids_ref[ns, pl.ds(nc, 1), :]
        row = jnp.concatenate([row, jnp.full((1, LANES - slots), -1, jnp.int32)], axis=1)
        row = jnp.broadcast_to(jnp.where(have[k], row, -1), (slots, LANES))
        hit = jnp.where((own == row) & (row >= 0), one, zero)
        shared = jnp.max(hit, axis=0, keepdims=True)
        matches.append(jnp.sum(hit, axis=1, keepdims=True))
        ranks.append(jnp.sum(jnp.where(row < own, shared, zero), axis=1, keepdims=True))
    free = one - (matches[0] + matches[1] + matches[2] + matches[3])
    subf = sub.astype(jnp.float32)
    lanef = lane.astype(jnp.float32)
    free_row = jnp.sum(jnp.where(sub == lane, free, zero), axis=0, keepdims=True)
    free_rank = jnp.sum(jnp.where(lane < sub, free_row, zero), axis=1, keepdims=True)
    place = jnp.zeros((slots, LANES), jnp.float32)
    skipped = jnp.int32(0)
    for k in range(FACES):
        at = matches[k] * (ranks[k] + k * SHARE - lanef)
        place = jnp.where((matches[k] > 0.5) & (jnp.abs(at) < 0.5), one, place)
        local = free_rank - (skipped * SHARE).astype(jnp.float32)
        inside = (local > -0.5) & (local < SHARE - 0.5) & (free > 0.5)
        inside = inside & jnp.logical_not(have[k])
        place = jnp.where(inside & (jnp.abs(local + k * SHARE - lanef) < 0.5), one, place)
        skipped = skipped + jnp.where(have[k], 0, 1)
    slot_row = jnp.sum(place * subf, axis=0, keepdims=True)
    energy_row = jnp.sum(place * own_energy, axis=0, keepdims=True)
    lane1 = lax.broadcasted_iota(jnp.int32, (1, LANES), 1)
    for q in range(slots):
        slots_ref[q] = jnp.sum(jnp.where(lane1 == q, slot_row, zero)).astype(jnp.int32)
        value = jnp.sum(jnp.where(lane1 == q, energy_row, zero), axis=1, keepdims=True)
        energy_out[q * ROWS : (q + 1) * ROWS, :] = jnp.broadcast_to(value, (ROWS, LANES))


def take(ref, at, rows, stride=1):
    half = ref.shape[0] // 2
    if stride == 1:
        if not isinstance(at, int):
            at = pl.multiple_of(at, ROWS)
        return ref[pl.ds(at, rows), :], ref[pl.ds(at + half, rows), :]
    return ref[pl.ds(at, rows, stride=stride), :], ref[pl.ds(at + half, rows, stride=stride), :]


def put(ref, at, i, value):
    if not isinstance(at, int):
        at = pl.multiple_of(at, ROWS)
    ref[pl.ds(at + i * (ref.shape[0] // 2), value.shape[0]), :] = value


def fill(out, index, pair):
    out[index, :, :LANES], out[index, :, LANES:] = pair


def pair_faces(axis, low, high):
    even = lax.rem(lax.axis_index(axis), 2) == 0
    return even, (jnp.where(even, high, low), jnp.where(even, low, high))


def pack_faces(fields, cx, cy, slots, out_refs, axis, columns):
    low, high = (LEFT, RIGHT) if columns else (BELOW, ABOVE)
    _, faces = pair_faces(axis, low, high)
    for out, face in zip(out_refs, faces):
        is_high = face == high
        for depth in range(2):
            if columns:
                first = jnp.where(is_high, cy - 1 - depth, depth)
                plane = lambda q: take(fields, q * (cx * cy) + first, cx, cy)
            else:
                first = jnp.where(is_high, cx - 1 - depth, depth) * cy
                plane = lambda q: take(fields, q * (cx * cy) + first, cy)
            for j in range(SHARE):
                fill(out, depth * SHARE + j, plane(face * SHARE + j))
            if depth == 0:
                s0 = s1 = None
                for q in range(slots):
                    v0, v1 = plane(q)
                    s0 = v0 * v0 if s0 is None else s0 + v0 * v0
                    s1 = v1 * v1 if s1 is None else s1 + v1 * v1
                fill(out, 2 * SHARE, (s0, s1))


def open_body(cx, cy, slots, fields_raw, mask_ref, coarse_ref, slots_ref, fields, msg_a, msg_b, mask_halves):
    cells = cx * cy
    for q in range(slots):
        at = pl.multiple_of(slots_ref[q] * cells, cells)
        for i in range(2):
            put(fields, q * cells, i, fields_raw[pl.ds(at, cells), i * LANES : (i + 1) * LANES])
    for i in range(2):
        put(mask_halves, 0, i, mask_ref[:, i * LANES : (i + 1) * LANES].astype(jnp.float32))
    pack_faces(fields, cx, cy, slots, (msg_a, msg_b), "col", True)
    _, faces = pair_faces("col", LEFT, RIGHT)
    capacity, coarse_y, _ = coarse_ref.shape
    for out, face in zip((msg_a, msg_b), faces):
        first = jnp.where(face == RIGHT, cy - 1, 0)
        fill(out, 2 * SHARE + 1, take(mask_halves, first, cx, cy))
        out[2 * SHARE + 2] = jnp.zeros((ROWS, out.shape[2]), jnp.float32)
        row = jnp.where(face == RIGHT, coarse_y - 1, 0)
        for p in range(capacity):
            out[2 * SHARE + 2, p : p + 1, :LANES] = coarse_ref[p, pl.ds(row, 1), :]


def slab_body(
    cx, cy, slots, slabs, cols, fields, mask_ref, coarse_ref, rows_ref, got_a, got_b, msg_a, msg_b, planes
):
    capacity, coarse_y, _ = coarse_ref.shape
    have = present(slabs, cols)
    even, _ = pair_faces("col", LEFT, RIGHT)
    thermal = 2 * SHARE + 2
    for p in range(capacity):
        from_a = got_a[thermal, p : p + 1, :LANES]
        from_b = got_b[thermal, p : p + 1, :LANES]
        lower = jnp.where(even, from_b, from_a)
        upper = jnp.where(even, from_a, from_b)
        base = p * ROWS
        planes[base : base + ROWS, :] = jnp.zeros((ROWS, LANES), jnp.float32)
        planes[base : base + 1, :] = jnp.where(have[LEFT], lower, coarse_ref[p, 0:1, :])
        planes[base + 1 : base + 1 + coarse_y, :] = coarse_ref[p]
        planes[base + 1 + coarse_y : base + 2 + coarse_y, :] = jnp.where(
            have[RIGHT], upper, coarse_ref[p, coarse_y - 1 : coarse_y, :]
        )
    pack_faces(fields, cx, cy, slots, (msg_a, msg_b), "slab", False)
    _, faces = pair_faces("slab", BELOW, ABOVE)
    live = rows_ref[lax.axis_index("slab")]
    for out, face in zip((msg_a, msg_b), faces):
        first = jnp.where(face == ABOVE, cx - 1, 0) * cy
        out[2 * SHARE + 1] = mask_ref[pl.ds(pl.multiple_of(first, ROWS), cy), :].astype(jnp.float32)
        row = jnp.where(face == ABOVE, live - 2, 0) * ROWS
        out[thermal, :, :LANES] = planes[pl.ds(pl.multiple_of(row, ROWS), ROWS), :]
        out[thermal, :, LANES:] = planes[pl.ds(pl.multiple_of(row + ROWS, ROWS), ROWS), :]


def axis_weights(cells):
    fine = np.arange(-1, cells + 1)
    lower = (2 * fine - 1) // 4
    weight = (2 * fine - 1 - 4 * lower) / 4.0
    out = np.zeros((cells + 2, cells // 2 + 2), np.float32)
    out[np.arange(cells + 2), lower + 1] += 1.0 - weight
    out[np.arange(cells + 2), lower + 2] += weight
    return out


def plane_weights(cx, cy):
    along, across = axis_weights(cx), axis_weights(cy)
    inner = [(x + 1, y + 1) for x in range(cx) for y in range(cy)]
    inner += [(0, y + 1) for y in range(cy)] + [(cx + 1, y + 1) for y in range(cy)]
    inner += [(x + 1, 0) for x in range(cx)] + [(x + 1, cy + 1) for x in range(cx)]
    out = np.zeros((len(inner), cx // 2 + 2, ROWS), np.float32)
    for row, (x, y) in enumerate(inner):
        out[row, :, : cy // 2 + 2] = along[x][:, None] * across[y][None, :]
    return out.reshape(len(inner), -1)


def height_weights(cells, coarse):
    fine = np.arange(cells)
    lower = (2 * fine - 1) // 4
    weight = (2 * fine - 1 - 4 * lower) / 4.0
    out = np.zeros((coarse, cells), np.float32)
    np.add.at(out, (np.clip(lower, 0, coarse - 1), fine), 1.0 - weight)
    np.add.at(out, (np.clip(lower + 1, 0, coarse - 1), fine), weight)
    return out


def mobility_body(
    cx, cy, slabs, cols, planes, rows_ref, mask_ref, weights, height, col_a, col_b, slab_a, slab_b, rate_ref, near
):
    s = lax.axis_index("slab")
    start = jnp.int32(0)
    for t in range(slabs):
        start = start + jnp.where(t < s, rows_ref[t], 0)
    end = start + rows_ref[s]
    even_s, _ = pair_faces("slab", BELOW, ABOVE)
    even_c, _ = pair_faces("col", LEFT, RIGHT)
    thermal, mask = 2 * SHARE + 2, 2 * SHARE + 1
    below = jnp.where(even_s, slab_b[thermal], slab_a[thermal])
    above = jnp.where(even_s, slab_a[thermal], slab_b[thermal])
    capacity = planes.shape[0] // ROWS
    for i in range(cx // 2 + 2):
        p = jnp.clip(s * (cx // 2) - 1 + i, 0, slabs * (cx // 2) - 1)
        own = planes[pl.ds(pl.multiple_of(jnp.clip(p - start, 0, capacity - 1) * ROWS, ROWS), ROWS), :]
        lower = jnp.where(p == start - 2, below[:, :LANES], below[:, LANES:])
        upper = jnp.where(p == end, above[:, :LANES], above[:, LANES:])
        near[i * ROWS : (i + 1) * ROWS, :] = jnp.where(p < start, lower, jnp.where(p < end, own, upper))
    flat = jnp.dot(weights[...], near[...], precision=HIGHEST, preferred_element_type=jnp.float32)
    profile = jnp.dot(flat, height[...], precision=HIGHEST, preferred_element_type=jnp.float32)
    mobility = jnp.exp(2.0 * (profile - 1.0)) * TIME_STEP
    cells = cx * cy
    rate_ref[0:cells, :] = mask_ref[...].astype(jnp.float32) * mobility[:cells]
    have = present(slabs, cols)
    masks = (
        jnp.where(even_s, slab_b[mask], slab_a[mask]),
        jnp.where(even_s, slab_a[mask], slab_b[mask]),
        jnp.where(even_c, col_b[mask], col_a[mask]),
        jnp.where(even_c, col_a[mask], col_b[mask]),
    )
    for k in range(FACES):
        at = cells + k * ROWS
        rate_ref[at : at + ROWS, :] = jnp.where(have[k], masks[k] * mobility[at : at + ROWS], 0.0)


def split(value):
    return value[:, :LANES], value[:, LANES:]


def along_height(v0, v1, first, last):
    r0, r1 = pltpu.roll(v0, 1, 1), pltpu.roll(v1, 1, 1)
    q0, q1 = pltpu.roll(v0, LANES - 1, 1), pltpu.roll(v1, LANES - 1, 1)
    return (
        jnp.where(first, 0.0, r0) + jnp.where(last, q1, q0),
        jnp.where(first, r0, r1) + jnp.where(last, 0.0, q1),
    )


def along_rows(v, top, bottom, lower, upper):
    down = jnp.where(top, 0.0 if lower is None else lower, pltpu.roll(v, 1, 0))
    up = jnp.where(bottom, 0.0 if upper is None else upper, pltpu.roll(v, ROWS - 1, 0))
    return down + up


def edges():
    lane = lax.broadcasted_iota(jnp.int32, (ROWS, LANES), 1)
    row = lax.broadcasted_iota(jnp.int32, (ROWS, LANES), 0)
    return lane == 0, lane == LANES - 1, row == 0, row == ROWS - 1


def spread_row(ref, base, x):
    row = ref[pl.ds(base + x, 1), :]
    return split(jnp.broadcast_to(row, (ROWS, 2 * LANES)))


def neighbours(x, last_x, load, centre, halo, kind, marks):
    first, last, top, bottom = marks
    v0, v1 = centre
    n0, n1 = along_height(v0, v1, first, last)
    low = high = (None, None)
    if kind == LEFT:
        low = halo(x)
    if kind == RIGHT:
        high = halo(x)
    n0 = n0 + along_rows(v0, top, bottom, low[0], high[0])
    n1 = n1 + along_rows(v1, top, bottom, low[1], high[1])
    sides = []
    if not (isinstance(x, int) and x == 0):
        sides.append(load(x - 1))
    elif kind == BELOW:
        sides.append(halo(None))
    if not (isinstance(x, int) and x == last_x):
        sides.append(load(x + 1))
    elif kind == ABOVE:
        sides.append(halo(None))
    for a, b in sides:
        n0, n1 = n0 + a, n1 + b
    return n0, n1


def over_planes(cx, visit, carry):
    carry = visit(0, carry)
    carry = lax.fori_loop(1, cx - 1, visit, carry)
    return visit(cx - 1, carry)


def slot_access(fields, halos, q, cells, cy):
    def load(x):
        return take(fields, q * cells + x * cy, cy)

    def halo(x):
        if x is None:
            return split(halos[q * ROWS : (q + 1) * ROWS, :])
        return spread_row(halos, q * ROWS, x)

    return load, halo


def plane_of(ref, base, x, cy):
    at = base + x * cy
    if not isinstance(x, int):
        at = pl.multiple_of(at, ROWS)
    return split(ref[pl.ds(at, cy), :])


def force_of(v, n, squares3, energy):
    return v * (squares3 + ((5.0 - energy) + v * (energy - 2.0 * v))) - n


def triple_squares(fields, x, slots, cells, cy):
    total = None
    for q in range(slots):
        v0, v1 = take(fields, q * cells + x * cy, cy)
        total = (v0 * v0, v1 * v1) if total is None else (total[0] + v0 * v0, total[1] + v1 * v1)
    return 2.0 * COUPLING * total[0], 2.0 * COUPLING * total[1]


def sums_body(
    cx, cy, slots, slabs, cols, devices, fields, rate_ref, energy, col_a, col_b, slab_a, slab_b,
    grown, grown_halo, sums_ref, halos, field_sum,
):
    cells = cx * cy
    marks = edges()
    first, last, top, bottom = marks
    have = present(slabs, cols)
    even_s, _ = pair_faces("slab", BELOW, ABOVE)
    even_c, _ = pair_faces("col", LEFT, RIGHT)
    arrived = ((slab_b, slab_a, even_s), (slab_a, slab_b, even_s), (col_b, col_a, even_c), (col_a, col_b, even_c))

    for k, (if_even, if_odd, even) in enumerate(arrived):
        pick = lambda i: jnp.where(even, if_even[i], if_odd[i])
        s0, s1 = split(2.0 * COUPLING * pick(2 * SHARE))
        h0, h1 = split(rate_ref[cells + k * ROWS : cells + (k + 1) * ROWS, :])
        for j in range(SHARE):
            q = k * SHARE + j
            plane = jnp.where(have[k], pick(j), 0.0)
            halos[q * ROWS : (q + 1) * ROWS, :] = plane
            v0, v1 = split(plane)
            o0, o1 = split(pick(SHARE + j))
            if k == BELOW:
                i0, i1 = take(fields, q * cells, cy)
            elif k == ABOVE:
                i0, i1 = take(fields, (q + 1) * cells - cy, cy)
            elif k == LEFT:
                i0, i1 = take(fields, q * cells, cx, cy)
            else:
                i0, i1 = take(fields, q * cells + cy - 1, cx, cy)
            n0, n1 = along_height(v0, v1, first, last)
            n0 = n0 + along_rows(v0, top, bottom, None, None) + o0 + i0
            n1 = n1 + along_rows(v1, top, bottom, None, None) + o1 + i1
            e = energy[q * ROWS : (q + 1) * ROWS, :]
            grown_halo[q * ROWS : (q + 1) * ROWS, :LANES] = v0 - h0 * force_of(v0, n0, s0, e)
            grown_halo[q * ROWS : (q + 1) * ROWS, LANES:] = v1 - h1 * force_of(v1, n1, s1, e)

    energy_sum = None
    for q in range(slots):
        e = energy[q * ROWS : (q + 1) * ROWS, :]
        energy_sum = e if energy_sum is None else energy_sum + e
    zero = jnp.zeros((ROWS, LANES), jnp.float32)

    def visit(x, carry):
        total, c0, c1, c2, c3, weight = carry
        squares = triple_squares(fields, x, slots, cells, cy)
        rate = plane_of(rate_ref, 0, x, cy)
        forces, powers = [zero, zero], [zero, zero]
        a1, a2, b1 = [zero, zero], [zero, zero], [zero, zero]
        for q in range(slots):
            load, halo = slot_access(fields, halos, q, cells, cy)
            centre = load(x)
            near = neighbours(x, cx - 1, load, centre, halo, q // SHARE, marks)
            e = energy[q * ROWS : (q + 1) * ROWS, :]
            for i in range(2):
                force = force_of(centre[i], near[i], squares[i], e)
                g = centre[i] - rate[i] * force
                put(grown, q * cells + x * cy, i, g)
                forces[i] = forces[i] + force
                powers[i] = powers[i] + g * ((5.0 - e) + g * (e - 2.0 * g))
                a1[i] = a1[i] + g
                a2[i] = a2[i] + g * g
                b1[i] = b1[i] + e * g
        at = x * cy if isinstance(x, int) else pl.multiple_of(x * cy, ROWS)
        for i in range(2):
            h = rate[i]
            field_sum[pl.ds(at, cy), i * LANES : (i + 1) * LANES] = a1[i]
            total = total + h * forces[i]
            c0 = c0 + h * (powers[i] + 2.0 * COUPLING * a1[i] * a2[i])
            linear = (
                energy_sum
                - 5.0 * slots
                - 2.0 * b1[i]
                + (6.0 - 2.0 * COUPLING * slots) * a2[i]
                - 4.0 * COUPLING * (a1[i] * a1[i])
            )
            c1 = c1 + h * h * linear
            c2 = c2 + h * h * h * (energy_sum + (6.0 * COUPLING * slots - 6.0) * a1[i])
            c3 = c3 + (h * h) * (h * h)
            weight = weight + h
        return total, c0, c1, c2, c3, weight

    total, c0, c1, c2, c3, weight = over_planes(cx, visit, (zero,) * 6)

    def face_sum(k, x):
        base = k * SHARE * ROWS
        if x is None:
            parts = [split(grown_halo[base + j * ROWS : base + (j + 1) * ROWS, :]) for j in range(SHARE)]
            rate = split(rate_ref[cells + k * ROWS : cells + (k + 1) * ROWS, :])
        else:
            parts = [spread_row(grown_halo, base + j * ROWS, x) for j in range(SHARE)]
            rate = spread_row(rate_ref, cells + k * ROWS, x)
        g = [parts[0][i] + parts[1][i] + parts[2][i] + parts[3][i] for i in range(2)]
        return g, rate

    def visit_sum(x, carry):
        c0, c1 = carry
        left, right = face_sum(LEFT, x), face_sum(RIGHT, x)
        rate = plane_of(rate_ref, 0, x, cy)
        sums = []
        for source, base, factor in ((field_sum, 0, 0), (rate_ref, 0, 1)):
            load = lambda y: plane_of(source, base, y, cy)
            v = load(x)
            near = list(along_height(v[0], v[1], first, last))
            for i in range(2):
                near[i] = near[i] + along_rows(v[i], top, bottom, None, None)
                if not (isinstance(x, int) and x == 0):
                    near[i] = near[i] + load(x - 1)[i]
                if not (isinstance(x, int) and x == cx - 1):
                    near[i] = near[i] + load(x + 1)[i]
                if factor:
                    near[i] = near[i] * float(slots)
                scale = float(SHARE) if factor else 1.0
                near[i] = near[i] + jnp.where(top, left[factor][i] * scale, 0.0)
                near[i] = near[i] + jnp.where(bottom, right[factor][i] * scale, 0.0)
                if isinstance(x, int):
                    near[i] = near[i] + face_sum(BELOW if x == 0 else ABOVE, None)[factor][i] * scale
            sums.append(near)
        for i in range(2):
            c0 = c0 - rate[i] * sums[0][i]
            c1 = c1 + rate[i] * sums[1][i]
        return c0, c1

    c0, c1 = over_planes(cx, visit_sum, (c0, c1))
    back = -1.0 / TIME_STEP
    scales = (back, back, back, back, back * (2.0 * slots - 2.0 * COUPLING * slots * slots), 1.0 / TIME_STEP)
    lane = lax.broadcasted_iota(jnp.int32, (1, LANES), 1)
    row = jnp.zeros((1, LANES), jnp.float32)
    for i, (part, scale) in enumerate(zip((total, c0, c1, c2, c3, weight), scales)):
        value = jnp.sum(jnp.sum(part, axis=0, keepdims=True), axis=1, keepdims=True) * scale
        row = jnp.where(lane == i, value, row)
    sums_ref[...] = jnp.broadcast_to(row[None], (devices, 1, LANES))


def multipliers(got, slots):
    total = jnp.sum(got[...], axis=0)
    lane = lax.broadcasted_iota(jnp.int32, (1, LANES), 1)
    part = [jnp.sum(jnp.where(lane == i, total, 0.0), axis=1, keepdims=True) for i in range(6)]
    whole = slots * part[5]
    here = part[0] / whole
    later = (part[1] + here * (part[2] + here * (part[3] + here * part[4]))) / whole
    spread = lambda value: jnp.broadcast_to(value, (ROWS, LANES))
    return spread(here), spread(later)


def advance(cx, cy, slots, got, grown, grown_halo, rate_ref, energy, halos, now, squares_ref, store):
    cells = cx * cy
    marks = edges()
    here, later = multipliers(got, slots)
    for k in range(FACES):
        h0, h1 = split(rate_ref[cells + k * ROWS : cells + (k + 1) * ROWS, :])
        for q in range(k * SHARE, (k + 1) * SHARE):
            v0, v1 = split(grown_halo[q * ROWS : (q + 1) * ROWS, :])
            halos[q * ROWS : (q + 1) * ROWS, :LANES] = v0 - here * h0
            halos[q * ROWS : (q + 1) * ROWS, LANES:] = v1 - here * h1

    def settle(x, carry):
        base = pl.multiple_of(x * cy, ROWS)
        h = split(rate_ref[pl.ds(base, cy), :])
        off = [here * h[i] for i in range(2)]
        squares = [None, None]
        for q in range(slots):
            at = q * cells + x * cy
            v = take(grown, at, cy)
            for i in range(2):
                f = v[i] - off[i]
                put(now, at, i, f)
                squares[i] = f * f if squares[i] is None else squares[i] + f * f
        for i in range(2):
            squares_ref[pl.ds(base, cy), i * LANES : (i + 1) * LANES] = 2.0 * COUPLING * squares[i]
        return carry

    lax.fori_loop(0, cx, settle, 0)

    def visit(x, carry):
        squares = plane_of(squares_ref, 0, x, cy)
        rate = plane_of(rate_ref, 0, x, cy)
        for q in range(slots):
            load, halo = slot_access(now, halos, q, cells, cy)
            centre = load(x)
            near = neighbours(x, cx - 1, load, centre, halo, q // SHARE, marks)
            e = energy[q * ROWS : (q + 1) * ROWS, :]
            for i in range(2):
                force = force_of(centre[i], near[i], squares[i], e)
                store(q, x, i, centre[i] - rate[i] * (force + later))
        return carry

    over_planes(cx, visit, 0)


def middle_body(
    cx, cy, slots, got, grown, grown_halo, rate_ref, energy, fields, col_a, col_b, slab_a, slab_b,
    halos, now, squares_ref,
):
    cells = cx * cy

    def store(q, x, i, value):
        put(fields, q * cells + x * cy, i, value)

    advance(cx, cy, slots, got, grown, grown_halo, rate_ref, energy, halos, now, squares_ref, store)
    pack_faces(fields, cx, cy, slots, (slab_a, slab_b), "slab", False)
    pack_faces(fields, cx, cy, slots, (col_a, col_b), "col", True)


def last_body(cx, cy, slots, got, grown, grown_halo, rate_ref, energy, slots_ref, out, halos, now, squares_ref):
    cells = cx * cy

    def store(q, x, i, value):
        at = pl.multiple_of(slots_ref[q] * cells + x * cy, ROWS)
        out[pl.ds(at, cy), i * LANES : (i + 1) * LANES] = value

    advance(cx, cy, slots, got, grown, grown_halo, rate_ref, energy, halos, now, squares_ref, store)


def exchange(first, second, axis):
    count = lax.axis_size(axis)
    one = [(i, i ^ 1) for i in range(count)]
    two = [(i, (i - 1) % count if i % 2 == 0 else (i + 1) % count) for i in range(count)]
    return lax.ppermute(first, axis, one), lax.ppermute(second, axis, two)


def per_device(order_params, layer_mask, coarse_temp, coarse_rows, grain_ids, energy):
    slots, cx, cy, cz = order_params.shape
    slabs, cols = lax.axis_size("slab"), lax.axis_size("col")
    devices = slabs * cols
    cells = cx * cy
    capacity, _, coarse_z = coarse_temp.shape
    raw = order_params.reshape(slots * cells, cz)
    mask = layer_mask.reshape(cells, cz)
    wide = FACES * ROWS
    message = f32(2 * SHARE + 3, ROWS, cz)
    short = f32(2 * SHARE + 1, ROWS, cz)
    state = f32(2 * slots * cells, cz // 2)
    halo = f32(slots * ROWS, cz)

    slot_order, slot_energy = call(
        functools.partial(order_body, slabs, cols, slots),
        (jax.ShapeDtypeStruct((slots,), jnp.int32), f32(slots * ROWS, LANES)),
        [VMEM, SMEM, SMEM],
        (SMEM, VMEM),
    )(grain_ids, grain_ids, energy)
    fields, col_a, col_b = call(
        functools.partial(open_body, cx, cy, slots),
        (state, message, message),
        [VMEM, VMEM, VMEM, SMEM],
        (VMEM,) * 3,
        [pltpu.VMEM((2 * cells, cz // 2), jnp.float32)],
    )(raw, mask, coarse_temp, slot_order)
    col_a, col_b = exchange(col_a, col_b, "col")
    slab_a, slab_b, planes = call(
        functools.partial(slab_body, cx, cy, slots, slabs, cols),
        (message, message, f32(capacity * ROWS, LANES)),
        [VMEM, VMEM, VMEM, SMEM, VMEM, VMEM],
        (VMEM,) * 3,
    )(fields, mask, coarse_temp, coarse_rows, col_a, col_b)
    slab_a, slab_b = exchange(slab_a, slab_b, "slab")
    weights = jnp.asarray(plane_weights(cx, cy))
    height = jnp.asarray(height_weights(cz, coarse_z))
    rate = call(
        functools.partial(mobility_body, cx, cy, slabs, cols),
        f32(cells + wide, cz),
        [VMEM, SMEM] + [VMEM] * 7,
        VMEM,
        [pltpu.VMEM(((cx // 2 + 2) * ROWS, LANES), jnp.float32)],
    )(planes, coarse_rows, mask, weights, height, col_a, col_b, slab_a, slab_b)

    buffers = [pltpu.VMEM(halo.shape, jnp.float32), pltpu.VMEM(state.shape, jnp.float32)]
    buffers += [pltpu.VMEM((cells, cz), jnp.float32)]
    for pair in range(STEPS // 2):
        grown, grown_halo, sums = call(
            functools.partial(sums_body, cx, cy, slots, slabs, cols, devices),
            (state, halo, f32(devices, 1, LANES)),
            [VMEM] * 7,
            (VMEM,) * 3,
            [pltpu.VMEM(halo.shape, jnp.float32), pltpu.VMEM((cells, cz), jnp.float32)],
        )(fields, rate, slot_energy, col_a, col_b, slab_a, slab_b)
        got = lax.all_to_all(sums, ("slab", "col"), 0, 0)
        if pair < STEPS // 2 - 1:
            fields, col_a, col_b, slab_a, slab_b = call(
                functools.partial(middle_body, cx, cy, slots),
                (state, short, short, short, short),
                [VMEM] * 5,
                (VMEM,) * 5,
                buffers,
            )(got, grown, grown_halo, rate, slot_energy)
            slab_a, slab_b = exchange(slab_a, slab_b, "slab")
            col_a, col_b = exchange(col_a, col_b, "col")
        else:
            fields = call(
                functools.partial(last_body, cx, cy, slots),
                f32(slots * cells, cz),
                [VMEM] * 5 + [SMEM],
                VMEM,
                buffers,
            )(got, grown, grown_halo, rate, slot_energy, slot_order)
    return fields.reshape(order_params.shape)


def solution(mesh):
    in_specs = (
        P(None, "slab", "col", None),
        P("slab", "col", None),
        P("slab", "col", None),
        P(),
        P(),
        P(),
    )
    out_specs = P(None, "slab", "col", None)
    return jax.shard_map(
        per_device, mesh=mesh, in_specs=in_specs, out_specs=out_specs, check_vma=False
    )
```

time: 279 us -> 62.1 us (0.22)
  blocking collectives: 174 us -> 21.5 us
  starting transfers between devices: 46.9 us -> 11 us
  other arithmetic: 15.9 us -> 0 us
  Pallas kernels: 0 us -> 13.5 us
  local copies, waits for them, and re-layouts: 13.9 us -> 3.47 us
  matrix products: 10 us -> 0 us
  between operations: 4.05 us -> 0.1 us
    psum x4 -> x0, blocking collectives: 174 us -> none  [total_rate(): return lax.psum(local_rate, ('slab', 'col'))]
    ppermute x20 -> x8, starting transfers between devices: 46.9 us -> 11 us  [exchange(): return (lax.ppermute(first, axis, one), lax.ppermute(second, axis, two))]
    all_to_all x0 -> x2, blocking collectives: none -> 21.5 us  [per_device(): got = lax.all_to_all(sums, ('slab', 'col'), 0, 0)]
    pallas_call x0 -> x8, Pallas kernels: none -> 13.5 us  [the longest x2 4.58 us: per_device(): call(functools.partial(sums_body, cx, cy, slots, slabs, cols, devices), (...]
    dot_general x39 -> x0, matrix products: 10 us -> none  [the longest x32 8.33 us: apply_slots(): jnp.einsum('qr,ryz->qyz', matrix, face_cells, precision=FULL_ACCURACY)]
    slice x14 -> x0, local copies, waits for them, and re-layouts: 9.47 us -> none  [the longest x4 2.48 us: per_device(): z_low = jnp.concatenate([zero_plane, fields[..., :-1]], axis=3)]
    sub x14 -> x0, other arithmetic: 7.86 us -> none  [the longest x4 6.9 us: rates(): squares - fields * fields]
    reduce_sum x6 -> x0, other arithmetic: 3.47 us -> none  [the longest x3 1.85 us: per_device(): local_rate = jnp.sum(deposited * jnp.sum(rate, axis=0))]
  transfers between devices with their start and end apart: 20 -> 8, of which waited for: 3 -> 6; matrix products, arithmetic and copies ran while one was open for 7% -> 0% of each run, Pallas kernels for 0% -> 0%
where the time goes in v2:
time: 62.1 us; the launch traced here: 61.8 us
  blocking collectives  21.5 us (35%)
  Pallas kernels  13.5 us (22%)
  waiting for transfers between devices  12.3 us (20%)
  starting transfers between devices  11 us (18%)
  local copies, waits for them, and re-layouts  3.47 us (6%)
    all_to_all x2, blocking collectives, per_device(): got = lax.all_to_all(sums, ('slab', 'col'), 0, 0)  21.5 us
    ppermute x8, waiting for transfers between devices, exchange(): return (lax.ppermute(first, axis, one), lax.ppermute(second, axis, two))  12.3 us
    ppermute x8, starting transfers between devices, exchange(): return (lax.ppermute(first, axis, one), lax.ppermute(second, axis, two))  11 us
    pallas_call x2, Pallas kernels, per_device(): call(functools.partial(sums_body, cx, cy, slots, slabs, cols, devices), (...  4.58 us
    unnamed x16, local copies, waits for them, and re-layouts  3.47 us
    pallas_call x1, Pallas kernels, per_device(): call(functools.partial(last_body, cx, cy, slots), f32(slots * cells, cz),...  3.07 us
    pallas_call x1, Pallas kernels, per_device(): call(functools.partial(order_body, slabs, cols, slots), (jax.ShapeDtypeSt...  1.78 us
    pallas_call x1, Pallas kernels, per_device(): call(functools.partial(middle_body, cx, cy, slots), (state, short, short,...  1.71 us
  transfers between devices with their start and end apart: 8, of which 6 were waited for; matrix products, arithmetic and copies ran while one was open for 0% of the time, Pallas kernels for 0%

profile of v2, /device:TPU:0, one launch (start us, length us, event | category | flops | bytes accessed | tf_op | source)
XLA Modules:
  0.0 61.8 jit_solution(6377107928225578955)
XLA Ops:
  0.0 0.7 %copy-done.3 = s32[8,4,16]{2,1,0:T(4,128)S(1)} copy-done((s32[8,4,16]{2,1,0:T(4,128)S(1)}, s32[8,4,16]{2,1,0:T(4,128)}, u32[]{:S(2)}) %copy-start.3) | copy-done | bytes 2072
  0.7 0.7 %copy-done.7 = f32[304]{0:T(512)S(1)} copy-done((f32[304]{0:T(512)S(1)}, f32[304]{0:T(512)}, u32[]{:S(2)}) %copy-start.7) | copy-done | bytes 1240
  1.4 1.8 %shard_map.82 = (s32[16]{0:T(128)S(1)}, f32[128,128]{1,0:T(8,128)S(1)}) custom-call(s32[8,4,16]{2,1,0:T(4,128)S(1)} %copy-done.3, s32[8,4,16]{2,1,0:T(4,128)S(1)} %copy-done.3, f32[304]{0:T(512)S(1)} %copy-done.7), custom_call_target="tpu_custom_call" | custom-call | flops 1000 | bytes 1000 | tf_op jit(solution)/shard_map/pallas_call | solution.py:593
  3.2 0.0 copy-done.4
  3.2 0.0 copy-start
  3.2 1.2 %copy-done = f32[16,8,8,256]{3,2,1,0:T(8,128)S(1)} copy-done((f32[16,8,8,256]{3,2,1,0:T(8,128)S(1)}, f32[16,8,8,256]{3,2,1,0:T(8,128)}, u32[]{:S(2)}) %copy-start) | copy-done | bytes 1048600
  4.4 0.8 %copy-done.1 = s32[8,8,256]{2,1,0:T(8,128)S(1)} copy-done((s32[8,8,256]{2,1,0:T(8,128)S(1)}, s32[8,8,256]{2,1,0:T(8,128)}, u32[]{:S(2)}) %copy-start.1) | copy-done | bytes 65560
  5.3 0.7 %shard_map.83 = (f32[2048,128]{1,0:T(8,128)S(1)}, f32[11,8,256]{2,1,0:T(8,128)S(1)}, f32[11,8,256]{2,1,0:T(8,128)S(1)}) custom-call(f32[1024,256]{1,0:T(8,128)S(1)} %bitcast.3, s32[64,256]{1,0:T(8,128)S(1)} %bitcast.4, f32[6,4,128]{2,1,0:T(4,128)S(1)} %copy-done.4, s32[16]{0:T(128)S(1)} %get-tuple-element.24.slots_ref), custom_call_target="tpu_custom_call" | custom-call | flops 1000 | bytes 1000 | tf_op jit(solution)/shard_map/pallas_call | solution.py:599
  6.0 0.5 collective-permute-start
  6.5 2.6 %collective-permute-start.1 = (f32[11,8,256]{2,1,0:T(8,128)S(1)}, f32[11,8,256]{2,1,0:T(8,128)S(1)}, u32[]{:S(2)}, u32[]{:S(2)}) collective-permute-start(f32[11,8,256]{2,1,0:T(8,128)S(1)} %get-tuple-element.27), channel_id=1, source_target_pairs={{0,3},{1,2},{2,1},{3,0},{4,7},{5,6},{6,5},{7,4},{8,11},{9,10},{10,... | collective-permute-start | bytes 270344 | tf_op jit(solution)/shard_map/ppermute | solution.py:576
  9.2 0.0 collective-permute-done.got_a.col_a
  9.2 2.9 %collective-permute-done.1.got_b.col_b = f32[11,8,256]{2,1,0:T(8,128)S(1)} collective-permute-done((f32[11,8,256]{2,1,0:T(8,128)S(1)}, f32[11,8,256]{2,1,0:T(8,128)S(1)}, u32[]{:S(2)}, u32[]{:S(2)}) %collective-permute-start.1) | collective-permute-done | bytes 90144 | tf_op jit(solution)/shard_map/ppermute | solution.py:576
  12.1 0.6 shard_map.84
  12.7 1.5 %collective-permute-start.2 = (f32[11,8,256]{2,1,0:T(8,128)S(1)}, f32[11,8,256]{2,1,0:T(8,128)S(1)}, u32[]{:S(2)}, u32[]{:S(2)}) collective-permute-start(f32[11,8,256]{2,1,0:T(8,128)S(1)} %get-tuple-element.29), channel_id=1, source_target_pairs={{0,4},{4,0},{8,12},{12,8},{16,20},{20,16},{24,28},{28,24},{1,5},{5... | collective-permute-start | bytes 270344 | tf_op jit(solution)/shard_map/ppermute | solution.py:576
  14.2 3.6 %collective-permute-start.3 = (f32[11,8,256]{2,1,0:T(8,128)S(1)}, f32[11,8,256]{2,1,0:T(8,128)S(1)}, u32[]{:S(2)}, u32[]{:S(2)}) collective-permute-start(f32[11,8,256]{2,1,0:T(8,128)S(1)} %get-tuple-element.30), channel_id=1, source_target_pairs={{0,28},{4,8},{8,4},{12,16},{16,12},{20,24},{24,20},{28,0},{1,29},{... | collective-permute-start | bytes 270344 | tf_op jit(solution)/shard_map/ppermute | solution.py:576
  17.7 0.8 %collective-permute-done.2.slab_a = f32[11,8,256]{2,1,0:T(8,128)S(1)} collective-permute-done((f32[11,8,256]{2,1,0:T(8,128)S(1)}, f32[11,8,256]{2,1,0:T(8,128)S(1)}, u32[]{:S(2)}, u32[]{:S(2)}) %collective-permute-start.2) | collective-permute-done | bytes 90144 | tf_op jit(solution)/shard_map/ppermute | solution.py:576
  18.5 3.0 %collective-permute-done.3.slab_b = f32[11,8,256]{2,1,0:T(8,128)S(1)} collective-permute-done((f32[11,8,256]{2,1,0:T(8,128)S(1)}, f32[11,8,256]{2,1,0:T(8,128)S(1)}, u32[]{:S(2)}, u32[]{:S(2)}) %collective-permute-start.3) | collective-permute-done | bytes 90144 | tf_op jit(solution)/shard_map/ppermute | solution.py:576
  21.5 1.0 %shard_map.85.rate_ref = f32[96,256]{1,0:T(8,128)S(1)} custom-call(f32[48,128]{1,0:T(8,128)S(1)} %get-tuple-element.28.planes, s32[8]{0:T(128)S(1)} %copy-done.6, s32[64,256]{1,0:T(8,128)S(1)} %bitcast.6, f32[96,48]{1,0:T(8,128)S(1)} %copy-done.5, f32[128,256]{1,0:T(8,128)S(1)} %copy-done.2, f32[11,8,256]{2,1,0:T(8,128)S(1)} %collective-permute-done.got_a.col_a, ...), custom_call_target="tpu_custom_call" | custom-call | flops 1000 | bytes 1000 | tf_op jit(solution)/shard_map/pallas_call | solution.py:616
  22.5 2.3 %shard_map.86 = (f32[2048,128]{1,0:T(8,128)S(1)}, f32[128,256]{1,0:T(8,128)S(1)}, f32[32,1,128]{2,1,0:T(1,128)S(1)}) custom-call(f32[2048,128]{1,0:T(8,128)S(1)} %get-tuple-element.25.fields, f32[96,256]{1,0:T(8,128)S(1)} %shard_map.85.rate_ref, f32[128,128]{1,0:T(8,128)S(1)} %get-tuple-element.31.energy, ...), custom_call_target="tpu_custom_call" | custom-call | flops 1000 | bytes 1000 | tf_op jit(solution)/shard_map/pallas_call | solution.py:627
  24.8 11.8 %all_to_all.10.got = f32[32,1,128]{2,1,0:T(1,128)S(1)} all-to-all(f32[32,1,128]{2,1,0:T(1,128)S(1)} %get-tuple-element.32), channel_id=1, replica_groups=mesh['slab'=8,'col'=4] {'slab','col'}, dimensions={0} | all-to-all | bytes 32768 | tf_op jit(solution)/shard_map/all_to_all | solution.py:634
  36.7 1.7 %shard_map.87 = (f32[2048,128]{1,0:T(8,128)S(1)}, f32[9,8,256]{2,1,0:T(8,128)S(1)}, f32[9,8,256]{2,1,0:T(8,128)S(1)}, f32[9,8,256]{2,1,0:T(8,128)S(1)}, f32[9,8,256]{2,1,0:T(8,128)S(1)}) custom-call(f32[32,1,128]{2,1,0:T(1,128)S(1)} %all_to_all.10.got, f32[2048,128]{1,0:T(8,128)S(1)} %get-tuple-element.33.grown, ...), custom_call_target="tpu_custom_call" | custom-call | flops 1000 | bytes 1000 | tf_op jit(solution)/shard_map/pallas_call | solution.py:636
  38.4 0.1 collective-permute-start.4
  38.5 0.6 %collective-permute-start.5 = (f32[9,8,256]{2,1,0:T(8,128)S(1)}, f32[9,8,256]{2,1,0:T(8,128)S(1)}, u32[]{:S(2)}, u32[]{:S(2)}) collective-permute-start(f32[9,8,256]{2,1,0:T(8,128)S(1)} %get-tuple-element.37), channel_id=1, source_target_pairs={{0,3},{1,2},{2,1},{3,0},{4,7},{5,6},{6,5},{7,4},{8,11},{9,10},{10,... | collective-permute-start | bytes 221192 | tf_op jit(solution)/shard_map/ppermute | solution.py:576
  39.1 0.6 %collective-permute-start.6 = (f32[9,8,256]{2,1,0:T(8,128)S(1)}, f32[9,8,256]{2,1,0:T(8,128)S(1)}, u32[]{:S(2)}, u32[]{:S(2)}) collective-permute-start(f32[9,8,256]{2,1,0:T(8,128)S(1)} %get-tuple-element.38), channel_id=1, source_target_pairs={{0,4},{4,0},{8,12},{12,8},{16,20},{20,16},{24,28},{28,24},{1,5},{5... | collective-permute-start | bytes 221192 | tf_op jit(solution)/shard_map/ppermute | solution.py:576
  39.8 1.4 %collective-permute-start.7 = (f32[9,8,256]{2,1,0:T(8,128)S(1)}, f32[9,8,256]{2,1,0:T(8,128)S(1)}, u32[]{:S(2)}, u32[]{:S(2)}) collective-permute-start(f32[9,8,256]{2,1,0:T(8,128)S(1)} %get-tuple-element.39), channel_id=1, source_target_pairs={{0,28},{4,8},{8,4},{12,16},{16,12},{20,24},{24,20},{28,0},{1,29},{... | collective-permute-start | bytes 221192 | tf_op jit(solution)/shard_map/ppermute | solution.py:576
  41.1 0.0 collective-permute-done.4.col_a
  41.1 1.4 %collective-permute-done.5.col_b = f32[9,8,256]{2,1,0:T(8,128)S(1)} collective-permute-done((f32[9,8,256]{2,1,0:T(8,128)S(1)}, f32[9,8,256]{2,1,0:T(8,128)S(1)}, u32[]{:S(2)}, u32[]{:S(2)}) %collective-permute-start.5) | collective-permute-done | bytes 73760 | tf_op jit(solution)/shard_map/ppermute | solution.py:576
  42.5 0.9 %collective-permute-done.6.slab_a = f32[9,8,256]{2,1,0:T(8,128)S(1)} collective-permute-done((f32[9,8,256]{2,1,0:T(8,128)S(1)}, f32[9,8,256]{2,1,0:T(8,128)S(1)}, u32[]{:S(2)}, u32[]{:S(2)}) %collective-permute-start.6) | collective-permute-done | bytes 73760 | tf_op jit(solution)/shard_map/ppermute | solution.py:576
  43.5 3.3 %collective-permute-done.7.slab_b = f32[9,8,256]{2,1,0:T(8,128)S(1)} collective-permute-done((f32[9,8,256]{2,1,0:T(8,128)S(1)}, f32[9,8,256]{2,1,0:T(8,128)S(1)}, u32[]{:S(2)}, u32[]{:S(2)}) %collective-permute-start.7) | collective-permute-done | bytes 73760 | tf_op jit(solution)/shard_map/ppermute | solution.py:576
  46.8 2.3 %shard_map.88 = (f32[2048,128]{1,0:T(8,128)S(1)}, f32[128,256]{1,0:T(8,128)S(1)}, f32[32,1,128]{2,1,0:T(1,128)S(1)}) custom-call(f32[2048,128]{1,0:T(8,128)S(1)} %get-tuple-element.35.fields, f32[96,256]{1,0:T(8,128)S(1)} %shard_map.85.rate_ref, f32[128,128]{1,0:T(8,128)S(1)} %get-tuple-element.31.energy, f32[9,8,256]{2,1,0:T(8,128)S(1)} %collective-permute-done.4.col_a, ...), custom_call_target="tpu_custom_call" | custom-call | flops 1000 | bytes 1000 | tf_op jit(solution)/shard_map/pallas_call | solution.py:627
  49.1 9.7 %all_to_all.11.got = f32[32,1,128]{2,1,0:T(1,128)S(1)} all-to-all(f32[32,1,128]{2,1,0:T(1,128)S(1)} %get-tuple-element.40), channel_id=1, replica_groups=mesh['slab'=8,'col'=4] {'slab','col'}, dimensions={0} | all-to-all | bytes 32768 | tf_op jit(solution)/shard_map/all_to_all | solution.py:634
  58.7 3.1 %shard_map.89 = f32[1024,256]{1,0:T(8,128)} custom-call(f32[32,1,128]{2,1,0:T(1,128)S(1)} %all_to_all.11.got, f32[2048,128]{1,0:T(8,128)S(1)} %get-tuple-element.41.grown, f32[128,256]{1,0:T(8,128)S(1)} %get-tuple-element.42.grown_halo, f32[96,256]{1,0:T(8,128)S(1)} %shard_map.85.rate_ref, f32[128,128]{1,0:T(8,128)S(1)} %get-tuple-element.31.energy, ...), custom_call_target="tpu_custom_call" | custom-call | flops 1000 | bytes 1000 | tf_op jit(solution)/shard_map/pallas_call | solution.py:646
  (10 shorter events, 0.0 us)
Async XLA Ops:
  0.0 0.7 %copy-start.3 = (s32[8,4,16]{2,1,0:T(4,128)S(1)}, s32[8,4,16]{2,1,0:T(4,128)}, u32[]{:S(2)}) copy-start(s32[8,4,16]{2,1,0:T(4,128)} %ids_smem.1) | copy-start | bytes 6148
  0.7 0.7 %copy-start.7 = (f32[304]{0:T(512)S(1)}, f32[304]{0:T(512)}, u32[]{:S(2)}) copy-start(f32[304]{0:T(512)} %energy_ref.1) | copy-start | bytes 3652
  1.4 1.8 %copy-start.4 = (f32[6,4,128]{2,1,0:T(4,128)S(1)}, f32[6,4,128]{2,1,0:T(4,128)}, u32[]{:S(2)}) copy-start(f32[6,4,128]{2,1,0:T(4,128)} %coarse_ref.3) | copy-start | bytes 36868
  3.2 1.2 %copy-start = (f32[16,8,8,256]{3,2,1,0:T(8,128)S(1)}, f32[16,8,8,256]{3,2,1,0:T(8,128)}, u32[]{:S(2)}) copy-start(f32[16,8,8,256]{3,2,1,0:T(8,128)} %param.8) | copy-start | bytes 3145732
  4.4 0.8 %copy-start.1 = (s32[8,8,256]{2,1,0:T(8,128)S(1)}, s32[8,8,256]{2,1,0:T(8,128)}, u32[]{:S(2)}) copy-start(s32[8,8,256]{2,1,0:T(8,128)} %param.9) | copy-start | bytes 196612
  6.0 3.2 %collective-permute-start = (f32[11,8,256]{2,1,0:T(8,128)S(1)}, f32[11,8,256]{2,1,0:T(8,128)S(1)}, u32[]{:S(2)}, u32[]{:S(2)}) collective-permute-start(f32[11,8,256]{2,1,0:T(8,128)S(1)} %get-tuple-element.26), channel_id=1, source_target_pairs={{0,1},{1,0},{2,3},{3,2},{4,5},{5,4},{6,7},{7,6},{8,9},{9,8},{10,11... | collective-permute-start | bytes 270344 | tf_op jit(solution)/shard_map/ppermute | solution.py:576
  6.5 5.5 %copy-start.6 = (s32[8]{0:T(128)S(1)}, s32[8]{0:T(128)}, u32[]{:S(2)}) copy-start(s32[8]{0:T(128)} %rows_ref.3) | copy-start | bytes 100
  6.5 5.5 %collective-permute-start.1 = (f32[11,8,256]{2,1,0:T(8,128)S(1)}, f32[11,8,256]{2,1,0:T(8,128)S(1)}, u32[]{:S(2)}, u32[]{:S(2)}) collective-permute-start(f32[11,8,256]{2,1,0:T(8,128)S(1)} %get-tuple-element.27), channel_id=1, source_target_pairs={{0,3},{1,2},{2,1},{3,0},{4,7},{5,6},{6,5},{7,4},{8,11},{9,10},{10,... | collective-permute-start | bytes 270344 | tf_op jit(solution)/shard_map/ppermute | solution.py:576
  12.1 9.4 %copy-start.2 = (f32[128,256]{1,0:T(8,128)S(1)}, f32[128,256]{1,0:T(8,128)}, u32[]{:S(2)}) copy-start(f32[128,256]{1,0:T(8,128)} %constant.5.clone.height) | copy-start | bytes 393220
  12.1 9.4 %copy-start.5 = (f32[96,48]{1,0:T(8,128)S(1)}, f32[96,48]{1,0:T(8,128)}, u32[]{:S(2)}) copy-start(f32[96,48]{1,0:T(8,128)} %constant.4.clone.weights) | copy-start | bytes 55300
  12.7 5.8 %collective-permute-start.2 = (f32[11,8,256]{2,1,0:T(8,128)S(1)}, f32[11,8,256]{2,1,0:T(8,128)S(1)}, u32[]{:S(2)}, u32[]{:S(2)}) collective-permute-start(f32[11,8,256]{2,1,0:T(8,128)S(1)} %get-tuple-element.29), channel_id=1, source_target_pairs={{0,4},{4,0},{8,12},{12,8},{16,20},{20,16},{24,28},{28,24},{1,5},{5... | collective-permute-start | bytes 270344 | tf_op jit(solution)/shard_map/ppermute | solution.py:576
  14.2 7.3 %collective-permute-start.3 = (f32[11,8,256]{2,1,0:T(8,128)S(1)}, f32[11,8,256]{2,1,0:T(8,128)S(1)}, u32[]{:S(2)}, u32[]{:S(2)}) collective-permute-start(f32[11,8,256]{2,1,0:T(8,128)S(1)} %get-tuple-element.30), channel_id=1, source_target_pairs={{0,28},{4,8},{8,4},{12,16},{16,12},{20,24},{24,20},{28,0},{1,29},{... | collective-permute-start | bytes 270344 | tf_op jit(solution)/shard_map/ppermute | solution.py:576
  38.4 2.7 %collective-permute-start.4 = (f32[9,8,256]{2,1,0:T(8,128)S(1)}, f32[9,8,256]{2,1,0:T(8,128)S(1)}, u32[]{:S(2)}, u32[]{:S(2)}) collective-permute-start(f32[9,8,256]{2,1,0:T(8,128)S(1)} %get-tuple-element.36), channel_id=1, source_target_pairs={{0,1},{1,0},{2,3},{3,2},{4,5},{5,4},{6,7},{7,6},{8,9},{9,8},{10,11... | collective-permute-start | bytes 221192 | tf_op jit(solution)/shard_map/ppermute | solution.py:576
  38.5 4.1 %collective-permute-start.5 = (f32[9,8,256]{2,1,0:T(8,128)S(1)}, f32[9,8,256]{2,1,0:T(8,128)S(1)}, u32[]{:S(2)}, u32[]{:S(2)}) collective-permute-start(f32[9,8,256]{2,1,0:T(8,128)S(1)} %get-tuple-element.37), channel_id=1, source_target_pairs={{0,3},{1,2},{2,1},{3,0},{4,7},{5,6},{6,5},{7,4},{8,11},{9,10},{10,... | collective-permute-start | bytes 221192 | tf_op jit(solution)/shard_map/ppermute | solution.py:576
  39.1 4.4 %collective-permute-start.6 = (f32[9,8,256]{2,1,0:T(8,128)S(1)}, f32[9,8,256]{2,1,0:T(8,128)S(1)}, u32[]{:S(2)}, u32[]{:S(2)}) collective-permute-start(f32[9,8,256]{2,1,0:T(8,128)S(1)} %get-tuple-element.38), channel_id=1, source_target_pairs={{0,4},{4,0},{8,12},{12,8},{16,20},{20,16},{24,28},{28,24},{1,5},{5... | collective-permute-start | bytes 221192 | tf_op jit(solution)/shard_map/ppermute | solution.py:576
  39.8 7.0 %collective-permute-start.7 = (f32[9,8,256]{2,1,0:T(8,128)S(1)}, f32[9,8,256]{2,1,0:T(8,128)S(1)}, u32[]{:S(2)}, u32[]{:S(2)}) collective-permute-start(f32[9,8,256]{2,1,0:T(8,128)S(1)} %get-tuple-element.39), channel_id=1, source_target_pairs={{0,28},{4,8},{8,4},{12,16},{16,12},{20,24},{24,20},{28,0},{1,29},{... | collective-permute-start | bytes 221192 | tf_op jit(solution)/shard_map/ppermute | solution.py:576

commit v3 on v2

--- a/solution.py
+++ b/solution.py
@@ -20,9 +20,10 @@
 
 VMEM = pl.BlockSpec(memory_space=pltpu.VMEM)
 SMEM = pl.BlockSpec(memory_space=pltpu.SMEM)
-
-
-def call(body, out_shape, in_specs, out_specs, scratch=(), flops=1000, size=1000):
+HBM = pl.BlockSpec(memory_space=pltpu.HBM)
+
+
+def call(body, out_shape, in_specs, out_specs, scratch=(), flops=1 << 20, size=1 << 20):
     return pl.pallas_call(
         body,
         out_shape=out_shape,
@@ -53,16 +54,13 @@
     )
 
 
-def order_body(slabs, cols, slots, ids_ref, ids_smem, energy_ref, slots_ref, energy_out):
+def slot_places(slabs, cols, slots, ids_ref, ids_smem):
     s, c = lax.axis_index("slab"), lax.axis_index("col")
     sub = lax.broadcasted_iota(jnp.int32, (slots, LANES), 0)
     lane = lax.broadcasted_iota(jnp.int32, (slots, LANES), 1)
     own = jnp.zeros((slots, LANES), jnp.int32)
-    own_energy = jnp.zeros((slots, LANES), jnp.float32)
     for q in range(slots):
-        grain = ids_smem[s, c, q]
-        own = jnp.where(sub == q, grain, own)
-        own_energy = jnp.where(sub == q, energy_ref[grain], own_energy)
+        own = jnp.where(sub == q, ids_smem[s, c, q], own)
     one, zero = jnp.float32(1.0), jnp.float32(0.0)
     have = present(slabs, cols)
     matches, ranks = [], []
@@ -75,7 +73,6 @@
         matches.append(jnp.sum(hit, axis=1, keepdims=True))
         ranks.append(jnp.sum(jnp.where(row < own, shared, zero), axis=1, keepdims=True))
     free = one - (matches[0] + matches[1] + matches[2] + matches[3])
-    subf = sub.astype(jnp.float32)
     lanef = lane.astype(jnp.float32)
     free_row = jnp.sum(jnp.where(sub == lane, free, zero), axis=0, keepdims=True)
     free_rank = jnp.sum(jnp.where(lane < sub, free_row, zero), axis=1, keepdims=True)
@@ -89,13 +86,7 @@
         inside = inside & jnp.logical_not(have[k])
         place = jnp.where(inside & (jnp.abs(local + k * SHARE - lanef) < 0.5), one, place)
         skipped = skipped + jnp.where(have[k], 0, 1)
-    slot_row = jnp.sum(place * subf, axis=0, keepdims=True)
-    energy_row = jnp.sum(place * own_energy, axis=0, keepdims=True)
-    lane1 = lax.broadcasted_iota(jnp.int32, (1, LANES), 1)
-    for q in range(slots):
-        slots_ref[q] = jnp.sum(jnp.where(lane1 == q, slot_row, zero)).astype(jnp.int32)
-        value = jnp.sum(jnp.where(lane1 == q, energy_row, zero), axis=1, keepdims=True)
-        energy_out[q * ROWS : (q + 1) * ROWS, :] = jnp.broadcast_to(value, (ROWS, LANES))
+    return place
 
 
 def take(ref, at, rows, stride=1):
@@ -122,7 +113,7 @@
     return even, (jnp.where(even, high, low), jnp.where(even, low, high))
 
 
-def pack_faces(fields, cx, cy, slots, out_refs, axis, columns):
+def pack_faces(fields, cx, cy, slots, out_refs, axis, columns, slot_of=lambda place: place):
     low, high = (LEFT, RIGHT) if columns else (BELOW, ABOVE)
     _, faces = pair_faces(axis, low, high)
     for out, face in zip(out_refs, faces):
@@ -135,7 +126,7 @@
                 first = jnp.where(is_high, cx - 1 - depth, depth) * cy
                 plane = lambda q: take(fields, q * (cx * cy) + first, cy)
             for j in range(SHARE):
-                fill(out, depth * SHARE + j, plane(face * SHARE + j))
+                fill(out, depth * SHARE + j, plane(slot_of(face * SHARE + j)))
             if depth == 0:
                 s0 = s1 = None
                 for q in range(slots):
@@ -145,24 +136,58 @@
                 fill(out, 2 * SHARE, (s0, s1))
 
 
-def open_body(cx, cy, slots, fields_raw, mask_ref, coarse_ref, slots_ref, fields, msg_a, msg_b, mask_halves):
+def open_body(
+    cx, cy, slots, slabs, cols, ids_hbm, fields_hbm, mask_hbm, coarse_hbm,
+    raw, mask, slots_ref, msg_a, msg_b, ids_smem, ids_ref, coarse_ref, mask_ref, sems,
+):
     cells = cx * cy
+    loads = [
+        pltpu.make_async_copy(ids_hbm, ids_smem, sems.at[0]),
+        pltpu.make_async_copy(ids_hbm, ids_ref, sems.at[1]),
+        pltpu.make_async_copy(coarse_hbm, coarse_ref, sems.at[2]),
+    ]
+    for i in range(2):
+        half = pl.ds(i * LANES, LANES)
+        loads.append(
+            pltpu.make_async_copy(mask_hbm.at[:, half], mask_ref.at[pl.ds(i * cells, cells), :], sems.at[3 + i])
+        )
+        rows = slots * cells
+        loads.append(
+            pltpu.make_async_copy(fields_hbm.at[:, half], raw.at[pl.ds(i * rows, rows), :], sems.at[5 + i])
+        )
+    for load in loads:
+        load.start()
+    loads[0].wait()
+    loads[1].wait()
+    place = slot_places(slabs, cols, slots, ids_ref, ids_smem)
+    sub = lax.broadcasted_iota(jnp.int32, (slots, LANES), 0).astype(jnp.float32)
+    slot_row = jnp.sum(place * sub, axis=0, keepdims=True)
+    lane = lax.broadcasted_iota(jnp.int32, (1, LANES), 1)
     for q in range(slots):
-        at = pl.multiple_of(slots_ref[q] * cells, cells)
-        for i in range(2):
-            put(fields, q * cells, i, fields_raw[pl.ds(at, cells), i * LANES : (i + 1) * LANES])
-    for i in range(2):
-        put(mask_halves, 0, i, mask_ref[:, i * LANES : (i + 1) * LANES].astype(jnp.float32))
-    pack_faces(fields, cx, cy, slots, (msg_a, msg_b), "col", True)
+        slots_ref[q] = jnp.sum(jnp.where(lane == q, slot_row, 0.0)).astype(jnp.int32)
+    for load in loads[2:]:
+        load.wait()
+    mask[...] = mask_ref[...].astype(jnp.float32)
+    pack_faces(raw, cx, cy, slots, (msg_a, msg_b), "col", True, lambda place: slots_ref[place])
     _, faces = pair_faces("col", LEFT, RIGHT)
     capacity, coarse_y, _ = coarse_ref.shape
     for out, face in zip((msg_a, msg_b), faces):
         first = jnp.where(face == RIGHT, cy - 1, 0)
-        fill(out, 2 * SHARE + 1, take(mask_halves, first, cx, cy))
+        fill(out, 2 * SHARE + 1, take(mask, first, cx, cy))
         out[2 * SHARE + 2] = jnp.zeros((ROWS, out.shape[2]), jnp.float32)
         row = jnp.where(face == RIGHT, coarse_y - 1, 0)
         for p in range(capacity):
             out[2 * SHARE + 2, p : p + 1, :LANES] = coarse_ref[p, pl.ds(row, 1), :]
+
+
+def arrange_body(cells, slots, raw, slots_ref, ids_ref, energy_ref, fields, energy_out):
+    s, c = lax.axis_index("slab"), lax.axis_index("col")
+    for q in range(slots):
+        slot = slots_ref[q]
+        for i, part in enumerate(take(raw, slot * cells, cells)):
+            put(fields, q * cells, i, part)
+        value = jnp.full((ROWS, LANES), energy_ref[ids_ref[s, c, slot]], jnp.float32)
+        energy_out[q * ROWS : (q + 1) * ROWS, :] = value
 
 
 def slab_body(
@@ -189,7 +214,7 @@
     live = rows_ref[lax.axis_index("slab")]
     for out, face in zip((msg_a, msg_b), faces):
         first = jnp.where(face == ABOVE, cx - 1, 0) * cy
-        out[2 * SHARE + 1] = mask_ref[pl.ds(pl.multiple_of(first, ROWS), cy), :].astype(jnp.float32)
+        fill(out, 2 * SHARE + 1, take(mask_ref, first, cy))
         row = jnp.where(face == ABOVE, live - 2, 0) * ROWS
         out[thermal, :, :LANES] = planes[pl.ds(pl.multiple_of(row, ROWS), ROWS), :]
         out[thermal, :, LANES:] = planes[pl.ds(pl.multiple_of(row + ROWS, ROWS), ROWS), :]
@@ -250,7 +275,9 @@
     profile = jnp.dot(flat, height[...], precision=HIGHEST, preferred_element_type=jnp.float32)
     mobility = jnp.exp(2.0 * (profile - 1.0)) * TIME_STEP
     cells = cx * cy
-    rate_ref[0:cells, :] = mask_ref[...].astype(jnp.float32) * mobility[:cells]
+    for i, part in enumerate(take(mask_ref, 0, cells)):
+        half = slice(i * LANES, (i + 1) * LANES)
+        rate_ref[0:cells, half] = part * mobility[:cells, half]
     have = present(slabs, cols)
     masks = (
         jnp.where(even_s, slab_b[mask], slab_a[mask]),
@@ -500,7 +527,7 @@
     return spread(here), spread(later)
 
 
-def advance(cx, cy, slots, got, grown, grown_halo, rate_ref, energy, halos, now, squares_ref, store):
+def advance(cx, cy, slots, got, grown, grown_halo, rate_ref, energy, halos, now, squares_ref, store, done=None):
     cells = cx * cy
     marks = edges()
     here, later = multipliers(got, slots)
@@ -540,6 +567,8 @@
             for i in range(2):
                 force = force_of(centre[i], near[i], squares[i], e)
                 store(q, x, i, centre[i] - rate[i] * (force + later))
+        if done is not None:
+            done(x)
         return carry
 
     over_planes(cx, visit, 0)
@@ -559,21 +588,43 @@
     pack_faces(fields, cx, cy, slots, (col_a, col_b), "col", True)
 
 
-def last_body(cx, cy, slots, got, grown, grown_halo, rate_ref, energy, slots_ref, out, halos, now, squares_ref):
-    cells = cx * cy
+def last_body(
+    cx, cy, slots, got, grown, grown_halo, rate_ref, energy, slots_ref, out, halos, now, squares_ref, result, sems
+):
+    def plane(x):
+        at = x * cy if isinstance(x, int) else pl.multiple_of(x * cy, ROWS)
+        rows = pl.ds(at, cy)
+        return pltpu.make_async_copy(result.at[:, rows, :], out.at[:, rows, :], sems.at[x])
 
     def store(q, x, i, value):
-        at = pl.multiple_of(slots_ref[q] * cells + x * cy, ROWS)
-        out[pl.ds(at, cy), i * LANES : (i + 1) * LANES] = value
-
-    advance(cx, cy, slots, got, grown, grown_halo, rate_ref, energy, halos, now, squares_ref, store)
-
-
-def exchange(first, second, axis):
-    count = lax.axis_size(axis)
+        at = x * cy if isinstance(x, int) else pl.multiple_of(x * cy, ROWS)
+        result[slots_ref[q], pl.ds(at, cy), i * LANES : (i + 1) * LANES] = value
+
+    def done(x):
+        plane(x).start()
+
+    advance(cx, cy, slots, got, grown, grown_halo, rate_ref, energy, halos, now, squares_ref, store, done)
+    for x in range(cx):
+        plane(x).wait()
+
+
+def exchange_cols(first, second):
+    count = lax.axis_size("col")
     one = [(i, i ^ 1) for i in range(count)]
     two = [(i, (i - 1) % count if i % 2 == 0 else (i + 1) % count) for i in range(count)]
-    return lax.ppermute(first, axis, one), lax.ppermute(second, axis, two)
+    return lax.ppermute(first, "col", one), lax.ppermute(second, "col", two)
+
+
+def exchange_slabs(first, second):
+    count, cols = lax.axis_size("slab"), lax.axis_size("col")
+    one = [(i, i ^ 1) for i in range(count)]
+    two = []
+    for s in range(count):
+        other = s - 1 if s % 2 == 0 else s + 1
+        for c in range(cols):
+            target = other * cols + c if 0 <= other < count else s * cols + (c ^ 1)
+            two.append((s * cols + c, target))
+    return lax.ppermute(second, ("slab", "col"), two), lax.ppermute(first, "slab", one)
 
 
 def per_device(order_params, layer_mask, coarse_temp, coarse_rows, grain_ids, energy):
@@ -590,27 +641,34 @@
     state = f32(2 * slots * cells, cz // 2)
     halo = f32(slots * ROWS, cz)
 
-    slot_order, slot_energy = call(
-        functools.partial(order_body, slabs, cols, slots),
-        (jax.ShapeDtypeStruct((slots,), jnp.int32), f32(slots * ROWS, LANES)),
-        [VMEM, SMEM, SMEM],
-        (SMEM, VMEM),
-    )(grain_ids, grain_ids, energy)
-    fields, col_a, col_b = call(
-        functools.partial(open_body, cx, cy, slots),
-        (state, message, message),
-        [VMEM, VMEM, VMEM, SMEM],
-        (VMEM,) * 3,
-        [pltpu.VMEM((2 * cells, cz // 2), jnp.float32)],
-    )(raw, mask, coarse_temp, slot_order)
-    col_a, col_b = exchange(col_a, col_b, "col")
+    hbm = lambda x: pltpu.with_memory_space_constraint(x, pltpu.HBM)
+    raw, mask, slot_order, col_a, col_b = call(
+        functools.partial(open_body, cx, cy, slots, slabs, cols),
+        (state, f32(2 * cells, LANES), jax.ShapeDtypeStruct((slots,), jnp.int32), message, message),
+        [HBM] * 4,
+        (VMEM, VMEM, SMEM, VMEM, VMEM),
+        [
+            pltpu.SMEM(grain_ids.shape, jnp.int32),
+            pltpu.VMEM(grain_ids.shape, jnp.int32),
+            pltpu.VMEM(coarse_temp.shape, jnp.float32),
+            pltpu.VMEM((2 * cells, LANES), jnp.int32),
+            pltpu.SemaphoreType.DMA((7,)),
+        ],
+    )(hbm(grain_ids), hbm(raw), hbm(mask), hbm(coarse_temp))
+    col_a, col_b = exchange_cols(col_a, col_b)
+    fields, slot_energy = call(
+        functools.partial(arrange_body, cells, slots),
+        (state, f32(slots * ROWS, LANES)),
+        [VMEM, SMEM, SMEM, SMEM],
+        (VMEM, VMEM),
+    )(raw, slot_order, grain_ids, energy)
     slab_a, slab_b, planes = call(
         functools.partial(slab_body, cx, cy, slots, slabs, cols),
         (message, message, f32(capacity * ROWS, LANES)),
         [VMEM, VMEM, VMEM, SMEM, VMEM, VMEM],
         (VMEM,) * 3,
     )(fields, mask, coarse_temp, coarse_rows, col_a, col_b)
-    slab_a, slab_b = exchange(slab_a, slab_b, "slab")
+    slab_b, slab_a = exchange_slabs(slab_a, slab_b)
     weights = jnp.asarray(plane_weights(cx, cy))
     height = jnp.asarray(height_weights(cz, coarse_z))
     rate = call(
@@ -640,15 +698,15 @@
                 (VMEM,) * 5,
                 buffers,
             )(got, grown, grown_halo, rate, slot_energy)
-            slab_a, slab_b = exchange(slab_a, slab_b, "slab")
-            col_a, col_b = exchange(col_a, col_b, "col")
+            slab_b, slab_a = exchange_slabs(slab_a, slab_b)
+            col_a, col_b = exchange_cols(col_a, col_b)
         else:
             fields = call(
                 functools.partial(last_body, cx, cy, slots),
-                f32(slots * cells, cz),
+                f32(slots, cells, cz),
                 [VMEM] * 5 + [SMEM],
-                VMEM,
-                buffers,
+                HBM,
+                buffers + [pltpu.VMEM((slots, cells, cz), jnp.float32), pltpu.SemaphoreType.DMA((cx,))],
             )(got, grown, grown_halo, rate, slot_energy, slot_order)
     return fields.reshape(order_params.shape)
 

time: 62.1 us -> 55 us (0.89)
  starting transfers between devices: 11 us -> 6.08 us
  local copies, waits for them, and re-layouts: 3.47 us -> 0.67 us
  blocking collectives: 21.5 us -> 24.2 us
  waiting for transfers between devices: 12.3 us -> 9.93 us
    ppermute x8, starting transfers between devices: 11 us -> 6.08 us  [the longest x4 3.88 us: exchange_cols(): return (lax.ppermute(first, 'col', one), lax.ppermute(second, 'col', two))]
    unnamed x16 -> x12, local copies, waits for them, and re-layouts: 3.47 us -> 0.67 us
    all_to_all x2, blocking collectives: 21.5 us -> 24.2 us  [per_device(): got = lax.all_to_all(sums, ('slab', 'col'), 0, 0)]
    ppermute x8, waiting for transfers between devices: 12.3 us -> 9.93 us  [the longest x2 5.19 us: exchange_slabs(): lax.ppermute(first, 'slab', one)]
  transfers between devices with their start and end apart: 8 -> 8, of which waited for: 6 -> 4; matrix products, arithmetic and copies ran while one was open for 0% -> 0% of each run, Pallas kernels for 0% -> 2%
where the time goes in v3:
time: 55 us; the launch traced here: 54.8 us
  blocking collectives  24.2 us (44%)
  Pallas kernels  13.8 us (25%)
  waiting for transfers between devices  9.93 us (18%)
  starting transfers between devices  6.08 us (11%)
  local copies, waits for them, and re-layouts  0.67 us (1%)
    all_to_all x2, blocking collectives, per_device(): got = lax.all_to_all(sums, ('slab', 'col'), 0, 0)  24.2 us
    ppermute x2, waiting for transfers between devices, exchange_slabs(): lax.ppermute(first, 'slab', one)  5.19 us
    ppermute x4, waiting for transfers between devices, exchange_cols(): return (lax.ppermute(first, 'col', one), lax.ppermute(second, 'col', two))  4.74 us
    pallas_call x2, Pallas kernels, per_device(): call(functools.partial(sums_body, cx, cy, slots, slabs, cols, devices), (...  4.6 us
    ppermute x4, starting transfers between devices, exchange_cols(): return (lax.ppermute(first, 'col', one), lax.ppermute(second, 'col', two))  3.88 us
    pallas_call x1, Pallas kernels, per_device(): call(functools.partial(last_body, cx, cy, slots), f32(slots, cells, cz),...  2.84 us
    pallas_call x1, Pallas kernels, per_device(): call(functools.partial(open_body, cx, cy, slots, slabs, cols), (state, f3...  2.15 us
    ppermute x2, starting transfers between devices, exchange_slabs(): lax.ppermute(first, 'slab', one)  2.12 us
  transfers between devices with their start and end apart: 8, of which 4 were waited for; matrix products, arithmetic and copies ran while one was open for 0% of the time, Pallas kernels for 2%

profile of v3, /device:TPU:0, one launch (start us, length us, event | category | flops | bytes accessed | tf_op | source)
XLA Modules:
  0.0 54.8 jit_solution(15074562024491390229)
XLA Ops:
  0.0 2.2 %shard_map.82 = (f32[2048,128]{1,0:T(8,128)S(1)}, f32[128,128]{1,0:T(8,128)S(1)}, s32[16]{0:T(128)S(1)}, f32[11,8,256]{2,1,0:T(8,128)S(1)}, f32[11,8,256]{2,1,0:T(8,128)S(1)}) custom-call(s32[8,4,16]{2,1,0:T(4,128)} %ids_ref.1, f32[1024,256]{1,0:T(8,128)} %bitcast.3, s32[64,256]{1,0:T(8,128)} %bitcast.4, f32[6,4,128]{2,1,0:T(4,128)} %coarse_ref.1), custom_call_target="tpu_custom_call" | custom-call | flops 1048576 | bytes 1048576 | tf_op jit(solution)/shard_map/pallas_call | solution.py:645
  2.2 0.5 collective-permute-start
  2.7 2.6 %collective-permute-start.1 = (f32[11,8,256]{2,1,0:T(8,128)S(1)}, f32[11,8,256]{2,1,0:T(8,128)S(1)}, u32[]{:S(2)}, u32[]{:S(2)}) collective-permute-start(f32[11,8,256]{2,1,0:T(8,128)S(1)} %get-tuple-element.31), channel_id=1, source_target_pairs={{0,3},{1,2},{2,1},{3,0},{4,7},{5,6},{6,5},{7,4},{8,11},{9,10},{10,... | collective-permute-start | bytes 270344 | tf_op jit(solution)/shard_map/ppermute | solution.py:615
  5.3 0.0 copy-done.1
  5.3 0.0 copy-done.4
  5.3 0.9 %shard_map.83 = (f32[2048,128]{1,0:T(8,128)S(1)}, f32[128,128]{1,0:T(8,128)S(1)}) custom-call(f32[2048,128]{1,0:T(8,128)S(1)} %get-tuple-element.26.raw, s32[16]{0:T(128)S(1)} %get-tuple-element.27.slots_ref, s32[8,4,16]{2,1,0:T(4,128)S(1)} %copy-done.1, f32[304]{0:T(512)S(1)} %copy-done.4), custom_call_target="tpu_custom_call" | custom-call | flops 1048576 | bytes 1048576 | tf_op jit(solution)/shard_map/pallas_call | solution.py:659
  6.2 0.0 collective-permute-done.got_a.col_a
  6.3 2.0 %collective-permute-done.1.got_b.col_b = f32[11,8,256]{2,1,0:T(8,128)S(1)} collective-permute-done((f32[11,8,256]{2,1,0:T(8,128)S(1)}, f32[11,8,256]{2,1,0:T(8,128)S(1)}, u32[]{:S(2)}, u32[]{:S(2)}) %collective-permute-start.1) | collective-permute-done | bytes 90144 | tf_op jit(solution)/shard_map/ppermute | solution.py:615
  8.2 0.0 copy-done.2
  8.2 0.7 %copy-done.5 = s32[8]{0:T(128)S(1)} copy-done((s32[8]{0:T(128)S(1)}, s32[8]{0:T(128)}, u32[]{:S(2)}) %copy-start.5) | copy-done | bytes 56
  8.9 0.6 %shard_map.84 = (f32[11,8,256]{2,1,0:T(8,128)S(1)}, f32[11,8,256]{2,1,0:T(8,128)S(1)}, f32[48,128]{1,0:T(8,128)S(1)}) custom-call(f32[2048,128]{1,0:T(8,128)S(1)} %get-tuple-element.28.fields, f32[128,128]{1,0:T(8,128)S(1)} %get-tuple-element.29.mask_ref, f32[6,4,128]{2,1,0:T(4,128)S(1)} %copy-done.2, s32[8]{0:T(128)S(1)} %copy-done.5, ...), custom_call_target="tpu_custom_call" | custom-call | flops 1048576 | bytes 1048576 | tf_op jit(solution)/shard_map/pallas_call | solution.py:665
  9.5 1.5 %collective-permute-start.2 = (f32[11,8,256]{2,1,0:T(8,128)S(1)}, f32[11,8,256]{2,1,0:T(8,128)S(1)}, u32[]{:S(2)}, u32[]{:S(2)}) collective-permute-start(f32[11,8,256]{2,1,0:T(8,128)S(1)} %get-tuple-element.33), channel_id=1, source_target_pairs={{0,4},{4,0},{8,12},{12,8},{16,20},{20,16},{24,28},{28,24},{1,5},{5... | collective-permute-start | bytes 270344 | tf_op jit(solution)/shard_map/ppermute | solution.py:627
  11.0 0.1 collective-permute-start.3
  11.1 4.3 %collective-permute-done.2.slab_a = f32[11,8,256]{2,1,0:T(8,128)S(1)} collective-permute-done((f32[11,8,256]{2,1,0:T(8,128)S(1)}, f32[11,8,256]{2,1,0:T(8,128)S(1)}, u32[]{:S(2)}, u32[]{:S(2)}) %collective-permute-start.2) | collective-permute-done | bytes 90144 | tf_op jit(solution)/shard_map/ppermute | solution.py:627
  15.3 0.0 collective-permute-done.3.slab_b
  15.3 0.0 copy-done
  15.3 0.0 copy-done.3
  15.3 1.0 %shard_map.85.rate_ref = f32[96,256]{1,0:T(8,128)S(1)} custom-call(f32[48,128]{1,0:T(8,128)S(1)} %get-tuple-element.32.planes, s32[8]{0:T(128)S(1)} %copy-done.5, f32[128,128]{1,0:T(8,128)S(1)} %get-tuple-element.29.mask_ref, f32[96,48]{1,0:T(8,128)S(1)} %copy-done.3, f32[128,256]{1,0:T(8,128)S(1)} %copy-done, ...), custom_call_target="tpu_custom_call" | custom-call | flops 1048576 | bytes 1048576 | tf_op jit(solution)/shard_map/pallas_call | solution.py:674
  16.4 2.3 %shard_map.86 = (f32[2048,128]{1,0:T(8,128)S(1)}, f32[128,256]{1,0:T(8,128)S(1)}, f32[32,1,128]{2,1,0:T(1,128)S(1)}) custom-call(f32[2048,128]{1,0:T(8,128)S(1)} %get-tuple-element.28.fields, f32[96,256]{1,0:T(8,128)S(1)} %shard_map.85.rate_ref, f32[128,128]{1,0:T(8,128)S(1)} %get-tuple-element.35.energy, ...), custom_call_target="tpu_custom_call" | custom-call | flops 1048576 | bytes 1048576 | tf_op jit(solution)/shard_map/pallas_call | solution.py:685
  18.7 13.0 %all_to_all.10.got = f32[32,1,128]{2,1,0:T(1,128)S(1)} all-to-all(f32[32,1,128]{2,1,0:T(1,128)S(1)} %get-tuple-element.36), channel_id=1, replica_groups=mesh['slab'=8,'col'=4] {'slab','col'}, dimensions={0} | all-to-all | bytes 32768 | tf_op jit(solution)/shard_map/all_to_all | solution.py:692
  31.7 1.6 %shard_map.87 = (f32[2048,128]{1,0:T(8,128)S(1)}, f32[9,8,256]{2,1,0:T(8,128)S(1)}, f32[9,8,256]{2,1,0:T(8,128)S(1)}, f32[9,8,256]{2,1,0:T(8,128)S(1)}, f32[9,8,256]{2,1,0:T(8,128)S(1)}) custom-call(f32[32,1,128]{2,1,0:T(1,128)S(1)} %all_to_all.10.got, f32[2048,128]{1,0:T(8,128)S(1)} %get-tuple-element.37.grown, ...), custom_call_target="tpu_custom_call" | custom-call | flops 1048576 | bytes 1048576 | tf_op jit(solution)/shard_map/pallas_call | solution.py:694
  33.4 0.1 collective-permute-start.4
  33.5 0.6 %collective-permute-start.5 = (f32[9,8,256]{2,1,0:T(8,128)S(1)}, f32[9,8,256]{2,1,0:T(8,128)S(1)}, u32[]{:S(2)}, u32[]{:S(2)}) collective-permute-start(f32[9,8,256]{2,1,0:T(8,128)S(1)} %get-tuple-element.41), channel_id=1, source_target_pairs={{0,3},{1,2},{2,1},{3,0},{4,7},{5,6},{6,5},{7,4},{8,11},{9,10},{10,... | collective-permute-start | bytes 221192 | tf_op jit(solution)/shard_map/ppermute | solution.py:615
  34.1 0.6 %collective-permute-start.6 = (f32[9,8,256]{2,1,0:T(8,128)S(1)}, f32[9,8,256]{2,1,0:T(8,128)S(1)}, u32[]{:S(2)}, u32[]{:S(2)}) collective-permute-start(f32[9,8,256]{2,1,0:T(8,128)S(1)} %get-tuple-element.42), channel_id=1, source_target_pairs={{0,4},{4,0},{8,12},{12,8},{16,20},{20,16},{24,28},{28,24},{1,5},{5... | collective-permute-start | bytes 221192 | tf_op jit(solution)/shard_map/ppermute | solution.py:627
  34.7 0.0 collective-permute-start.7
  34.8 0.0 collective-permute-done.4.col_a
  34.8 2.8 %collective-permute-done.5.col_b = f32[9,8,256]{2,1,0:T(8,128)S(1)} collective-permute-done((f32[9,8,256]{2,1,0:T(8,128)S(1)}, f32[9,8,256]{2,1,0:T(8,128)S(1)}, u32[]{:S(2)}, u32[]{:S(2)}) %collective-permute-start.5) | collective-permute-done | bytes 73760 | tf_op jit(solution)/shard_map/ppermute | solution.py:615
  37.5 0.9 %collective-permute-done.6.slab_a = f32[9,8,256]{2,1,0:T(8,128)S(1)} collective-permute-done((f32[9,8,256]{2,1,0:T(8,128)S(1)}, f32[9,8,256]{2,1,0:T(8,128)S(1)}, u32[]{:S(2)}, u32[]{:S(2)}) %collective-permute-start.6) | collective-permute-done | bytes 73760 | tf_op jit(solution)/shard_map/ppermute | solution.py:627
  38.5 0.0 collective-permute-done.7.slab_b
  38.5 2.3 %shard_map.88 = (f32[2048,128]{1,0:T(8,128)S(1)}, f32[128,256]{1,0:T(8,128)S(1)}, f32[32,1,128]{2,1,0:T(1,128)S(1)}) custom-call(f32[2048,128]{1,0:T(8,128)S(1)} %get-tuple-element.39.fields, f32[96,256]{1,0:T(8,128)S(1)} %shard_map.85.rate_ref, f32[128,128]{1,0:T(8,128)S(1)} %get-tuple-element.35.energy, f32[9,8,256]{2,1,0:T(8,128)S(1)} %collective-permute-done.4.col_a, ...), custom_call_target="tpu_custom_call" | custom-call | flops 1048576 | bytes 1048576 | tf_op jit(solution)/shard_map/pallas_call | solution.py:685
  40.8 11.2 %all_to_all.11.got = f32[32,1,128]{2,1,0:T(1,128)S(1)} all-to-all(f32[32,1,128]{2,1,0:T(1,128)S(1)} %get-tuple-element.44), channel_id=1, replica_groups=mesh['slab'=8,'col'=4] {'slab','col'}, dimensions={0} | all-to-all | bytes 32768 | tf_op jit(solution)/shard_map/all_to_all | solution.py:692
  52.0 2.8 %shard_map.89 = f32[16,64,256]{2,1,0:T(8,128)} custom-call(f32[32,1,128]{2,1,0:T(1,128)S(1)} %all_to_all.11.got, f32[2048,128]{1,0:T(8,128)S(1)} %get-tuple-element.45.grown, f32[128,256]{1,0:T(8,128)S(1)} %get-tuple-element.46.grown_halo, f32[96,256]{1,0:T(8,128)S(1)} %shard_map.85.rate_ref, f32[128,128]{1,0:T(8,128)S(1)} %get-tuple-element.35.energy, ...), custom_call_target="tpu_custom_call" | custom-call | flops 1048576 | bytes 1048576 | tf_op jit(solution)/shard_map/pallas_call | solution.py:704
  (6 shorter events, 0.0 us)
Async XLA Ops:
  0.0 5.3 %copy-start.1 = (s32[8,4,16]{2,1,0:T(4,128)S(1)}, s32[8,4,16]{2,1,0:T(4,128)}, u32[]{:S(2)}) copy-start(s32[8,4,16]{2,1,0:T(4,128)} %ids_ref.1) | copy-start | bytes 6148
  2.2 4.1 %collective-permute-start = (f32[11,8,256]{2,1,0:T(8,128)S(1)}, f32[11,8,256]{2,1,0:T(8,128)S(1)}, u32[]{:S(2)}, u32[]{:S(2)}) collective-permute-start(f32[11,8,256]{2,1,0:T(8,128)S(1)} %get-tuple-element.30), channel_id=1, source_target_pairs={{0,1},{1,0},{2,3},{3,2},{4,5},{5,4},{6,7},{7,6},{8,9},{9,8},{10,11... | collective-permute-start | bytes 270344 | tf_op jit(solution)/shard_map/ppermute | solution.py:615
  2.7 2.7 %copy-start.4 = (f32[304]{0:T(512)S(1)}, f32[304]{0:T(512)}, u32[]{:S(2)}) copy-start(f32[304]{0:T(512)} %energy_ref.1) | copy-start | bytes 3652
  2.7 5.5 %collective-permute-start.1 = (f32[11,8,256]{2,1,0:T(8,128)S(1)}, f32[11,8,256]{2,1,0:T(8,128)S(1)}, u32[]{:S(2)}, u32[]{:S(2)}) collective-permute-start(f32[11,8,256]{2,1,0:T(8,128)S(1)} %get-tuple-element.31), channel_id=1, source_target_pairs={{0,3},{1,2},{2,1},{3,0},{4,7},{5,6},{6,5},{7,4},{8,11},{9,10},{10,... | collective-permute-start | bytes 270344 | tf_op jit(solution)/shard_map/ppermute | solution.py:615
  5.3 2.9 %copy-start.2 = (f32[6,4,128]{2,1,0:T(4,128)S(1)}, f32[6,4,128]{2,1,0:T(4,128)}, u32[]{:S(2)}) copy-start(f32[6,4,128]{2,1,0:T(4,128)} %coarse_ref.1) | copy-start | bytes 36868
  8.2 0.7 %copy-start.5 = (s32[8]{0:T(128)S(1)}, s32[8]{0:T(128)}, u32[]{:S(2)}) copy-start(s32[8]{0:T(128)} %rows_ref.3) | copy-start | bytes 100
  8.9 6.5 %copy-start = (f32[128,256]{1,0:T(8,128)S(1)}, f32[128,256]{1,0:T(8,128)}, u32[]{:S(2)}) copy-start(f32[128,256]{1,0:T(8,128)} %constant.5.clone.height) | copy-start | bytes 393220
  8.9 6.5 %copy-start.3 = (f32[96,48]{1,0:T(8,128)S(1)}, f32[96,48]{1,0:T(8,128)}, u32[]{:S(2)}) copy-start(f32[96,48]{1,0:T(8,128)} %constant.4.clone.weights) | copy-start | bytes 55300
  9.5 5.8 %collective-permute-start.2 = (f32[11,8,256]{2,1,0:T(8,128)S(1)}, f32[11,8,256]{2,1,0:T(8,128)S(1)}, u32[]{:S(2)}, u32[]{:S(2)}) collective-permute-start(f32[11,8,256]{2,1,0:T(8,128)S(1)} %get-tuple-element.33), channel_id=1, source_target_pairs={{0,4},{4,0},{8,12},{12,8},{16,20},{20,16},{24,28},{28,24},{1,5},{5... | collective-permute-start | bytes 270344 | tf_op jit(solution)/shard_map/ppermute | solution.py:627
  11.0 4.3 %collective-permute-start.3 = (f32[11,8,256]{2,1,0:T(8,128)S(1)}, f32[11,8,256]{2,1,0:T(8,128)S(1)}, u32[]{:S(2)}, u32[]{:S(2)}) collective-permute-start(f32[11,8,256]{2,1,0:T(8,128)S(1)} %get-tuple-element.34), channel_id=1, source_target_pairs={{0,1},{1,0},{2,3},{3,2},{4,8},{5,9},{6,10},{7,11},{8,4},{9,5},{10,... | collective-permute-start | bytes 270344 | tf_op jit(solution)/shard_map/ppermute | solution.py:627
  33.4 1.4 %collective-permute-start.4 = (f32[9,8,256]{2,1,0:T(8,128)S(1)}, f32[9,8,256]{2,1,0:T(8,128)S(1)}, u32[]{:S(2)}, u32[]{:S(2)}) collective-permute-start(f32[9,8,256]{2,1,0:T(8,128)S(1)} %get-tuple-element.40), channel_id=1, source_target_pairs={{0,1},{1,0},{2,3},{3,2},{4,5},{5,4},{6,7},{7,6},{8,9},{9,8},{10,11... | collective-permute-start | bytes 221192 | tf_op jit(solution)/shard_map/ppermute | solution.py:615
  33.5 4.1 %collective-permute-start.5 = (f32[9,8,256]{2,1,0:T(8,128)S(1)}, f32[9,8,256]{2,1,0:T(8,128)S(1)}, u32[]{:S(2)}, u32[]{:S(2)}) collective-permute-start(f32[9,8,256]{2,1,0:T(8,128)S(1)} %get-tuple-element.41), channel_id=1, source_target_pairs={{0,3},{1,2},{2,1},{3,0},{4,7},{5,6},{6,5},{7,4},{8,11},{9,10},{10,... | collective-permute-start | bytes 221192 | tf_op jit(solution)/shard_map/ppermute | solution.py:615
  34.1 4.4 %collective-permute-start.6 = (f32[9,8,256]{2,1,0:T(8,128)S(1)}, f32[9,8,256]{2,1,0:T(8,128)S(1)}, u32[]{:S(2)}, u32[]{:S(2)}) collective-permute-start(f32[9,8,256]{2,1,0:T(8,128)S(1)} %get-tuple-element.42), channel_id=1, source_target_pairs={{0,4},{4,0},{8,12},{12,8},{16,20},{20,16},{24,28},{28,24},{1,5},{5... | collective-permute-start | bytes 221192 | tf_op jit(solution)/shard_map/ppermute | solution.py:627
  34.7 3.7 %collective-permute-start.7 = (f32[9,8,256]{2,1,0:T(8,128)S(1)}, f32[9,8,256]{2,1,0:T(8,128)S(1)}, u32[]{:S(2)}, u32[]{:S(2)}) collective-permute-start(f32[9,8,256]{2,1,0:T(8,128)S(1)} %get-tuple-element.43), channel_id=1, source_target_pairs={{0,1},{1,0},{2,3},{3,2},{4,8},{5,9},{6,10},{7,11},{8,4},{9,5},{10,... | collective-permute-start | bytes 221192 | tf_op jit(solution)/shard_map/ppermute | solution.py:627

commit v4 on v3

v4 whole, which is shorter than its diff:
```python
import functools

import jax
import jax.numpy as jnp
import numpy as np
from jax import lax
from jax.experimental import pallas as pl
from jax.experimental.pallas import tpu as pltpu
from jax.sharding import PartitionSpec as P

SHARE = 4
STEPS = 4
TIME_STEP = 0.05
COUPLING = 1.5
BELOW, ABOVE, LEFT, RIGHT = range(4)
FACES = 4
LANES = 128
ROWS = 8
HIGHEST = lax.Precision.HIGHEST

VMEM = pl.BlockSpec(memory_space=pltpu.VMEM)
SMEM = pl.BlockSpec(memory_space=pltpu.SMEM)
HBM = pl.BlockSpec(memory_space=pltpu.HBM)


def call(body, out_shape, in_specs, out_specs, scratch=(), flops=1 << 20, size=1 << 20):
    return pl.pallas_call(
        body,
        out_shape=out_shape,
        in_specs=in_specs,
        out_specs=out_specs,
        scratch_shapes=list(scratch),
        compiler_params=pltpu.CompilerParams(vmem_limit_bytes=20 << 20),
        cost_estimate=pl.CostEstimate(flops=flops, bytes_accessed=size, transcendentals=0),
    )


def f32(*shape):
    return jax.ShapeDtypeStruct(shape, jnp.float32)


def present(slabs, cols):
    s, c = lax.axis_index("slab"), lax.axis_index("col")
    return (s > 0, s < slabs - 1, c > 0, c < cols - 1)


def beside(slabs, cols):
    s, c = lax.axis_index("slab"), lax.axis_index("col")
    return (
        (jnp.maximum(s - 1, 0), c),
        (jnp.minimum(s + 1, slabs - 1), c),
        (s, jnp.maximum(c - 1, 0)),
        (s, jnp.minimum(c + 1, cols - 1)),
    )


def slot_places(slabs, cols, slots, ids_ref, ids_smem):
    s, c = lax.axis_index("slab"), lax.axis_index("col")
    sub = lax.broadcasted_iota(jnp.int32, (slots, LANES), 0)
    lane = lax.broadcasted_iota(jnp.int32, (slots, LANES), 1)
    own = jnp.zeros((slots, LANES), jnp.int32)
    for q in range(slots):
        own = jnp.where(sub == q, ids_smem[s, c, q], own)
    one, zero = jnp.float32(1.0), jnp.float32(0.0)
    have = present(slabs, cols)
    matches, ranks = [], []
    for k, (ns, nc) in enumerate(beside(slabs, cols)):
        row = ids_ref[ns, pl.ds(nc, 1), :]
        row = jnp.concatenate([row, jnp.full((1, LANES - slots), -1, jnp.int32)], axis=1)
        row = jnp.broadcast_to(jnp.where(have[k], row, -1), (slots, LANES))
        hit = jnp.where((own == row) & (row >= 0), one, zero)
        shared = jnp.max(hit, axis=0, keepdims=True)
        matches.append(jnp.sum(hit, axis=1, keepdims=True))
        ranks.append(jnp.sum(jnp.where(row < own, shared, zero), axis=1, keepdims=True))
    free = one - (matches[0] + matches[1] + matches[2] + matches[3])
    lanef = lane.astype(jnp.float32)
    free_row = jnp.sum(jnp.where(sub == lane, free, zero), axis=0, keepdims=True)
    free_rank = jnp.sum(jnp.where(lane < sub, free_row, zero), axis=1, keepdims=True)
    place = jnp.zeros((slots, LANES), jnp.float32)
    skipped = jnp.int32(0)
    for k in range(FACES):
        at = matches[k] * (ranks[k] + k * SHARE - lanef)
        place = jnp.where((matches[k] > 0.5) & (jnp.abs(at) < 0.5), one, place)
        local = free_rank - (skipped * SHARE).astype(jnp.float32)
        inside = (local > -0.5) & (local < SHARE - 0.5) & (free > 0.5)
        inside = inside & jnp.logical_not(have[k])
        place = jnp.where(inside & (jnp.abs(local + k * SHARE - lanef) < 0.5), one, place)
        skipped = skipped + jnp.where(have[k], 0, 1)
    return place


def take(ref, at, rows, stride=1):
    half = ref.shape[0] // 2
    if stride == 1:
        if not isinstance(at, int):
            at = pl.multiple_of(at, ROWS)
        return ref[pl.ds(at, rows), :], ref[pl.ds(at + half, rows), :]
    return ref[pl.ds(at, rows, stride=stride), :], ref[pl.ds(at + half, rows, stride=stride), :]


def put(ref, at, i, value):
    if not isinstance(at, int):
        at = pl.multiple_of(at, ROWS)
    ref[pl.ds(at + i * (ref.shape[0] // 2), value.shape[0]), :] = value


def spread(ref, row):
    half = ref.shape[0] // 2
    return tuple(jnp.broadcast_to(ref[pl.ds(row + i * half, 1), :], (ROWS, LANES)) for i in range(2))


class Kept:
    def __init__(self, ref, base, cx, cy, slots):
        self.ref, self.cy, self.cells = ref, cy, cx * cy
        self.base = base
        self.near_base = base + self.cells + FACES * ROWS
        self.energy_base = self.near_base + FACES * self.cells
        self.slots_base = self.energy_base + slots * ROWS

    @staticmethod
    def rows(cells, slots):
        return cells + FACES * ROWS + FACES * cells + slots * ROWS + ROWS

    def rate(self, x):
        return take(self.ref, self.base + x * self.cy, self.cy)

    def rate_beside(self, k):
        return take(self.ref, self.base + self.cells + k * ROWS, ROWS)

    def near(self, k, x):
        return take(self.ref, self.near_base + k * self.cells + x * self.cy, self.cy)

    def energy(self, q):
        return self.ref[self.energy_base + q * ROWS : self.energy_base + (q + 1) * ROWS, :]


def keep_on(out, out_base, kept, count):
    for i in range(2):
        put(out, out_base, i, take(kept.ref, kept.base, count)[i])


def fill(out, index, pair):
    out[index, :, :LANES], out[index, :, LANES:] = pair


def pair_faces(axis, low, high):
    even = lax.rem(lax.axis_index(axis), 2) == 0
    return even, (jnp.where(even, high, low), jnp.where(even, low, high))


def pack_faces(fields, cx, cy, slots, out_refs, axis, columns, slot_of=lambda place: place[0] * SHARE + place[1]):
    low, high = (LEFT, RIGHT) if columns else (BELOW, ABOVE)
    _, faces = pair_faces(axis, low, high)
    for out, face in zip(out_refs, faces):
        is_high = face == high
        for depth in range(2):
            if columns:
                first = jnp.where(is_high, cy - 1 - depth, depth)
                plane = lambda q: take(fields, q * (cx * cy) + first, cx, cy)
            else:
                first = jnp.where(is_high, cx - 1 - depth, depth) * cy
                plane = lambda q: take(fields, q * (cx * cy) + first, cy)
            for j in range(SHARE):
                fill(out, depth * SHARE + j, plane(slot_of((face, j))))
            if depth == 0:
                s0 = s1 = None
                for q in range(slots):
                    v0, v1 = plane(q)
                    s0 = v0 * v0 if s0 is None else s0 + v0 * v0
                    s1 = v1 * v1 if s1 is None else s1 + v1 * v1
                fill(out, 2 * SHARE, (s0, s1))


def open_body(
    cx, cy, slots, slabs, cols, ids_hbm, rows_hbm, fields_hbm, mask_hbm, coarse_hbm,
    raw, mask, slots_ref, bounds, planes, msg_a, msg_b, ids_smem, rows_smem, ids_ref, coarse_ref, mask_ref, sems,
):
    cells = cx * cy
    loads = [
        pltpu.make_async_copy(ids_hbm, ids_smem, sems.at[0]),
        pltpu.make_async_copy(ids_hbm, ids_ref, sems.at[1]),
        pltpu.make_async_copy(rows_hbm, rows_smem, sems.at[2]),
        pltpu.make_async_copy(coarse_hbm, coarse_ref, sems.at[3]),
    ]
    for i in range(2):
        half = pl.ds(i * LANES, LANES)
        loads.append(
            pltpu.make_async_copy(mask_hbm.at[:, half], mask_ref.at[pl.ds(i * cells, cells), :], sems.at[4 + i])
        )
        rows = slots * cells
        loads.append(
            pltpu.make_async_copy(fields_hbm.at[:, half], raw.at[pl.ds(i * rows, rows), :], sems.at[6 + i])
        )
    for load in loads:
        load.start()
    for load in loads[:4]:
        load.wait()
    place = slot_places(slabs, cols, slots, ids_ref, ids_smem)
    sub = lax.broadcasted_iota(jnp.int32, (slots, LANES), 0).astype(jnp.float32)
    slot_row = jnp.sum(place * sub, axis=0, keepdims=True)
    slots_ref[...] = jnp.broadcast_to(slot_row, (ROWS, LANES))
    lane = lax.broadcasted_iota(jnp.int32, (1, LANES), 1)
    taken = lambda q: jnp.sum(jnp.where(lane == q, slot_row, 0.0)).astype(jnp.int32)
    left = [taken(LEFT * SHARE + j) for j in range(SHARE)]
    right = [taken(RIGHT * SHARE + j) for j in range(SHARE)]

    s = lax.axis_index("slab")
    start = jnp.int32(0)
    for t in range(slabs):
        start = start + jnp.where(t < s, rows_smem[t], 0)
    live = rows_smem[s]
    bounds[0:ROWS, :] = jnp.full((ROWS, LANES), start, jnp.int32)
    bounds[ROWS : 2 * ROWS, :] = jnp.full((ROWS, LANES), start + live, jnp.int32)
    capacity, coarse_y, _ = coarse_ref.shape
    chosen = [
        jnp.clip(plane - start, 0, capacity - 1) for plane in near_planes(cx, slabs)
    ] + [jnp.int32(0), jnp.int32(1), live - 2, live - 1]
    _, faces = pair_faces("col", LEFT, RIGHT)
    for out in (msg_a, msg_b):
        out[2 * SHARE + 2] = jnp.zeros((ROWS, out.shape[2]), jnp.float32)
    planes[...] = jnp.zeros(planes.shape, jnp.float32)
    for i, p in enumerate(chosen):
        planes[i * ROWS + 1 : i * ROWS + 1 + coarse_y, :] = coarse_ref[p]
        for out, face in zip((msg_a, msg_b), faces):
            row = jnp.where(face == RIGHT, coarse_y - 1, 0)
            spot = slice(i // ROWS * LANES, (i // ROWS + 1) * LANES)
            out[2 * SHARE + 2, i % ROWS : i % ROWS + 1, spot] = coarse_ref[p, pl.ds(row, 1), :]

    for load in loads[4:]:
        load.wait()
    mask[...] = mask_ref[...].astype(jnp.float32)

    def slot_of(place):
        face, j = place
        return jnp.where(face == RIGHT, right[j], left[j])

    pack_faces(raw, cx, cy, slots, (msg_a, msg_b), "col", True, slot_of)
    for out, face in zip((msg_a, msg_b), faces):
        first = jnp.where(face == RIGHT, cy - 1, 0)
        fill(out, 2 * SHARE + 1, take(mask, first, cx, cy))


def near_planes(cx, slabs):
    s = lax.axis_index("slab")
    half = cx // 2
    return [jnp.clip(s * half - 1 + i, 0, slabs * half - 1) for i in range(half + 2)]


def arrange_body(
    cx, cy, slots, raw, mask, slots_ref, ids_ref, energy_ref, fields, energy_out, pre_a, pre_b
):
    cells = cx * cy
    s, c = lax.axis_index("slab"), lax.axis_index("col")
    for q in range(slots):
        slot = slots_ref[0, q].astype(jnp.int32)
        for i, part in enumerate(take(raw, slot * cells, cells)):
            put(fields, q * cells, i, part)
        value = jnp.full((ROWS, LANES), energy_ref[ids_ref[s, c, slot]], jnp.float32)
        energy_out[q * ROWS : (q + 1) * ROWS, :] = value
    pack_faces(fields, cx, cy, slots, (pre_a, pre_b), "slab", False)
    _, faces = pair_faces("slab", BELOW, ABOVE)
    for out, face in zip((pre_a, pre_b), faces):
        first = jnp.where(face == ABOVE, cx - 1, 0) * cy
        fill(out, 2 * SHARE + 1, take(mask, first, cy))


def slab_body(cx, slabs, cols, coarse_y, own, pre_a, pre_b, got_a, got_b, msg_a, msg_b, planes):
    have = present(slabs, cols)
    even, _ = pair_faces("col", LEFT, RIGHT)
    thermal = 2 * SHARE + 2
    from_a, from_b = got_a[thermal], got_b[thermal]
    lower = jnp.where(even, from_b, from_a)
    upper = jnp.where(even, from_a, from_b)
    sub = lax.broadcasted_iota(jnp.int32, (ROWS, LANES), 0)
    last = coarse_y + 1
    widened = []
    for i in range(cx // 2 + 6):
        plane = own[i * ROWS : (i + 1) * ROWS, :]
        spot = slice(i // ROWS * LANES, (i // ROWS + 1) * LANES)
        below = jnp.where(have[LEFT], lower[i % ROWS : i % ROWS + 1, spot], plane[1:2, :])
        above = jnp.where(have[RIGHT], upper[i % ROWS : i % ROWS + 1, spot], plane[coarse_y : coarse_y + 1, :])
        plane = jnp.where(sub == 0, below, jnp.where(sub == last, above, plane))
        widened.append(plane)
        if i < cx // 2 + 2:
            planes[i * ROWS : (i + 1) * ROWS, :] = plane
    first = cx // 2 + 2
    _, faces = pair_faces("slab", BELOW, ABOVE)
    for out, pre, face in zip((msg_a, msg_b), (pre_a, pre_b), faces):
        out[:thermal] = pre[...]
        for i in range(2):
            plane = jnp.where(face == ABOVE, widened[first + 2 + i], widened[first + i])
            out[thermal, :, i * LANES : (i + 1) * LANES] = plane


def axis_weights(cells):
    fine = np.arange(-1, cells + 1)
    lower = (2 * fine - 1) // 4
    weight = (2 * fine - 1 - 4 * lower) / 4.0
    out = np.zeros((cells + 2, cells // 2 + 2), np.float32)
    out[np.arange(cells + 2), lower + 1] += 1.0 - weight
    out[np.arange(cells + 2), lower + 2] += weight
    return out


def plane_weights(cx, cy):
    along, across = axis_weights(cx), axis_weights(cy)
    inner = [(x + 1, y + 1) for x in range(cx) for y in range(cy)]
    inner += [(0, y + 1) for y in range(cy)] + [(cx + 1, y + 1) for y in range(cy)]
    inner += [(x + 1, 0) for x in range(cx)] + [(x + 1, cy + 1) for x in range(cx)]
    out = np.zeros((len(inner), cx // 2 + 2, ROWS), np.float32)
    for row, (x, y) in enumerate(inner):
        out[row, :, : cy // 2 + 2] = along[x][:, None] * across[y][None, :]
    return out.reshape(len(inner), -1)


def height_weights(cells, coarse):
    fine = np.arange(cells)
    lower = (2 * fine - 1) // 4
    weight = (2 * fine - 1 - 4 * lower) / 4.0
    out = np.zeros((coarse, cells), np.float32)
    np.add.at(out, (np.clip(lower, 0, coarse - 1), fine), 1.0 - weight)
    np.add.at(out, (np.clip(lower + 1, 0, coarse - 1), fine), weight)
    return out


def mobility_body(
    cx, cy, slots, slabs, cols, planes, bounds, mask_ref, weights, height, energy, slots_ref,
    col_a, col_b, slab_a, slab_b, keep, near,
):
    start, end = bounds[0:ROWS, :], bounds[ROWS : 2 * ROWS, :]
    even_s, _ = pair_faces("slab", BELOW, ABOVE)
    even_c, _ = pair_faces("col", LEFT, RIGHT)
    thermal, mask = 2 * SHARE + 2, 2 * SHARE + 1
    below = jnp.where(even_s, slab_b[thermal], slab_a[thermal])
    above = jnp.where(even_s, slab_a[thermal], slab_b[thermal])
    for i, p in enumerate(near_planes(cx, slabs)):
        p = jnp.full((ROWS, LANES), p, jnp.int32)
        own = planes[i * ROWS : (i + 1) * ROWS, :]
        lower = jnp.where(p == start - 2, below[:, :LANES], below[:, LANES:])
        upper = jnp.where(p == end, above[:, :LANES], above[:, LANES:])
        near[i * ROWS : (i + 1) * ROWS, :] = jnp.where(p < start, lower, jnp.where(p < end, own, upper))
    flat = jnp.dot(weights[...], near[...], precision=HIGHEST, preferred_element_type=jnp.float32)
    profile = jnp.dot(flat, height[...], precision=HIGHEST, preferred_element_type=jnp.float32)
    mobility = jnp.exp(2.0 * (profile - 1.0)) * TIME_STEP
    cells = cx * cy
    kept = Kept(keep, 0, cx, cy, slots)
    for i, part in enumerate(take(mask_ref, 0, cells)):
        put(keep, 0, i, part * mobility[:cells, i * LANES : (i + 1) * LANES])
    have = present(slabs, cols)
    masks = (
        jnp.where(even_s, slab_b[mask], slab_a[mask]),
        jnp.where(even_s, slab_a[mask], slab_b[mask]),
        jnp.where(even_c, col_b[mask], col_a[mask]),
        jnp.where(even_c, col_a[mask], col_b[mask]),
    )
    for k in range(FACES):
        at = cells + k * ROWS
        for i, part in enumerate(split(jnp.where(have[k], masks[k] * mobility[at : at + ROWS], 0.0))):
            put(keep, at, i, part)
    for i in range(2):
        put(keep, kept.energy_base, i, energy[...])
        put(keep, kept.slots_base, i, slots_ref[...])
    marks = edges()
    top, bottom = marks[2:]
    for x in range(cx):
        sums = neighbours(x, cx - 1, kept.rate, kept.rate(x), None, None, marks)
        extra = [None] * FACES
        if x == 0:
            extra[BELOW] = kept.rate_beside(BELOW)
        if x == cx - 1:
            extra[ABOVE] = kept.rate_beside(ABOVE)
        extra[LEFT] = [jnp.where(top, v, 0.0) for v in spread(keep, cells + LEFT * ROWS + x)]
        extra[RIGHT] = [jnp.where(bottom, v, 0.0) for v in spread(keep, cells + RIGHT * ROWS + x)]
        for k in range(FACES):
            for i in range(2):
                value = sums[i] if extra[k] is None else sums[i] + extra[k][i]
                put(keep, kept.near_base + k * cells + x * cy, i, value)


def split(value):
    return value[:, :LANES], value[:, LANES:]


def along_height(v0, v1, first, last):
    r0, r1 = pltpu.roll(v0, 1, 1), pltpu.roll(v1, 1, 1)
    q0, q1 = pltpu.roll(v0, LANES - 1, 1), pltpu.roll(v1, LANES - 1, 1)
    return (
        jnp.where(first, 0.0, r0) + jnp.where(last, q1, q0),
        jnp.where(first, r0, r1) + jnp.where(last, 0.0, q1),
    )


def along_rows(v, top, bottom, lower, upper):
    down = jnp.where(top, 0.0 if lower is None else lower, pltpu.roll(v, 1, 0))
    up = jnp.where(bottom, 0.0 if upper is None else upper, pltpu.roll(v, ROWS - 1, 0))
    return down + up


def edges():
    lane = lax.broadcasted_iota(jnp.int32, (ROWS, LANES), 1)
    row = lax.broadcasted_iota(jnp.int32, (ROWS, LANES), 0)
    return lane == 0, lane == LANES - 1, row == 0, row == ROWS - 1


def neighbours(x, last_x, load, centre, halo, kind, marks):
    first, last, top, bottom = marks
    v0, v1 = centre
    n0, n1 = along_height(v0, v1, first, last)
    low = high = (None, None)
    if kind == LEFT:
        low = halo(x)
    if kind == RIGHT:
        high = halo(x)
    n0 = n0 + along_rows(v0, top, bottom, low[0], high[0])
    n1 = n1 + along_rows(v1, top, bottom, low[1], high[1])
    sides = []
    if not (isinstance(x, int) and x == 0):
        sides.append(load(x - 1))
    elif kind == BELOW:
        sides.append(halo(None))
    if not (isinstance(x, int) and x == last_x):
        sides.append(load(x + 1))
    elif kind == ABOVE:
        sides.append(halo(None))
    for a, b in sides:
        n0, n1 = n0 + a, n1 + b
    return n0, n1


def over_planes(cx, visit, carry):
    carry = visit(0, carry)
    carry = lax.fori_loop(1, cx - 1, visit, carry)
    return visit(cx - 1, carry)


def slot_access(fields, halos, base, q, cells, cy):
    def load(x):
        return take(fields, q * cells + x * cy, cy)

    def halo(x):
        if x is None:
            return take(halos, base + q * ROWS, ROWS)
        return spread(halos, base + q * ROWS + x)

    return load, halo


def force_of(v, n, squares3, energy):
    return v * (squares3 + ((5.0 - energy) + v * (energy - 2.0 * v))) - n


def triple_squares(fields, x, slots, cells, cy):
    total = None
    for q in range(slots):
        v0, v1 = take(fields, q * cells + x * cy, cy)
        total = (v0 * v0, v1 * v1) if total is None else (total[0] + v0 * v0, total[1] + v1 * v1)
    return 2.0 * COUPLING * total[0], 2.0 * COUPLING * total[1]


def inner_body(cx, cy, slots, base, *refs):
    fields, force_out = refs[0], refs[-1]
    cells = cx * cy
    marks = edges()
    if base is None:
        energy = lambda q: refs[1][q * ROWS : (q + 1) * ROWS, :]
    else:
        energy = Kept(fields, base, cx, cy, slots).energy

    def visit(x, carry):
        squares = triple_squares(fields, x, slots, cells, cy)
        for q in range(slots):
            load, _ = slot_access(fields, None, None, q, cells, cy)
            centre = load(x)
            near = neighbours(x, cx - 1, load, centre, None, None, marks)
            e = energy(q)
            for i in range(2):
                put(force_out, q * cells + x * cy, i, force_of(centre[i], near[i], squares[i], e))
        return carry

    over_planes(cx, visit, 0)


def arrivals(col_a, col_b, slab_a, slab_b):
    even_s, _ = pair_faces("slab", BELOW, ABOVE)
    even_c, _ = pair_faces("col", LEFT, RIGHT)
    pairs = ((slab_b, slab_a, even_s), (slab_a, slab_b, even_s), (col_b, col_a, even_c), (col_a, col_b, even_c))
    return [functools.partial(lambda u, v, even, i: jnp.where(even, u[i], v[i]), *pair) for pair in pairs]


class Grown:
    def __init__(self, cx, cy, slots):
        self.cells = cx * cy
        self.sum = slots * self.cells
        self.squares = self.sum + self.cells
        self.halos = self.squares + self.cells
        self.kept = self.halos + slots * ROWS
        self.count = Kept.rows(self.cells, slots)
        self.rows = self.kept + self.count


def sums_body(
    cx, cy, slots, slabs, cols, devices, base, fields, keep, force_in, col_a, col_b, slab_a, slab_b,
    grown, sums_ref, halos,
):
    cells = cx * cy
    marks = edges()
    first, last, top, bottom = marks
    have = present(slabs, cols)
    kept = Kept(keep, base, cx, cy, slots)
    layout = Grown(cx, cy, slots)
    keep_on(grown, layout.kept, kept, layout.count)
    for k, pick in enumerate(arrivals(col_a, col_b, slab_a, slab_b)):
        s0, s1 = split(2.0 * COUPLING * pick(2 * SHARE))
        h0, h1 = kept.rate_beside(k)
        for j in range(SHARE):
            q = k * SHARE + j
            v0, v1 = split(jnp.where(have[k], pick(j), 0.0))
            put(halos, q * ROWS, 0, v0)
            put(halos, q * ROWS, 1, v1)
            o0, o1 = split(pick(SHARE + j))
            if k == BELOW:
                i0, i1 = take(fields, q * cells, cy)
            elif k == ABOVE:
                i0, i1 = take(fields, (q + 1) * cells - cy, cy)
            elif k == LEFT:
                i0, i1 = take(fields, q * cells, cx, cy)
            else:
                i0, i1 = take(fields, q * cells + cy - 1, cx, cy)
            n0, n1 = along_height(v0, v1, first, last)
            n0 = n0 + along_rows(v0, top, bottom, None, None) + o0 + i0
            n1 = n1 + along_rows(v1, top, bottom, None, None) + o1 + i1
            e = kept.energy(q)
            put(grown, layout.halos + q * ROWS, 0, v0 - h0 * force_of(v0, n0, s0, e))
            put(grown, layout.halos + q * ROWS, 1, v1 - h1 * force_of(v1, n1, s1, e))

    energy_sum = None
    for q in range(slots):
        energy_sum = kept.energy(q) if energy_sum is None else energy_sum + kept.energy(q)
    zero = jnp.zeros((ROWS, LANES), jnp.float32)

    def visit(x, carry):
        total, c0, c1, c2, c3, weight = carry
        rate = kept.rate(x)
        forces, powers = [zero, zero], [zero, zero]
        a2, b1 = [zero, zero], [zero, zero]
        a1 = [[zero, zero] for _ in range(FACES)]
        for q in range(slots):
            k = q // SHARE
            centre = take(fields, q * cells + x * cy, cy)
            inner = take(force_in, q * cells + x * cy, cy)
            e = kept.energy(q)
            cross = (None, None)
            if k in (LEFT, RIGHT):
                row = spread(halos, q * ROWS + x)
                cross = [jnp.where(top if k == LEFT else bottom, row[i], 0.0) for i in range(2)]
            elif isinstance(x, int) and (k, x) in ((BELOW, 0), (ABOVE, cx - 1)):
                cross = take(halos, q * ROWS, ROWS)
            for i in range(2):
                force = inner[i] if cross[i] is None else inner[i] - cross[i]
                g = centre[i] - rate[i] * force
                put(grown, q * cells + x * cy, i, g)
                weighted, square = e * g, g * g
                forces[i] = forces[i] + force
                powers[i] = powers[i] + g * (weighted - (square + square))
                a1[k][i] = a1[k][i] + g
                a2[i] = a2[i] + square
                b1[i] = b1[i] + weighted
        beside = [kept.near(k, x) for k in range(FACES)]
        for i in range(2):
            h = rate[i]
            whole = (a1[0][i] + a1[1][i]) + (a1[2][i] + a1[3][i])
            near = [beside[k][i] for k in range(FACES)]
            put(grown, layout.sum + x * cy, i, whole)
            put(grown, layout.squares + x * cy, i, a2[i])
            total = total + h * forces[i]
            c0 = c0 + h * (powers[i] + 5.0 * whole - b1[i] + 2.0 * COUPLING * whole * a2[i])
            for k in range(FACES):
                c0 = c0 - a1[k][i] * near[k]
            linear = (
                energy_sum
                - 5.0 * slots
                - 2.0 * b1[i]
                + (6.0 - 2.0 * COUPLING * slots) * a2[i]
                - 4.0 * COUPLING * (whole * whole)
            )
            c1 = c1 + h * (h * linear + float(SHARE) * ((near[0] + near[1]) + (near[2] + near[3])))
            c2 = c2 + h * h * h * (energy_sum + (6.0 * COUPLING * slots - 6.0) * whole)
            c3 = c3 + (h * h) * (h * h)
            weight = weight + h
        return total, c0, c1, c2, c3, weight

    parts = over_planes(cx, visit, (zero,) * 6)
    back = -1.0 / TIME_STEP
    scales = (back, back, back, back, back * (2.0 * slots - 2.0 * COUPLING * slots * slots), 1.0 / TIME_STEP)
    lane = lax.broadcasted_iota(jnp.int32, (1, LANES), 1)
    row = jnp.zeros((1, LANES), jnp.float32)
    for i, (part, scale) in enumerate(zip(parts, scales)):
        value = jnp.sum(jnp.sum(part, axis=0, keepdims=True), axis=1, keepdims=True) * scale
        row = jnp.where(lane == i, value, row)
    sums_ref[...] = jnp.broadcast_to(row[None], (devices, 1, LANES))


def near_body(cx, cy, slots, grown, near_out):
    cells = cx * cy
    marks = edges()
    halos = Grown(cx, cy, slots).halos

    def visit(x, carry):
        for q in range(slots):
            load, halo = slot_access(grown, grown, halos, q, cells, cy)
            near = neighbours(x, cx - 1, load, load(x), halo, q // SHARE, marks)
            for i in range(2):
                put(near_out, q * cells + x * cy, i, near[i])
        return carry

    over_planes(cx, visit, 0)


def multipliers(got, slots):
    total = jnp.sum(got[...], axis=0)
    lane = lax.broadcasted_iota(jnp.int32, (1, LANES), 1)
    part = [jnp.sum(jnp.where(lane == i, total, 0.0), axis=1, keepdims=True) for i in range(6)]
    whole = slots * part[5]
    here = part[0] / whole
    later = (part[1] + here * (part[2] + here * (part[3] + here * part[4]))) / whole
    return jnp.broadcast_to(here, (ROWS, LANES)), jnp.broadcast_to(later, (ROWS, LANES))


def settle(cx, cy, slots, got, grown, near_in, store, done=None):
    cells = cx * cy
    here, later = multipliers(got, slots)
    layout = Grown(cx, cy, slots)
    kept = Kept(grown, layout.kept, cx, cy, slots)
    for k in range(FACES):

        def visit(x, carry):
            rate = kept.rate(x)
            near = kept.near(k, x)
            a1 = take(grown, layout.sum + x * cy, cy)
            a2 = take(grown, layout.squares + x * cy, cy)
            off = [here * rate[i] for i in range(2)]
            base = [
                5.0 + 2.0 * COUPLING * (a2[i] - off[i] * (2.0 * a1[i] - float(slots) * off[i])) for i in range(2)
            ]
            extra = [here * near[i] + later for i in range(2)]
            for q in range(k * SHARE, (k + 1) * SHARE):
                e = kept.energy(q)
                g = take(grown, q * cells + x * cy, cy)
                n = take(near_in, q * cells + x * cy, cy)
                for i in range(2):
                    f = g[i] - off[i]
                    force = f * ((base[i] - e) + f * (e - (f + f))) - (n[i] - extra[i])
                    store(q, x, i, f - rate[i] * force)
            return carry

        lax.fori_loop(0, cx, visit, 0)
        if done is not None:
            done(k)


def middle_body(cx, cy, slots, got, grown, near_in, fields, col_a, col_b, slab_a, slab_b):
    def store(q, x, i, value):
        put(fields, q * cx * cy + x * cy, i, value)

    settle(cx, cy, slots, got, grown, near_in, store)
    pack_faces(fields, cx, cy, slots, (slab_a, slab_b), "slab", False)
    pack_faces(fields, cx, cy, slots, (col_a, col_b), "col", True)
    layout = Grown(cx, cy, slots)
    keep_on(fields, slots * cx * cy, Kept(grown, layout.kept, cx, cy, slots), layout.count)


def last_body(cx, cy, slots, got, grown, near_in, out, result, order, sems, order_sem):
    kept = Kept(grown, Grown(cx, cy, slots).kept, cx, cy, slots)
    fetch = pltpu.make_async_copy(grown.at[pl.ds(kept.slots_base, ROWS), :], order, order_sem)
    fetch.start()

    def store(q, x, i, value):
        at = x * cy if isinstance(x, int) else pl.multiple_of(x * cy, ROWS)
        result[q, pl.ds(at, cy), i * LANES : (i + 1) * LANES] = value

    def send(q):
        return pltpu.make_async_copy(result.at[q], out.at[order[0, q].astype(jnp.int32)], sems.at[q])

    def done(k):
        if k == 0:
            fetch.wait()
        for q in range(k * SHARE, (k + 1) * SHARE):
            send(q).start()

    settle(cx, cy, slots, got, grown, near_in, store, done)
    for q in range(slots):
        send(q).wait()


def exchange_cols(first, second):
    count = lax.axis_size("col")
    one = [(i, i ^ 1) for i in range(count)]
    two = [(i, (i - 1) % count if i % 2 == 0 else (i + 1) % count) for i in range(count)]
    return lax.ppermute(first, "col", one), lax.ppermute(second, "col", two)


def exchange_slabs(first, second):
    count, cols = lax.axis_size("slab"), lax.axis_size("col")
    one = [(i, i ^ 1) for i in range(count)]
    two = []
    for s in range(count):
        other = s - 1 if s % 2 == 0 else s + 1
        for c in range(cols):
            target = other * cols + c if 0 <= other < count else s * cols + (c ^ 1)
            two.append((s * cols + c, target))
    return lax.ppermute(second, ("slab", "col"), two), lax.ppermute(first, "slab", one)


def per_device(order_params, layer_mask, coarse_temp, coarse_rows, grain_ids, energy):
    slots, cx, cy, cz = order_params.shape
    slabs, cols = lax.axis_size("slab"), lax.axis_size("col")
    devices = slabs * cols
    cells = cx * cy
    capacity, _, coarse_z = coarse_temp.shape
    raw = order_params.reshape(slots * cells, cz)
    mask = layer_mask.reshape(cells, cz)
    message = f32(2 * SHARE + 3, ROWS, cz)
    short = f32(2 * SHARE + 1, ROWS, cz)
    state = f32(2 * slots * cells, cz // 2)

    hbm = lambda x: pltpu.with_memory_space_constraint(x, pltpu.HBM)
    near = cx // 2 + 2
    raw, mask, slot_order, bounds, planes, col_a, col_b = call(
        functools.partial(open_body, cx, cy, slots, slabs, cols),
        (
            state,
            f32(2 * cells, LANES),
            f32(ROWS, LANES),
            jax.ShapeDtypeStruct((2 * ROWS, LANES), jnp.int32),
            f32((near + 4) * ROWS, LANES),
            message,
            message,
        ),
        [HBM] * 5,
        (VMEM,) * 7,
        [
            pltpu.SMEM(grain_ids.shape, jnp.int32),
            pltpu.SMEM(coarse_rows.shape, jnp.int32),
            pltpu.VMEM(grain_ids.shape, jnp.int32),
            pltpu.VMEM(coarse_temp.shape, jnp.float32),
            pltpu.VMEM((2 * cells, LANES), jnp.int32),
            pltpu.SemaphoreType.DMA((8,)),
        ],
    )(hbm(grain_ids), hbm(coarse_rows), hbm(raw), hbm(mask), hbm(coarse_temp))
    col_a, col_b = exchange_cols(col_a, col_b)
    packed = f32(2 * SHARE + 2, ROWS, cz)
    fields, slot_energy, pre_a, pre_b = call(
        functools.partial(arrange_body, cx, cy, slots),
        (state, f32(slots * ROWS, LANES), packed, packed),
        [VMEM, VMEM, SMEM, SMEM, SMEM],
        (VMEM,) * 4,
    )(raw, mask, slot_order, grain_ids, energy)
    slab_a, slab_b, planes = call(
        functools.partial(slab_body, cx, slabs, cols, coarse_temp.shape[1]),
        (message, message, f32(near * ROWS, LANES)),
        [VMEM] * 5,
        (VMEM,) * 3,
    )(planes, pre_a, pre_b, col_a, col_b)
    slab_b, slab_a = exchange_slabs(slab_a, slab_b)
    weights = jnp.asarray(plane_weights(cx, cy))
    height = jnp.asarray(height_weights(cz, coarse_z))
    count = Kept.rows(cells, slots)
    keep = call(
        functools.partial(mobility_body, cx, cy, slots, slabs, cols),
        f32(2 * count, LANES),
        [VMEM] * 11,
        VMEM,
        [pltpu.VMEM((near * ROWS, LANES), jnp.float32)],
    )(planes, bounds, mask, weights, height, slot_energy, slot_order, col_a, col_b, slab_a, slab_b)

    for pair in range(STEPS // 2):
        base = None if pair == 0 else slots * cells
        inputs = (fields, slot_energy) if pair == 0 else (fields,)
        force = call(
            functools.partial(inner_body, cx, cy, slots, base),
            state,
            [VMEM] * len(inputs),
            VMEM,
            flops=1 << 23,
            size=1 << 22,
        )(*inputs)
        grown, sums = call(
            functools.partial(sums_body, cx, cy, slots, slabs, cols, devices, base or 0),
            (f32(2 * Grown(cx, cy, slots).rows, LANES), f32(devices, 1, LANES)),
            [VMEM] * 7,
            (VMEM,) * 2,
            [pltpu.VMEM((2 * slots * ROWS, LANES), jnp.float32)],
        )(fields, keep if pair == 0 else fields, force, col_a, col_b, slab_a, slab_b)
        got = lax.all_to_all(sums, ("slab", "col"), 0, 0)
        grown_near = call(
            functools.partial(near_body, cx, cy, slots),
            state,
            [VMEM],
            VMEM,
            flops=1 << 23,
            size=1 << 22,
        )(grown)
        if pair < STEPS // 2 - 1:
            fields, col_a, col_b, slab_a, slab_b = call(
                functools.partial(middle_body, cx, cy, slots),
                (f32(2 * (slots * cells + count), LANES), short, short, short, short),
                [VMEM] * 3,
                (VMEM,) * 5,
            )(got, grown, grown_near)
            slab_b, slab_a = exchange_slabs(slab_a, slab_b)
            col_a, col_b = exchange_cols(col_a, col_b)
        else:
            fields = call(
                functools.partial(last_body, cx, cy, slots),
                f32(slots, cells, cz),
                [VMEM] * 3,
                HBM,
                [
                    pltpu.VMEM((slots, cells, cz), jnp.float32),
                    pltpu.SMEM((ROWS, LANES), jnp.float32),
                    pltpu.SemaphoreType.DMA((slots,)),
                    pltpu.SemaphoreType.DMA(()),
                ],
            )(got, grown, grown_near)
    return fields.reshape(order_params.shape)


def solution(mesh):
    in_specs = (
        P(None, "slab", "col", None),
        P("slab", "col", None),
        P("slab", "col", None),
        P(),
        P(),
        P(),
    )
    out_specs = P(None, "slab", "col", None)
    return jax.shard_map(
        per_device, mesh=mesh, in_specs=in_specs, out_specs=out_specs, check_vma=False
    )
```

time: 55 us -> 50 us (0.909)
  blocking collectives: 24.2 us -> 0 us
  starting transfers between devices: 6.08 us -> 16.4 us
  waiting for transfers between devices: 9.93 us -> 18.1 us
  local copies, waits for them, and re-layouts: 0.67 us -> 1.41 us
    all_to_all x2 -> x0, blocking collectives: 24.2 us -> none  [per_device(): got = lax.all_to_all(sums, ('slab', 'col'), 0, 0)]
    all_to_all x0 -> x2, waiting for transfers between devices: none -> 11.9 us  [per_device(): got = lax.all_to_all(sums, ('slab', 'col'), 0, 0)]
    all_to_all x0 -> x2, starting transfers between devices: none -> 10.3 us  [per_device(): got = lax.all_to_all(sums, ('slab', 'col'), 0, 0)]
    ppermute x4, waiting for transfers between devices: 4.74 us -> 2.09 us  [exchange_cols(): return (lax.ppermute(first, 'col', one), lax.ppermute(second, 'col', two))]
    pallas_call x6 -> x10, Pallas kernels: 8.8 us -> 9.99 us  [the longest x2 2.97 us: per_device(): call(functools.partial(sums_body, cx, cy, slots, slabs, cols, devices, ba...]
    ppermute x2, waiting for transfers between devices: 5.19 us -> 4.06 us  [exchange_slabs(): lax.ppermute(first, 'slab', one)]
    pallas_call x1, Pallas kernels: 2.84 us -> 2 us  [per_device(): call(functools.partial(last_body, cx, cy, slots), f32(slots, cells, cz),...]
    unnamed x12 -> x8, local copies, waits for them, and re-layouts: 0.67 us -> 1.41 us
  transfers between devices with their start and end apart: 8 -> 10, of which waited for: 4 -> 6; matrix products, arithmetic and copies ran while one was open for 0% -> 0% of each run, Pallas kernels for 2% -> 11%
where the time goes in v4:
time: 50 us; the launch traced here: 49.6 us
  waiting for transfers between devices  18.1 us (36%)
  starting transfers between devices  16.4 us (33%)
  Pallas kernels  13.6 us (27%)
  local copies, waits for them, and re-layouts  1.41 us (3%)
    all_to_all x2, waiting for transfers between devices, per_device(): got = lax.all_to_all(sums, ('slab', 'col'), 0, 0)  11.9 us
    all_to_all x2, starting transfers between devices, per_device(): got = lax.all_to_all(sums, ('slab', 'col'), 0, 0)  10.3 us
    ppermute x2, waiting for transfers between devices, exchange_slabs(): lax.ppermute(first, 'slab', one)  4.06 us
    ppermute x4, starting transfers between devices, exchange_cols(): return (lax.ppermute(first, 'col', one), lax.ppermute(second, 'col', two))  3.88 us
    pallas_call x2, Pallas kernels, per_device(): call(functools.partial(sums_body, cx, cy, slots, slabs, cols, devices, ba...  2.97 us
    pallas_call x2, Pallas kernels, per_device(): call(functools.partial(inner_body, cx, cy, slots, base), state, [VMEM] *...  2.25 us
    pallas_call x2, Pallas kernels, per_device(): call(functools.partial(near_body, cx, cy, slots), state, [VMEM], VMEM, fl...  2.19 us
    ppermute x2, starting transfers between devices, exchange_slabs(): lax.ppermute(first, 'slab', one)  2.1 us
  transfers between devices with their start and end apart: 10, of which 6 were waited for; matrix products, arithmetic and copies ran while one was open for 0% of the time, Pallas kernels for 11%

profile of v4, /device:TPU:0, one launch (start us, length us, event | category | flops | bytes accessed | tf_op | source)
XLA Modules:
  0.0 49.6 jit_solution(11935138489015003681)
XLA Ops:
  0.0 1.6 %shard_map.82 = (f32[2048,128]{1,0:T(8,128)S(1)}, f32[128,128]{1,0:T(8,128)S(1)}, f32[8,128]{1,0:T(8,128)S(1)}, s32[16,128]{1,0:T(8,128)S(1)}, f32[80,128]{1,0:T...) custom-call(s32[8,4,16]{2,1,0:T(4,128)} %ids_ref.1, s32[8]{0:T(128)} %rows_hbm.1, f32[1024,256]{1,0:T(8,128)} %bitcast.3, ...), custom_call_target="tpu_custom_call" | custom-call | flops 1048576 | bytes 1048576 | tf_op jit(solution)/shard_map/pallas_call | solution.py:728
  1.7 0.5 %collective-permute-start = (f32[11,8,256]{2,1,0:T(8,128)S(1)}, f32[11,8,256]{2,1,0:T(8,128)S(1)}, u32[]{:S(2)}, u32[]{:S(2)}) collective-permute-start(f32[11,8,256]{2,1,0:T(8,128)S(1)} %get-tuple-element.35), channel_id=1, source_target_pairs={{0,1},{1,0},{2,3},{3,2},{4,5},{5,4},{6,7},{7,6},{8,9},{9,8},{10,11... | collective-permute-start | bytes 270344 | tf_op jit(solution)/shard_map/ppermute | solution.py:699
  2.2 2.6 %collective-permute-start.1 = (f32[11,8,256]{2,1,0:T(8,128)S(1)}, f32[11,8,256]{2,1,0:T(8,128)S(1)}, u32[]{:S(2)}, u32[]{:S(2)}) collective-permute-start(f32[11,8,256]{2,1,0:T(8,128)S(1)} %get-tuple-element.36), channel_id=1, source_target_pairs={{0,3},{1,2},{2,1},{3,0},{4,7},{5,6},{6,5},{7,4},{8,11},{9,10},{10,... | collective-permute-start | bytes 270344 | tf_op jit(solution)/shard_map/ppermute | solution.py:699
  4.8 0.7 %copy-done.1 = s32[8,4,16]{2,1,0:T(4,128)S(1)} copy-done((s32[8,4,16]{2,1,0:T(4,128)S(1)}, s32[8,4,16]{2,1,0:T(4,128)}, u32[]{:S(2)}) %copy-start.1) | copy-done | bytes 2072
  5.5 0.7 %copy-done.3 = f32[304]{0:T(512)S(1)} copy-done((f32[304]{0:T(512)S(1)}, f32[304]{0:T(512)}, u32[]{:S(2)}) %copy-start.3) | copy-done | bytes 1240
  6.2 1.0 %shard_map.83 = (f32[2048,128]{1,0:T(8,128)S(1)}, f32[128,128]{1,0:T(8,128)S(1)}, f32[10,8,256]{2,1,0:T(8,128)S(1)}, f32[10,8,256]{2,1,0:T(8,128)S(1)}) custom-call(f32[2048,128]{1,0:T(8,128)S(1)} %get-tuple-element.28.raw, f32[128,128]{1,0:T(8,128)S(1)} %get-tuple-element.29.mask.mask_ref, f32[8,128]{1,0:T(8,128)S(1)} %get-tuple-element.30.slots_ref, ...), custom_call_target="tpu_custom_call" | custom-call | flops 1048576 | bytes 1048576 | tf_op jit(solution)/shard_map/pallas_call | solution.py:752
  7.3 0.0 collective-permute-done.got_a.col_a
  7.3 0.4 collective-permute-done.1.got_b.col_b
  7.7 1.5 %collective-permute-start.2 = (f32[11,8,256]{2,1,0:T(8,128)S(1)}, f32[11,8,256]{2,1,0:T(8,128)S(1)}, u32[]{:S(2)}, u32[]{:S(2)}) collective-permute-start(f32[11,8,256]{2,1,0:T(8,128)S(1)} %get-tuple-element.40), channel_id=1, source_target_pairs={{0,4},{4,0},{8,12},{12,8},{16,20},{20,16},{24,28},{28,24},{1,5},{5... | collective-permute-start | bytes 270344 | tf_op jit(solution)/shard_map/ppermute | solution.py:711
  9.2 0.1 collective-permute-start.3
  9.3 1.1 %shard_map.86.force_in = f32[2048,128]{1,0:T(8,128)S(1)} custom-call(f32[2048,128]{1,0:T(8,128)S(1)} %get-tuple-element.31.refs_0_.fields, f32[128,128]{1,0:T(8,128)S(1)} %get-tuple-element.39.energy.refs_1_), custom_call_target="tpu_custom_call" | custom-call | flops 8388608 | bytes 4194304 | tf_op jit(solution)/shard_map/pallas_call | solution.py:779
  10.4 3.1 %collective-permute-done.2.slab_a = f32[11,8,256]{2,1,0:T(8,128)S(1)} collective-permute-done((f32[11,8,256]{2,1,0:T(8,128)S(1)}, f32[11,8,256]{2,1,0:T(8,128)S(1)}, u32[]{:S(2)}, u32[]{:S(2)}) %collective-permute-start.2) | collective-permute-done | bytes 90144 | tf_op jit(solution)/shard_map/ppermute | solution.py:711
  13.5 0.0 collective-permute-done.3.slab_b
  13.6 0.5 %shard_map.85.keep = f32[976,128]{1,0:T(8,128)S(1)} custom-call(f32[48,128]{1,0:T(8,128)S(1)} %get-tuple-element.37.planes, s32[16,128]{1,0:T(8,128)S(1)} %get-tuple-element.38.bounds, f32[128,128]{1,0:T(8,128)S(1)} %get-tuple-element.29.mask.mask_ref, f32[96,48]{1,0:T(8,128)S(1)} %copy-done.2, f32[128,256]{1,0:T(8,128)S(1)} %copy-done, ...), custom_call_target="tpu_custom_call" | custom-call | flops 1048576 | bytes 1048576 | tf_op jit(solution)/shard_map/pallas_call | solution.py:768
  14.1 1.5 %shard_map.87 = (f32[3536,128]{1,0:T(8,128)S(1)}, f32[32,1,128]{2,1,0:T(1,128)}) custom-call(f32[2048,128]{1,0:T(8,128)S(1)} %get-tuple-element.31.refs_0_.fields, f32[976,128]{1,0:T(8,128)S(1)} %shard_map.85.keep, f32[2048,128]{1,0:T(8,128)S(1)} %shard_map.86.force_in, f32[11,8,256]{2,1,0:T(8,128)S(1)} %collective-permute-done.got_a.col_a, ...), custom_call_target="tpu_custom_call" | custom-call | flops 1048576 | bytes 1048576 | tf_op jit(solution)/shard_map/pallas_call | solution.py:787
  15.6 6.1 %all-to-all-start = ((f32[32,1,128]{2,1,0:T(1,128)}), f32[32,1,128]{2,1,0:T(1,128)S(1)}, u32[]{:S(2)}, u32[]{:S(2)}) async-start(f32[32,1,128]{2,1,0:T(1,128)} %get-tuple-element.42), calls=%async_computation | async-start | bytes 32768 | tf_op jit(solution)/shard_map/all_to_all | solution.py:794
  21.7 1.1 %shard_map.88.near_in = f32[2048,128]{1,0:T(8,128)S(1)} custom-call(f32[3536,128]{1,0:T(8,128)S(1)} %get-tuple-element.43.grown), custom_call_target="tpu_custom_call" | custom-call | flops 8388608 | bytes 4194304 | tf_op jit(solution)/shard_map/pallas_call | solution.py:795
  22.8 6.0 %all-to-all-done.got = f32[32,1,128]{2,1,0:T(1,128)S(1)} async-done(((f32[32,1,128]{2,1,0:T(1,128)}), f32[32,1,128]{2,1,0:T(1,128)S(1)}, u32[]{:S(2)}, u32[]{:S(2)}) %all-to-all-start) | async-done | bytes 16416 | tf_op jit(solution)/shard_map/all_to_all | solution.py:794
  28.8 1.0 %shard_map.89 = (f32[3024,128]{1,0:T(8,128)S(1)}, f32[9,8,256]{2,1,0:T(8,128)S(1)}, f32[9,8,256]{2,1,0:T(8,128)S(1)}, f32[9,8,256]{2,1,0:T(8,128)S(1)}, f32[9,8,256]{2,1,0:T(8,128)S(1)}) custom-call(f32[32,1,128]{2,1,0:T(1,128)S(1)} %all-to-all-done.got, f32[3536,128]{1,0:T(8,128)S(1)} %get-tuple-element.43.grown, f32[2048,128]{1,0:T(8,128)S(1)} %shard_map.88.near_in), custom_call_target="tpu_custom_call" | custom-call | flops 1048576 | bytes 1048576 | tf_op jit(solution)/shard_map/pallas_call | solution.py:804
  29.8 0.1 collective-permute-start.4
  29.8 0.6 %collective-permute-start.5 = (f32[9,8,256]{2,1,0:T(8,128)S(1)}, f32[9,8,256]{2,1,0:T(8,128)S(1)}, u32[]{:S(2)}, u32[]{:S(2)}) collective-permute-start(f32[9,8,256]{2,1,0:T(8,128)S(1)} %get-tuple-element.46), channel_id=1, source_target_pairs={{0,3},{1,2},{2,1},{3,0},{4,7},{5,6},{6,5},{7,4},{8,11},{9,10},{10,... | collective-permute-start | bytes 221192 | tf_op jit(solution)/shard_map/ppermute | solution.py:699
  30.5 0.6 %collective-permute-start.6 = (f32[9,8,256]{2,1,0:T(8,128)S(1)}, f32[9,8,256]{2,1,0:T(8,128)S(1)}, u32[]{:S(2)}, u32[]{:S(2)}) collective-permute-start(f32[9,8,256]{2,1,0:T(8,128)S(1)} %get-tuple-element.47), channel_id=1, source_target_pairs={{0,4},{4,0},{8,12},{12,8},{16,20},{20,16},{24,28},{28,24},{1,5},{5... | collective-permute-start | bytes 221192 | tf_op jit(solution)/shard_map/ppermute | solution.py:711
  31.1 0.0 collective-permute-start.7
  31.1 1.1 %shard_map.90.force_in = f32[2048,128]{1,0:T(8,128)S(1)} custom-call(f32[3024,128]{1,0:T(8,128)S(1)} %get-tuple-element.44.refs_0_.fields.keep), custom_call_target="tpu_custom_call" | custom-call | flops 8388608 | bytes 4194304 | tf_op jit(solution)/shard_map/pallas_call | solution.py:779
  32.3 0.0 collective-permute-done.4.col_a
  32.3 1.6 %collective-permute-done.5.col_b = f32[9,8,256]{2,1,0:T(8,128)S(1)} collective-permute-done((f32[9,8,256]{2,1,0:T(8,128)S(1)}, f32[9,8,256]{2,1,0:T(8,128)S(1)}, u32[]{:S(2)}, u32[]{:S(2)}) %collective-permute-start.5) | collective-permute-done | bytes 73760 | tf_op jit(solution)/shard_map/ppermute | solution.py:699
  33.9 0.9 %collective-permute-done.6.slab_a = f32[9,8,256]{2,1,0:T(8,128)S(1)} collective-permute-done((f32[9,8,256]{2,1,0:T(8,128)S(1)}, f32[9,8,256]{2,1,0:T(8,128)S(1)}, u32[]{:S(2)}, u32[]{:S(2)}) %collective-permute-start.6) | collective-permute-done | bytes 73760 | tf_op jit(solution)/shard_map/ppermute | solution.py:711
  34.8 1.5 %shard_map.91 = (f32[3536,128]{1,0:T(8,128)S(1)}, f32[32,1,128]{2,1,0:T(1,128)}) custom-call(f32[3024,128]{1,0:T(8,128)S(1)} %get-tuple-element.44.refs_0_.fields.keep, f32[3024,128]{1,0:T(8,128)S(1)} %get-tuple-element.44.refs_0_.fields.keep, f32[2048,128]{1,0:T(8,128)S(1)} %shard_map.90.force_in, f32[9,8,256]{2,1,0:T(8,128)S(1)} %collective-permute-done.4.col_a, ...), custom_call_target="tpu_custom_call" | custom-call | flops 1048576 | bytes 1048576 | tf_op jit(solution)/shard_map/pallas_call | solution.py:787
  36.3 4.2 %all-to-all-start.1 = ((f32[32,1,128]{2,1,0:T(1,128)}), f32[32,1,128]{2,1,0:T(1,128)S(1)}, u32[]{:S(2)}, u32[]{:S(2)}) async-start(f32[32,1,128]{2,1,0:T(1,128)} %get-tuple-element.49), calls=%async_computation.1 | async-start | bytes 32768 | tf_op jit(solution)/shard_map/all_to_all | solution.py:794
  40.6 1.1 %shard_map.92.near_in = f32[2048,128]{1,0:T(8,128)S(1)} custom-call(f32[3536,128]{1,0:T(8,128)S(1)} %get-tuple-element.50.grown), custom_call_target="tpu_custom_call" | custom-call | flops 8388608 | bytes 4194304 | tf_op jit(solution)/shard_map/pallas_call | solution.py:795
  41.7 6.0 %all-to-all-done.1.got = f32[32,1,128]{2,1,0:T(1,128)S(1)} async-done(((f32[32,1,128]{2,1,0:T(1,128)}), f32[32,1,128]{2,1,0:T(1,128)S(1)}, u32[]{:S(2)}, u32[]{:S(2)}) %all-to-all-start.1) | async-done | bytes 16416 | tf_op jit(solution)/shard_map/all_to_all | solution.py:794
  47.6 2.0 %shard_map.93 = f32[16,64,256]{2,1,0:T(8,128)} custom-call(f32[32,1,128]{2,1,0:T(1,128)S(1)} %all-to-all-done.1.got, f32[3536,128]{1,0:T(8,128)S(1)} %get-tuple-element.50.grown, f32[2048,128]{1,0:T(8,128)S(1)} %shard_map.92.near_in), custom_call_target="tpu_custom_call" | custom-call | flops 1048576 | bytes 1048576 | tf_op jit(solution)/shard_map/pallas_call | solution.py:813
  (8 shorter events, 0.0 us)
Async XLA Ops:
  1.7 5.6 %collective-permute-start = (f32[11,8,256]{2,1,0:T(8,128)S(1)}, f32[11,8,256]{2,1,0:T(8,128)S(1)}, u32[]{:S(2)}, u32[]{:S(2)}) collective-permute-start(f32[11,8,256]{2,1,0:T(8,128)S(1)} %get-tuple-element.35), channel_id=1, source_target_pairs={{0,1},{1,0},{2,3},{3,2},{4,5},{5,4},{6,7},{7,6},{8,9},{9,8},{10,11... | collective-permute-start | bytes 270344 | tf_op jit(solution)/shard_map/ppermute | solution.py:699
  2.2 5.5 %collective-permute-start.1 = (f32[11,8,256]{2,1,0:T(8,128)S(1)}, f32[11,8,256]{2,1,0:T(8,128)S(1)}, u32[]{:S(2)}, u32[]{:S(2)}) collective-permute-start(f32[11,8,256]{2,1,0:T(8,128)S(1)} %get-tuple-element.36), channel_id=1, source_target_pairs={{0,3},{1,2},{2,1},{3,0},{4,7},{5,6},{6,5},{7,4},{8,11},{9,10},{10,... | collective-permute-start | bytes 270344 | tf_op jit(solution)/shard_map/ppermute | solution.py:699
  4.8 0.7 %copy-start.1 = (s32[8,4,16]{2,1,0:T(4,128)S(1)}, s32[8,4,16]{2,1,0:T(4,128)}, u32[]{:S(2)}) copy-start(s32[8,4,16]{2,1,0:T(4,128)} %ids_ref.1) | copy-start | bytes 6148
  5.5 0.7 %copy-start.3 = (f32[304]{0:T(512)S(1)}, f32[304]{0:T(512)}, u32[]{:S(2)}) copy-start(f32[304]{0:T(512)} %energy_ref.1) | copy-start | bytes 3652
  6.2 7.3 %copy-start = (f32[128,256]{1,0:T(8,128)S(1)}, f32[128,256]{1,0:T(8,128)}, u32[]{:S(2)}) copy-start(f32[128,256]{1,0:T(8,128)} %constant.5.clone.height) | copy-start | bytes 393220
  6.2 7.3 %copy-start.2 = (f32[96,48]{1,0:T(8,128)S(1)}, f32[96,48]{1,0:T(8,128)}, u32[]{:S(2)}) copy-start(f32[96,48]{1,0:T(8,128)} %constant.4.clone.weights) | copy-start | bytes 55300
  7.7 5.8 %collective-permute-start.2 = (f32[11,8,256]{2,1,0:T(8,128)S(1)}, f32[11,8,256]{2,1,0:T(8,128)S(1)}, u32[]{:S(2)}, u32[]{:S(2)}) collective-permute-start(f32[11,8,256]{2,1,0:T(8,128)S(1)} %get-tuple-element.40), channel_id=1, source_target_pairs={{0,4},{4,0},{8,12},{12,8},{16,20},{20,16},{24,28},{28,24},{1,5},{5... | collective-permute-start | bytes 270344 | tf_op jit(solution)/shard_map/ppermute | solution.py:711
  9.2 4.3 %collective-permute-start.3 = (f32[11,8,256]{2,1,0:T(8,128)S(1)}, f32[11,8,256]{2,1,0:T(8,128)S(1)}, u32[]{:S(2)}, u32[]{:S(2)}) collective-permute-start(f32[11,8,256]{2,1,0:T(8,128)S(1)} %get-tuple-element.41), channel_id=1, source_target_pairs={{0,1},{1,0},{2,3},{3,2},{4,8},{5,9},{6,10},{7,11},{8,4},{9,5},{10,... | collective-permute-start | bytes 270344 | tf_op jit(solution)/shard_map/ppermute | solution.py:711
  15.6 13.2 %all-to-all-start = ((f32[32,1,128]{2,1,0:T(1,128)}), f32[32,1,128]{2,1,0:T(1,128)S(1)}, u32[]{:S(2)}, u32[]{:S(2)}) async-start(f32[32,1,128]{2,1,0:T(1,128)} %get-tuple-element.42), calls=%async_computation | async-start | bytes 32768 | tf_op jit(solution)/shard_map/all_to_all | solution.py:794
  29.8 2.5 %collective-permute-start.4 = (f32[9,8,256]{2,1,0:T(8,128)S(1)}, f32[9,8,256]{2,1,0:T(8,128)S(1)}, u32[]{:S(2)}, u32[]{:S(2)}) collective-permute-start(f32[9,8,256]{2,1,0:T(8,128)S(1)} %get-tuple-element.45), channel_id=1, source_target_pairs={{0,1},{1,0},{2,3},{3,2},{4,5},{5,4},{6,7},{7,6},{8,9},{9,8},{10,11... | collective-permute-start | bytes 221192 | tf_op jit(solution)/shard_map/ppermute | solution.py:699
  29.8 4.1 %collective-permute-start.5 = (f32[9,8,256]{2,1,0:T(8,128)S(1)}, f32[9,8,256]{2,1,0:T(8,128)S(1)}, u32[]{:S(2)}, u32[]{:S(2)}) collective-permute-start(f32[9,8,256]{2,1,0:T(8,128)S(1)} %get-tuple-element.46), channel_id=1, source_target_pairs={{0,3},{1,2},{2,1},{3,0},{4,7},{5,6},{6,5},{7,4},{8,11},{9,10},{10,... | collective-permute-start | bytes 221192 | tf_op jit(solution)/shard_map/ppermute | solution.py:699
  30.5 4.4 %collective-permute-start.6 = (f32[9,8,256]{2,1,0:T(8,128)S(1)}, f32[9,8,256]{2,1,0:T(8,128)S(1)}, u32[]{:S(2)}, u32[]{:S(2)}) collective-permute-start(f32[9,8,256]{2,1,0:T(8,128)S(1)} %get-tuple-element.47), channel_id=1, source_target_pairs={{0,4},{4,0},{8,12},{12,8},{16,20},{20,16},{24,28},{28,24},{1,5},{5... | collective-permute-start | bytes 221192 | tf_op jit(solution)/shard_map/ppermute | solution.py:711
  31.1 3.7 %collective-permute-start.7 = (f32[9,8,256]{2,1,0:T(8,128)S(1)}, f32[9,8,256]{2,1,0:T(8,128)S(1)}, u32[]{:S(2)}, u32[]{:S(2)}) collective-permute-start(f32[9,8,256]{2,1,0:T(8,128)S(1)} %get-tuple-element.48), channel_id=1, source_target_pairs={{0,1},{1,0},{2,3},{3,2},{4,8},{5,9},{6,10},{7,11},{8,4},{9,5},{10,... | collective-permute-start | bytes 221192 | tf_op jit(solution)/shard_map/ppermute | solution.py:711
  36.3 11.3 %all-to-all-start.1 = ((f32[32,1,128]{2,1,0:T(1,128)}), f32[32,1,128]{2,1,0:T(1,128)S(1)}, u32[]{:S(2)}, u32[]{:S(2)}) async-start(f32[32,1,128]{2,1,0:T(1,128)} %get-tuple-element.49), calls=%async_computation.1 | async-start | bytes 32768 | tf_op jit(solution)/shard_map/all_to_all | solution.py:794

commit v5 on v4

--- a/solution.py
+++ b/solution.py
@@ -658,15 +658,18 @@
             done(k)
 
 
-def middle_body(cx, cy, slots, got, grown, near_in, fields, col_a, col_b, slab_a, slab_b):
+def middle_body(cx, cy, slots, got, grown, near_in, fields, slab_a, slab_b):
     def store(q, x, i, value):
         put(fields, q * cx * cy + x * cy, i, value)
 
     settle(cx, cy, slots, got, grown, near_in, store)
     pack_faces(fields, cx, cy, slots, (slab_a, slab_b), "slab", False)
-    pack_faces(fields, cx, cy, slots, (col_a, col_b), "col", True)
     layout = Grown(cx, cy, slots)
     keep_on(fields, slots * cx * cy, Kept(grown, layout.kept, cx, cy, slots), layout.count)
+
+
+def cols_body(cx, cy, slots, fields, col_a, col_b):
+    pack_faces(fields, cx, cy, slots, (col_a, col_b), "col", True)
 
 
 def last_body(cx, cy, slots, got, grown, near_in, out, result, order, sems, order_sem):
@@ -801,12 +804,15 @@
             size=1 << 22,
         )(grown)
         if pair < STEPS // 2 - 1:
-            fields, col_a, col_b, slab_a, slab_b = call(
+            fields, slab_a, slab_b = call(
                 functools.partial(middle_body, cx, cy, slots),
-                (f32(2 * (slots * cells + count), LANES), short, short, short, short),
+                (f32(2 * (slots * cells + count), LANES), short, short),
                 [VMEM] * 3,
-                (VMEM,) * 5,
+                (VMEM,) * 3,
             )(got, grown, grown_near)
+            col_a, col_b = call(
+                functools.partial(cols_body, cx, cy, slots), (short, short), [VMEM], (VMEM,) * 2
+            )(fields)
             slab_b, slab_a = exchange_slabs(slab_a, slab_b)
             col_a, col_b = exchange_cols(col_a, col_b)
         else:

time: 50 us -> 48.8 us (0.976)
  starting transfers between devices: 16.4 us -> 14.9 us
    all_to_all x2, starting transfers between devices: 10.3 us -> 8.69 us  [per_device(): got = lax.all_to_all(sums, ('slab', 'col'), 0, 0)]
    ppermute x2, waiting for transfers between devices: 4.06 us -> 4.81 us  [exchange_slabs(): lax.ppermute(first, 'slab', one)]
  transfers between devices with their start and end apart: 10 -> 10, of which waited for: 6 -> 6; matrix products, arithmetic and copies ran while one was open for 0% -> 0% of each run, Pallas kernels for 11% -> 12%
where the time goes in v5:
time: 48.8 us; the launch traced here: 48.4 us
  waiting for transfers between devices  18.4 us (38%)
  starting transfers between devices  14.9 us (31%)
  Pallas kernels  13.6 us (28%)
  local copies, waits for them, and re-layouts  1.41 us (3%)
    all_to_all x2, waiting for transfers between devices, per_device(): got = lax.all_to_all(sums, ('slab', 'col'), 0, 0)  11.9 us
    all_to_all x2, starting transfers between devices, per_device(): got = lax.all_to_all(sums, ('slab', 'col'), 0, 0)  8.69 us
    ppermute x2, waiting for transfers between devices, exchange_slabs(): lax.ppermute(first, 'slab', one)  4.81 us
    ppermute x4, starting transfers between devices, exchange_cols(): return (lax.ppermute(first, 'col', one), lax.ppermute(second, 'col', two))  4.02 us
    pallas_call x2, Pallas kernels, per_device(): call(functools.partial(sums_body, cx, cy, slots, slabs, cols, devices, ba...  2.96 us
    pallas_call x2, Pallas kernels, per_device(): call(functools.partial(inner_body, cx, cy, slots, base), state, [VMEM] *...  2.25 us
    pallas_call x2, Pallas kernels, per_device(): call(functools.partial(near_body, cx, cy, slots), state, [VMEM], VMEM, fl...  2.19 us
    ppermute x2, starting transfers between devices, exchange_slabs(): lax.ppermute(first, 'slab', one)  2.1 us
  transfers between devices with their start and end apart: 10, of which 6 were waited for; matrix products, arithmetic and copies ran while one was open for 0% of the time, Pallas kernels for 12%

profile of v5, /device:TPU:0, one launch (start us, length us, event | category | flops | bytes accessed | tf_op | source)
XLA Modules:
  0.0 48.4 jit_solution(12837005793488292465)
XLA Ops:
  0.0 1.6 %shard_map.82 = (f32[2048,128]{1,0:T(8,128)S(1)}, f32[128,128]{1,0:T(8,128)S(1)}, f32[8,128]{1,0:T(8,128)S(1)}, s32[16,128]{1,0:T(8,128)S(1)}, f32[80,128]{1,0:T...) custom-call(s32[8,4,16]{2,1,0:T(4,128)} %ids_ref.1, s32[8]{0:T(128)} %rows_hbm.1, f32[1024,256]{1,0:T(8,128)} %bitcast.3, ...), custom_call_target="tpu_custom_call" | custom-call | flops 1048576 | bytes 1048576 | tf_op jit(solution)/shard_map/pallas_call | solution.py:731
  1.7 0.5 %collective-permute-start = (f32[11,8,256]{2,1,0:T(8,128)S(1)}, f32[11,8,256]{2,1,0:T(8,128)S(1)}, u32[]{:S(2)}, u32[]{:S(2)}) collective-permute-start(f32[11,8,256]{2,1,0:T(8,128)S(1)} %get-tuple-element.35), channel_id=1, source_target_pairs={{0,1},{1,0},{2,3},{3,2},{4,5},{5,4},{6,7},{7,6},{8,9},{9,8},{10,11... | collective-permute-start | bytes 270344 | tf_op jit(solution)/shard_map/ppermute | solution.py:702
  2.2 2.6 %collective-permute-start.1 = (f32[11,8,256]{2,1,0:T(8,128)S(1)}, f32[11,8,256]{2,1,0:T(8,128)S(1)}, u32[]{:S(2)}, u32[]{:S(2)}) collective-permute-start(f32[11,8,256]{2,1,0:T(8,128)S(1)} %get-tuple-element.36), channel_id=1, source_target_pairs={{0,3},{1,2},{2,1},{3,0},{4,7},{5,6},{6,5},{7,4},{8,11},{9,10},{10,... | collective-permute-start | bytes 270344 | tf_op jit(solution)/shard_map/ppermute | solution.py:702
  4.8 0.7 %copy-done.1 = s32[8,4,16]{2,1,0:T(4,128)S(1)} copy-done((s32[8,4,16]{2,1,0:T(4,128)S(1)}, s32[8,4,16]{2,1,0:T(4,128)}, u32[]{:S(2)}) %copy-start.1) | copy-done | bytes 2072
  5.5 0.7 %copy-done.3 = f32[304]{0:T(512)S(1)} copy-done((f32[304]{0:T(512)S(1)}, f32[304]{0:T(512)}, u32[]{:S(2)}) %copy-start.3) | copy-done | bytes 1240
  6.2 1.0 %shard_map.83 = (f32[2048,128]{1,0:T(8,128)S(1)}, f32[128,128]{1,0:T(8,128)S(1)}, f32[10,8,256]{2,1,0:T(8,128)S(1)}, f32[10,8,256]{2,1,0:T(8,128)S(1)}) custom-call(f32[2048,128]{1,0:T(8,128)S(1)} %get-tuple-element.28.raw, f32[128,128]{1,0:T(8,128)S(1)} %get-tuple-element.29.mask.mask_ref, f32[8,128]{1,0:T(8,128)S(1)} %get-tuple-element.30.slots_ref, ...), custom_call_target="tpu_custom_call" | custom-call | flops 1048576 | bytes 1048576 | tf_op jit(solution)/shard_map/pallas_call | solution.py:755
  7.3 0.4 collective-permute-done.1.got_b.col_b
  7.7 1.5 %collective-permute-start.2 = (f32[11,8,256]{2,1,0:T(8,128)S(1)}, f32[11,8,256]{2,1,0:T(8,128)S(1)}, u32[]{:S(2)}, u32[]{:S(2)}) collective-permute-start(f32[11,8,256]{2,1,0:T(8,128)S(1)} %get-tuple-element.40), channel_id=1, source_target_pairs={{0,4},{4,0},{8,12},{12,8},{16,20},{20,16},{24,28},{28,24},{1,5},{5... | collective-permute-start | bytes 270344 | tf_op jit(solution)/shard_map/ppermute | solution.py:714
  9.2 0.1 collective-permute-start.3
  9.3 1.1 %shard_map.86.force_in = f32[2048,128]{1,0:T(8,128)S(1)} custom-call(f32[2048,128]{1,0:T(8,128)S(1)} %get-tuple-element.31.refs_0_.fields, f32[128,128]{1,0:T(8,128)S(1)} %get-tuple-element.39.energy.refs_1_), custom_call_target="tpu_custom_call" | custom-call | flops 8388608 | bytes 4194304 | tf_op jit(solution)/shard_map/pallas_call | solution.py:782
  10.4 3.1 %collective-permute-done.2.slab_a = f32[11,8,256]{2,1,0:T(8,128)S(1)} collective-permute-done((f32[11,8,256]{2,1,0:T(8,128)S(1)}, f32[11,8,256]{2,1,0:T(8,128)S(1)}, u32[]{:S(2)}, u32[]{:S(2)}) %collective-permute-start.2) | collective-permute-done | bytes 90144 | tf_op jit(solution)/shard_map/ppermute | solution.py:714
  13.5 0.0 collective-permute-done.3.slab_b
  13.6 0.5 %shard_map.85.keep = f32[976,128]{1,0:T(8,128)S(1)} custom-call(f32[48,128]{1,0:T(8,128)S(1)} %get-tuple-element.37.planes, s32[16,128]{1,0:T(8,128)S(1)} %get-tuple-element.38.bounds, f32[128,128]{1,0:T(8,128)S(1)} %get-tuple-element.29.mask.mask_ref, f32[96,48]{1,0:T(8,128)S(1)} %copy-done.2, f32[128,256]{1,0:T(8,128)S(1)} %copy-done, ...), custom_call_target="tpu_custom_call" | custom-call | flops 1048576 | bytes 1048576 | tf_op jit(solution)/shard_map/pallas_call | solution.py:771
  14.1 1.5 %shard_map.87 = (f32[3536,128]{1,0:T(8,128)S(1)}, f32[32,1,128]{2,1,0:T(1,128)}) custom-call(f32[2048,128]{1,0:T(8,128)S(1)} %get-tuple-element.31.refs_0_.fields, f32[976,128]{1,0:T(8,128)S(1)} %shard_map.85.keep, f32[2048,128]{1,0:T(8,128)S(1)} %shard_map.86.force_in, f32[11,8,256]{2,1,0:T(8,128)S(1)} %collective-permute-done.got_a.col_a, ...), custom_call_target="tpu_custom_call" | custom-call | flops 1048576 | bytes 1048576 | tf_op jit(solution)/shard_map/pallas_call | solution.py:790
  15.6 6.1 %all-to-all-start = ((f32[32,1,128]{2,1,0:T(1,128)}), f32[32,1,128]{2,1,0:T(1,128)S(1)}, u32[]{:S(2)}, u32[]{:S(2)}) async-start(f32[32,1,128]{2,1,0:T(1,128)} %get-tuple-element.42), calls=%async_computation | async-start | bytes 32768 | tf_op jit(solution)/shard_map/all_to_all | solution.py:797
  21.7 1.1 %shard_map.88.near_in = f32[2048,128]{1,0:T(8,128)S(1)} custom-call(f32[3536,128]{1,0:T(8,128)S(1)} %get-tuple-element.43.grown), custom_call_target="tpu_custom_call" | custom-call | flops 8388608 | bytes 4194304 | tf_op jit(solution)/shard_map/pallas_call | solution.py:798
  22.8 6.0 %all-to-all-done.got = f32[32,1,128]{2,1,0:T(1,128)S(1)} async-done(((f32[32,1,128]{2,1,0:T(1,128)}), f32[32,1,128]{2,1,0:T(1,128)S(1)}, u32[]{:S(2)}, u32[]{:S(2)}) %all-to-all-start) | async-done | bytes 16416 | tf_op jit(solution)/shard_map/all_to_all | solution.py:797
  28.8 0.9 %shard_map.89 = (f32[3024,128]{1,0:T(8,128)S(1)}, f32[9,8,256]{2,1,0:T(8,128)S(1)}, f32[9,8,256]{2,1,0:T(8,128)S(1)}) custom-call(f32[32,1,128]{2,1,0:T(1,128)S(1)} %all-to-all-done.got, f32[3536,128]{1,0:T(8,128)S(1)} %get-tuple-element.43.grown, f32[2048,128]{1,0:T(8,128)S(1)} %shard_map.88.near_in), custom_call_target="tpu_custom_call" | custom-call | flops 1048576 | bytes 1048576 | tf_op jit(solution)/shard_map/pallas_call | solution.py:807
  29.7 0.6 %collective-permute-start.6 = (f32[9,8,256]{2,1,0:T(8,128)S(1)}, f32[9,8,256]{2,1,0:T(8,128)S(1)}, u32[]{:S(2)}, u32[]{:S(2)}) collective-permute-start(f32[9,8,256]{2,1,0:T(8,128)S(1)} %get-tuple-element.47), channel_id=1, source_target_pairs={{0,4},{4,0},{8,12},{12,8},{16,20},{20,16},{24,28},{28,24},{1,5},{5... | collective-permute-start | bytes 221192 | tf_op jit(solution)/shard_map/ppermute | solution.py:714
  30.3 0.0 collective-permute-start.7
  30.3 0.1 shard_map.91
  30.4 0.6 %collective-permute-start.4 = (f32[9,8,256]{2,1,0:T(8,128)S(1)}, f32[9,8,256]{2,1,0:T(8,128)S(1)}, u32[]{:S(2)}, u32[]{:S(2)}) collective-permute-start(f32[9,8,256]{2,1,0:T(8,128)S(1)} %get-tuple-element.45), channel_id=1, source_target_pairs={{0,1},{1,0},{2,3},{3,2},{4,5},{5,4},{6,7},{7,6},{8,9},{9,8},{10,11... | collective-permute-start | bytes 221192 | tf_op jit(solution)/shard_map/ppermute | solution.py:702
  31.0 0.3 collective-permute-start.5
  31.3 1.1 %shard_map.90.force_in = f32[2048,128]{1,0:T(8,128)S(1)} custom-call(f32[3024,128]{1,0:T(8,128)S(1)} %get-tuple-element.44.refs_0_.fields.keep), custom_call_target="tpu_custom_call" | custom-call | flops 8388608 | bytes 4194304 | tf_op jit(solution)/shard_map/pallas_call | solution.py:782
  32.4 1.7 %collective-permute-done.6.slab_a = f32[9,8,256]{2,1,0:T(8,128)S(1)} collective-permute-done((f32[9,8,256]{2,1,0:T(8,128)S(1)}, f32[9,8,256]{2,1,0:T(8,128)S(1)}, u32[]{:S(2)}, u32[]{:S(2)}) %collective-permute-start.6) | collective-permute-done | bytes 73760 | tf_op jit(solution)/shard_map/ppermute | solution.py:714
  34.1 0.0 collective-permute-done.7.slab_b
  34.1 1.2 %collective-permute-done.5.col_b = f32[9,8,256]{2,1,0:T(8,128)S(1)} collective-permute-done((f32[9,8,256]{2,1,0:T(8,128)S(1)}, f32[9,8,256]{2,1,0:T(8,128)S(1)}, u32[]{:S(2)}, u32[]{:S(2)}) %collective-permute-start.5) | collective-permute-done | bytes 73760 | tf_op jit(solution)/shard_map/ppermute | solution.py:702
  35.3 1.5 %shard_map.92 = (f32[3536,128]{1,0:T(8,128)S(1)}, f32[32,1,128]{2,1,0:T(1,128)}) custom-call(f32[3024,128]{1,0:T(8,128)S(1)} %get-tuple-element.44.refs_0_.fields.keep, f32[3024,128]{1,0:T(8,128)S(1)} %get-tuple-element.44.refs_0_.fields.keep, f32[2048,128]{1,0:T(8,128)S(1)} %shard_map.90.force_in, f32[9,8,256]{2,1,0:T(8,128)S(1)} %collective-permute-done.4.col_a, ...), custom_call_target="tpu_custom_call" | custom-call | flops 1048576 | bytes 1048576 | tf_op jit(solution)/shard_map/pallas_call | solution.py:790
  36.7 2.6 %all-to-all-start.1 = ((f32[32,1,128]{2,1,0:T(1,128)}), f32[32,1,128]{2,1,0:T(1,128)S(1)}, u32[]{:S(2)}, u32[]{:S(2)}) async-start(f32[32,1,128]{2,1,0:T(1,128)} %get-tuple-element.49), calls=%async_computation.1 | async-start | bytes 32768 | tf_op jit(solution)/shard_map/all_to_all | solution.py:797
  39.4 1.1 %shard_map.93.near_in = f32[2048,128]{1,0:T(8,128)S(1)} custom-call(f32[3536,128]{1,0:T(8,128)S(1)} %get-tuple-element.50.grown), custom_call_target="tpu_custom_call" | custom-call | flops 8388608 | bytes 4194304 | tf_op jit(solution)/shard_map/pallas_call | solution.py:798
  40.4 6.0 %all-to-all-done.1.got = f32[32,1,128]{2,1,0:T(1,128)S(1)} async-done(((f32[32,1,128]{2,1,0:T(1,128)}), f32[32,1,128]{2,1,0:T(1,128)S(1)}, u32[]{:S(2)}, u32[]{:S(2)}) %all-to-all-start.1) | async-done | bytes 16416 | tf_op jit(solution)/shard_map/all_to_all | solution.py:797
  46.4 2.0 %shard_map.94 = f32[16,64,256]{2,1,0:T(8,128)} custom-call(f32[32,1,128]{2,1,0:T(1,128)S(1)} %all-to-all-done.1.got, f32[3536,128]{1,0:T(8,128)S(1)} %get-tuple-element.50.grown, f32[2048,128]{1,0:T(8,128)S(1)} %shard_map.93.near_in), custom_call_target="tpu_custom_call" | custom-call | flops 1048576 | bytes 1048576 | tf_op jit(solution)/shard_map/pallas_call | solution.py:819
  (9 shorter events, 0.0 us)
Async XLA Ops:
  1.7 5.6 %collective-permute-start = (f32[11,8,256]{2,1,0:T(8,128)S(1)}, f32[11,8,256]{2,1,0:T(8,128)S(1)}, u32[]{:S(2)}, u32[]{:S(2)}) collective-permute-start(f32[11,8,256]{2,1,0:T(8,128)S(1)} %get-tuple-element.35), channel_id=1, source_target_pairs={{0,1},{1,0},{2,3},{3,2},{4,5},{5,4},{6,7},{7,6},{8,9},{9,8},{10,11... | collective-permute-start | bytes 270344 | tf_op jit(solution)/shard_map/ppermute | solution.py:702
  2.2 5.5 %collective-permute-start.1 = (f32[11,8,256]{2,1,0:T(8,128)S(1)}, f32[11,8,256]{2,1,0:T(8,128)S(1)}, u32[]{:S(2)}, u32[]{:S(2)}) collective-permute-start(f32[11,8,256]{2,1,0:T(8,128)S(1)} %get-tuple-element.36), channel_id=1, source_target_pairs={{0,3},{1,2},{2,1},{3,0},{4,7},{5,6},{6,5},{7,4},{8,11},{9,10},{10,... | collective-permute-start | bytes 270344 | tf_op jit(solution)/shard_map/ppermute | solution.py:702
  4.8 0.7 %copy-start.1 = (s32[8,4,16]{2,1,0:T(4,128)S(1)}, s32[8,4,16]{2,1,0:T(4,128)}, u32[]{:S(2)}) copy-start(s32[8,4,16]{2,1,0:T(4,128)} %ids_ref.1) | copy-start | bytes 6148
  5.5 0.7 %copy-start.3 = (f32[304]{0:T(512)S(1)}, f32[304]{0:T(512)}, u32[]{:S(2)}) copy-start(f32[304]{0:T(512)} %energy_ref.1) | copy-start | bytes 3652
  6.2 7.3 %copy-start = (f32[128,256]{1,0:T(8,128)S(1)}, f32[128,256]{1,0:T(8,128)}, u32[]{:S(2)}) copy-start(f32[128,256]{1,0:T(8,128)} %constant.5.clone.height) | copy-start | bytes 393220
  6.2 7.3 %copy-start.2 = (f32[96,48]{1,0:T(8,128)S(1)}, f32[96,48]{1,0:T(8,128)}, u32[]{:S(2)}) copy-start(f32[96,48]{1,0:T(8,128)} %constant.4.clone.weights) | copy-start | bytes 55300
  7.7 5.8 %collective-permute-start.2 = (f32[11,8,256]{2,1,0:T(8,128)S(1)}, f32[11,8,256]{2,1,0:T(8,128)S(1)}, u32[]{:S(2)}, u32[]{:S(2)}) collective-permute-start(f32[11,8,256]{2,1,0:T(8,128)S(1)} %get-tuple-element.40), channel_id=1, source_target_pairs={{0,4},{4,0},{8,12},{12,8},{16,20},{20,16},{24,28},{28,24},{1,5},{5... | collective-permute-start | bytes 270344 | tf_op jit(solution)/shard_map/ppermute | solution.py:714
  9.2 4.3 %collective-permute-start.3 = (f32[11,8,256]{2,1,0:T(8,128)S(1)}, f32[11,8,256]{2,1,0:T(8,128)S(1)}, u32[]{:S(2)}, u32[]{:S(2)}) collective-permute-start(f32[11,8,256]{2,1,0:T(8,128)S(1)} %get-tuple-element.41), channel_id=1, source_target_pairs={{0,1},{1,0},{2,3},{3,2},{4,8},{5,9},{6,10},{7,11},{8,4},{9,5},{10,... | collective-permute-start | bytes 270344 | tf_op jit(solution)/shard_map/ppermute | solution.py:714
  15.6 13.2 %all-to-all-start = ((f32[32,1,128]{2,1,0:T(1,128)}), f32[32,1,128]{2,1,0:T(1,128)S(1)}, u32[]{:S(2)}, u32[]{:S(2)}) async-start(f32[32,1,128]{2,1,0:T(1,128)} %get-tuple-element.42), calls=%async_computation | async-start | bytes 32768 | tf_op jit(solution)/shard_map/all_to_all | solution.py:797
  29.7 4.4 %collective-permute-start.6 = (f32[9,8,256]{2,1,0:T(8,128)S(1)}, f32[9,8,256]{2,1,0:T(8,128)S(1)}, u32[]{:S(2)}, u32[]{:S(2)}) collective-permute-start(f32[9,8,256]{2,1,0:T(8,128)S(1)} %get-tuple-element.47), channel_id=1, source_target_pairs={{0,4},{4,0},{8,12},{12,8},{16,20},{20,16},{24,28},{28,24},{1,5},{5... | collective-permute-start | bytes 221192 | tf_op jit(solution)/shard_map/ppermute | solution.py:714
  30.3 3.8 %collective-permute-start.7 = (f32[9,8,256]{2,1,0:T(8,128)S(1)}, f32[9,8,256]{2,1,0:T(8,128)S(1)}, u32[]{:S(2)}, u32[]{:S(2)}) collective-permute-start(f32[9,8,256]{2,1,0:T(8,128)S(1)} %get-tuple-element.48), channel_id=1, source_target_pairs={{0,1},{1,0},{2,3},{3,2},{4,8},{5,9},{6,10},{7,11},{8,4},{9,5},{10,... | collective-permute-start | bytes 221192 | tf_op jit(solution)/shard_map/ppermute | solution.py:714
  30.4 3.7 %collective-permute-start.4 = (f32[9,8,256]{2,1,0:T(8,128)S(1)}, f32[9,8,256]{2,1,0:T(8,128)S(1)}, u32[]{:S(2)}, u32[]{:S(2)}) collective-permute-start(f32[9,8,256]{2,1,0:T(8,128)S(1)} %get-tuple-element.45), channel_id=1, source_target_pairs={{0,1},{1,0},{2,3},{3,2},{4,5},{5,4},{6,7},{7,6},{8,9},{9,8},{10,11... | collective-permute-start | bytes 221192 | tf_op jit(solution)/shard_map/ppermute | solution.py:702
  31.0 4.3 %collective-permute-start.5 = (f32[9,8,256]{2,1,0:T(8,128)S(1)}, f32[9,8,256]{2,1,0:T(8,128)S(1)}, u32[]{:S(2)}, u32[]{:S(2)}) collective-permute-start(f32[9,8,256]{2,1,0:T(8,128)S(1)} %get-tuple-element.46), channel_id=1, source_target_pairs={{0,3},{1,2},{2,1},{3,0},{4,7},{5,6},{6,5},{7,4},{8,11},{9,10},{10,... | collective-permute-start | bytes 221192 | tf_op jit(solution)/shard_map/ppermute | solution.py:702
  36.7 9.7 %all-to-all-start.1 = ((f32[32,1,128]{2,1,0:T(1,128)}), f32[32,1,128]{2,1,0:T(1,128)S(1)}, u32[]{:S(2)}, u32[]{:S(2)}) async-start(f32[32,1,128]{2,1,0:T(1,128)} %get-tuple-element.49), calls=%async_computation.1 | async-start | bytes 32768 | tf_op jit(solution)/shard_map/all_to_all | solution.py:797

commit v6 on v5

--- a/solution.py
+++ b/solution.py
@@ -96,6 +96,11 @@
             at = pl.multiple_of(at, ROWS)
         return ref[pl.ds(at, rows), :], ref[pl.ds(at + half, rows), :]
     return ref[pl.ds(at, rows, stride=stride), :], ref[pl.ds(at + half, rows, stride=stride), :]
+
+
+def take_shifted(ref, at, rows, by):
+    half = ref.shape[0] // 2
+    return ref[pl.ds(at + by, rows), :], ref[pl.ds(at + by + half, rows), :]
 
 
 def put(ref, at, i, value):
@@ -390,9 +395,10 @@
     )
 
 
-def along_rows(v, top, bottom, lower, upper):
-    down = jnp.where(top, 0.0 if lower is None else lower, pltpu.roll(v, 1, 0))
-    up = jnp.where(bottom, 0.0 if upper is None else upper, pltpu.roll(v, ROWS - 1, 0))
+def along_rows(v, top, bottom, lower, upper, shifted=None):
+    before, after = shifted or (pltpu.roll(v, 1, 0), pltpu.roll(v, ROWS - 1, 0))
+    down = jnp.where(top, 0.0 if lower is None else lower, before)
+    up = jnp.where(bottom, 0.0 if upper is None else upper, after)
     return down + up
 
 
@@ -402,7 +408,7 @@
     return lane == 0, lane == LANES - 1, row == 0, row == ROWS - 1
 
 
-def neighbours(x, last_x, load, centre, halo, kind, marks):
+def neighbours(x, last_x, load, centre, halo, kind, marks, shift=None):
     first, last, top, bottom = marks
     v0, v1 = centre
     n0, n1 = along_height(v0, v1, first, last)
@@ -411,8 +417,12 @@
         low = halo(x)
     if kind == RIGHT:
         high = halo(x)
-    n0 = n0 + along_rows(v0, top, bottom, low[0], high[0])
-    n1 = n1 + along_rows(v1, top, bottom, low[1], high[1])
+    shifted = (None, None)
+    if shift is not None and 0 < x < last_x:
+        before, after = shift(x, -1), shift(x, 1)
+        shifted = tuple(zip(before, after))
+    n0 = n0 + along_rows(v0, top, bottom, low[0], high[0], shifted[0])
+    n1 = n1 + along_rows(v1, top, bottom, low[1], high[1], shifted[1])
     sides = []
     if not (isinstance(x, int) and x == 0):
         sides.append(load(x - 1))
@@ -471,13 +481,15 @@
         for q in range(slots):
             load, _ = slot_access(fields, None, None, q, cells, cy)
             centre = load(x)
-            near = neighbours(x, cx - 1, load, centre, None, None, marks)
+            shift = lambda y, by: take_shifted(fields, q * cells + y * cy, cy, by)
+            near = neighbours(x, cx - 1, load, centre, None, None, marks, shift)
             e = energy(q)
             for i in range(2):
                 put(force_out, q * cells + x * cy, i, force_of(centre[i], near[i], squares[i], e))
         return carry
 
-    over_planes(cx, visit, 0)
+    for x in range(cx):
+        visit(x, 0)
 
 
 def arrivals(col_a, col_b, slab_a, slab_b):
@@ -600,22 +612,6 @@
     sums_ref[...] = jnp.broadcast_to(row[None], (devices, 1, LANES))
 
 
-def near_body(cx, cy, slots, grown, near_out):
-    cells = cx * cy
-    marks = edges()
-    halos = Grown(cx, cy, slots).halos
-
-    def visit(x, carry):
-        for q in range(slots):
-            load, halo = slot_access(grown, grown, halos, q, cells, cy)
-            near = neighbours(x, cx - 1, load, load(x), halo, q // SHARE, marks)
-            for i in range(2):
-                put(near_out, q * cells + x * cy, i, near[i])
-        return carry
-
-    over_planes(cx, visit, 0)
-
-
 def multipliers(got, slots):
     total = jnp.sum(got[...], axis=0)
     lane = lax.broadcasted_iota(jnp.int32, (1, LANES), 1)
@@ -626,8 +622,9 @@
     return jnp.broadcast_to(here, (ROWS, LANES)), jnp.broadcast_to(later, (ROWS, LANES))
 
 
-def settle(cx, cy, slots, got, grown, near_in, store, done=None):
+def settle(cx, cy, slots, got, grown, store, done=None):
     cells = cx * cy
+    marks = edges()
     here, later = multipliers(got, slots)
     layout = Grown(cx, cy, slots)
     kept = Kept(grown, layout.kept, cx, cy, slots)
@@ -645,24 +642,27 @@
             extra = [here * near[i] + later for i in range(2)]
             for q in range(k * SHARE, (k + 1) * SHARE):
                 e = kept.energy(q)
-                g = take(grown, q * cells + x * cy, cy)
-                n = take(near_in, q * cells + x * cy, cy)
+                load, halo = slot_access(grown, grown, layout.halos, q, cells, cy)
+                shift = lambda y, by: take_shifted(grown, q * cells + y * cy, cy, by)
+                g = load(x)
+                n = neighbours(x, cx - 1, load, g, halo, k, marks, shift)
                 for i in range(2):
                     f = g[i] - off[i]
                     force = f * ((base[i] - e) + f * (e - (f + f))) - (n[i] - extra[i])
                     store(q, x, i, f - rate[i] * force)
             return carry
 
-        lax.fori_loop(0, cx, visit, 0)
+        for x in range(cx):
+            visit(x, 0)
         if done is not None:
             done(k)
 
 
-def middle_body(cx, cy, slots, got, grown, near_in, fields, slab_a, slab_b):
+def middle_body(cx, cy, slots, got, grown, fields, slab_a, slab_b):
     def store(q, x, i, value):
         put(fields, q * cx * cy + x * cy, i, value)
 
-    settle(cx, cy, slots, got, grown, near_in, store)
+    settle(cx, cy, slots, got, grown, store)
     pack_faces(fields, cx, cy, slots, (slab_a, slab_b), "slab", False)
     layout = Grown(cx, cy, slots)
     keep_on(fields, slots * cx * cy, Kept(grown, layout.kept, cx, cy, slots), layout.count)
@@ -672,7 +672,7 @@
     pack_faces(fields, cx, cy, slots, (col_a, col_b), "col", True)
 
 
-def last_body(cx, cy, slots, got, grown, near_in, out, result, order, sems, order_sem):
+def last_body(cx, cy, slots, got, grown, out, result, order, sems, order_sem):
     kept = Kept(grown, Grown(cx, cy, slots).kept, cx, cy, slots)
     fetch = pltpu.make_async_copy(grown.at[pl.ds(kept.slots_base, ROWS), :], order, order_sem)
     fetch.start()
@@ -690,7 +690,7 @@
         for q in range(k * SHARE, (k + 1) * SHARE):
             send(q).start()
 
-    settle(cx, cy, slots, got, grown, near_in, store, done)
+    settle(cx, cy, slots, got, grown, store, done)
     for q in range(slots):
         send(q).wait()
 
@@ -795,21 +795,13 @@
             [pltpu.VMEM((2 * slots * ROWS, LANES), jnp.float32)],
         )(fields, keep if pair == 0 else fields, force, col_a, col_b, slab_a, slab_b)
         got = lax.all_to_all(sums, ("slab", "col"), 0, 0)
-        grown_near = call(
-            functools.partial(near_body, cx, cy, slots),
-            state,
-            [VMEM],
-            VMEM,
-            flops=1 << 23,
-            size=1 << 22,
-        )(grown)
         if pair < STEPS // 2 - 1:
             fields, slab_a, slab_b = call(
                 functools.partial(middle_body, cx, cy, slots),
                 (f32(2 * (slots * cells + count), LANES), short, short),
-                [VMEM] * 3,
+                [VMEM] * 2,
                 (VMEM,) * 3,
-            )(got, grown, grown_near)
+            )(got, grown)
             col_a, col_b = call(
                 functools.partial(cols_body, cx, cy, slots), (short, short), [VMEM], (VMEM,) * 2
             )(fields)
@@ -819,7 +811,7 @@
             fields = call(
                 functools.partial(last_body, cx, cy, slots),
                 f32(slots, cells, cz),
-                [VMEM] * 3,
+                [VMEM] * 2,
                 HBM,
                 [
                     pltpu.VMEM((slots, cells, cz), jnp.float32),
@@ -827,7 +819,7 @@
                     pltpu.SemaphoreType.DMA((slots,)),
                     pltpu.SemaphoreType.DMA(()),
                 ],
-            )(got, grown, grown_near)
+            )(got, grown)
     return fields.reshape(order_params.shape)
 
 

time: 48.8 us -> 47.7 us (0.977)
  blocking collectives: 0 us -> 22.6 us
  waiting for transfers between devices: 18.4 us -> 7.33 us
  starting transfers between devices: 14.9 us -> 6.19 us
  Pallas kernels: 13.6 us -> 9.72 us
    all_to_all x0 -> x2, blocking collectives: none -> 22.6 us  [per_device(): got = lax.all_to_all(sums, ('slab', 'col'), 0, 0)]
    all_to_all x2 -> x0, waiting for transfers between devices: 11.9 us -> none  [per_device(): got = lax.all_to_all(sums, ('slab', 'col'), 0, 0)]
    all_to_all x2 -> x0, starting transfers between devices: 8.69 us -> none  [per_device(): got = lax.all_to_all(sums, ('slab', 'col'), 0, 0)]
    pallas_call x2 -> x0, Pallas kernels: 2.19 us -> none  [per_device(): call(functools.partial(near_body, cx, cy, slots), state, [VMEM], VMEM, fl...]
    pallas_call x2, Pallas kernels: 2.96 us -> 1.74 us  [per_device(): call(functools.partial(sums_body, cx, cy, slots, slabs, cols, devices, ba...]
    ppermute x2, waiting for transfers between devices: 4.81 us -> 5.7 us  [exchange_slabs(): lax.ppermute(first, 'slab', one)]
    pallas_call x2, Pallas kernels: 2.25 us -> 1.38 us  [per_device(): call(functools.partial(inner_body, cx, cy, slots, base), state, [VMEM] *...]
  transfers between devices with their start and end apart: 10 -> 8, of which waited for: 6 -> 4; matrix products, arithmetic and copies ran while one was open for 0% -> 0% of each run, Pallas kernels for 12% -> 5%
where the time goes in v6:
time: 47.7 us; the launch traced here: 47.3 us
  blocking collectives  22.6 us (47%)
  Pallas kernels  9.72 us (20%)
  waiting for transfers between devices  7.33 us (15%)
  starting transfers between devices  6.19 us (13%)
  local copies, waits for them, and re-layouts  1.41 us (3%)
    all_to_all x2, blocking collectives, per_device(): got = lax.all_to_all(sums, ('slab', 'col'), 0, 0)  22.6 us
    ppermute x2, waiting for transfers between devices, exchange_slabs(): lax.ppermute(first, 'slab', one)  5.7 us
    ppermute x4, starting transfers between devices, exchange_cols(): return (lax.ppermute(first, 'col', one), lax.ppermute(second, 'col', two))  4.02 us
    pallas_call x1, Pallas kernels, per_device(): call(functools.partial(last_body, cx, cy, slots), f32(slots, cells, cz),...  2.15 us
    ppermute x2, starting transfers between devices, exchange_slabs(): lax.ppermute(first, 'slab', one)  2.08 us
    pallas_call x2, Pallas kernels, per_device(): call(functools.partial(sums_body, cx, cy, slots, slabs, cols, devices, ba...  1.74 us
    pallas_call x1, Pallas kernels, per_device(): call(functools.partial(open_body, cx, cy, slots, slabs, cols), (state, f3...  1.64 us
    ppermute x4, waiting for transfers between devices, exchange_cols(): return (lax.ppermute(first, 'col', one), lax.ppermute(second, 'col', two))  1.63 us
  transfers between devices with their start and end apart: 8, of which 4 were waited for; matrix products, arithmetic and copies ran while one was open for 0% of the time, Pallas kernels for 5%

profile of v6, /device:TPU:0, one launch (start us, length us, event | category | flops | bytes accessed | tf_op | source)
XLA Modules:
  0.0 47.3 jit_solution(7258328902498412724)
XLA Ops:
  0.0 1.6 %shard_map.82 = (f32[2048,128]{1,0:T(8,128)S(1)}, f32[128,128]{1,0:T(8,128)S(1)}, f32[8,128]{1,0:T(8,128)S(1)}, s32[16,128]{1,0:T(8,128)S(1)}, f32[80,128]{1,0:T...) custom-call(s32[8,4,16]{2,1,0:T(4,128)} %ids_ref.1, s32[8]{0:T(128)} %rows_hbm.1, f32[1024,256]{1,0:T(8,128)} %bitcast.3, ...), custom_call_target="tpu_custom_call" | custom-call | flops 1048576 | bytes 1048576 | tf_op jit(solution)/shard_map/pallas_call | solution.py:731
  1.7 0.5 %collective-permute-start = (f32[11,8,256]{2,1,0:T(8,128)S(1)}, f32[11,8,256]{2,1,0:T(8,128)S(1)}, u32[]{:S(2)}, u32[]{:S(2)}) collective-permute-start(f32[11,8,256]{2,1,0:T(8,128)S(1)} %get-tuple-element.35), channel_id=1, source_target_pairs={{0,1},{1,0},{2,3},{3,2},{4,5},{5,4},{6,7},{7,6},{8,9},{9,8},{10,11... | collective-permute-start | bytes 270344 | tf_op jit(solution)/shard_map/ppermute | solution.py:702
  2.2 2.6 %collective-permute-start.1 = (f32[11,8,256]{2,1,0:T(8,128)S(1)}, f32[11,8,256]{2,1,0:T(8,128)S(1)}, u32[]{:S(2)}, u32[]{:S(2)}) collective-permute-start(f32[11,8,256]{2,1,0:T(8,128)S(1)} %get-tuple-element.36), channel_id=1, source_target_pairs={{0,3},{1,2},{2,1},{3,0},{4,7},{5,6},{6,5},{7,4},{8,11},{9,10},{10,... | collective-permute-start | bytes 270344 | tf_op jit(solution)/shard_map/ppermute | solution.py:702
  4.8 0.7 %copy-done.1 = s32[8,4,16]{2,1,0:T(4,128)S(1)} copy-done((s32[8,4,16]{2,1,0:T(4,128)S(1)}, s32[8,4,16]{2,1,0:T(4,128)}, u32[]{:S(2)}) %copy-start.1) | copy-done | bytes 2072
  5.5 0.7 %copy-done.3 = f32[304]{0:T(512)S(1)} copy-done((f32[304]{0:T(512)S(1)}, f32[304]{0:T(512)}, u32[]{:S(2)}) %copy-start.3) | copy-done | bytes 1240
  6.2 1.0 %shard_map.83 = (f32[2048,128]{1,0:T(8,128)S(1)}, f32[128,128]{1,0:T(8,128)S(1)}, f32[10,8,256]{2,1,0:T(8,128)S(1)}, f32[10,8,256]{2,1,0:T(8,128)S(1)}) custom-call(f32[2048,128]{1,0:T(8,128)S(1)} %get-tuple-element.28.raw, f32[128,128]{1,0:T(8,128)S(1)} %get-tuple-element.29.mask.mask_ref, f32[8,128]{1,0:T(8,128)S(1)} %get-tuple-element.30.slots_ref, ...), custom_call_target="tpu_custom_call" | custom-call | flops 1048576 | bytes 1048576 | tf_op jit(solution)/shard_map/pallas_call | solution.py:755
  7.3 0.0 collective-permute-done.got_a.col_a
  7.3 0.4 collective-permute-done.1.got_b.col_b
  7.7 1.5 %collective-permute-start.2 = (f32[11,8,256]{2,1,0:T(8,128)S(1)}, f32[11,8,256]{2,1,0:T(8,128)S(1)}, u32[]{:S(2)}, u32[]{:S(2)}) collective-permute-start(f32[11,8,256]{2,1,0:T(8,128)S(1)} %get-tuple-element.40), channel_id=1, source_target_pairs={{0,4},{4,0},{8,12},{12,8},{16,20},{20,16},{24,28},{28,24},{1,5},{5... | collective-permute-start | bytes 270344 | tf_op jit(solution)/shard_map/ppermute | solution.py:714
  9.2 0.1 collective-permute-start.3
  9.3 0.7 %shard_map.86.force_in = f32[2048,128]{1,0:T(8,128)S(1)} custom-call(f32[2048,128]{1,0:T(8,128)S(1)} %get-tuple-element.31.refs_0_.fields, f32[128,128]{1,0:T(8,128)S(1)} %get-tuple-element.39.energy.refs_1_), custom_call_target="tpu_custom_call" | custom-call | flops 8388608 | bytes 4194304 | tf_op jit(solution)/shard_map/pallas_call | solution.py:782
  10.0 3.5 %collective-permute-done.2.slab_a = f32[11,8,256]{2,1,0:T(8,128)S(1)} collective-permute-done((f32[11,8,256]{2,1,0:T(8,128)S(1)}, f32[11,8,256]{2,1,0:T(8,128)S(1)}, u32[]{:S(2)}, u32[]{:S(2)}) %collective-permute-start.2) | collective-permute-done | bytes 90144 | tf_op jit(solution)/shard_map/ppermute | solution.py:714
  13.5 0.0 collective-permute-done.3.slab_b
  13.6 0.0 copy-done
  13.6 0.0 copy-done.2
  13.6 0.5 %shard_map.85.keep = f32[976,128]{1,0:T(8,128)S(1)} custom-call(f32[48,128]{1,0:T(8,128)S(1)} %get-tuple-element.37.planes, s32[16,128]{1,0:T(8,128)S(1)} %get-tuple-element.38.bounds, f32[128,128]{1,0:T(8,128)S(1)} %get-tuple-element.29.mask.mask_ref, f32[96,48]{1,0:T(8,128)S(1)} %copy-done.2, f32[128,256]{1,0:T(8,128)S(1)} %copy-done, ...), custom_call_target="tpu_custom_call" | custom-call | flops 1048576 | bytes 1048576 | tf_op jit(solution)/shard_map/pallas_call | solution.py:771
  14.1 0.9 %shard_map.87 = (f32[3536,128]{1,0:T(8,128)S(1)}, f32[32,1,128]{2,1,0:T(1,128)S(1)}) custom-call(f32[2048,128]{1,0:T(8,128)S(1)} %get-tuple-element.31.refs_0_.fields, f32[976,128]{1,0:T(8,128)S(1)} %shard_map.85.keep, f32[2048,128]{1,0:T(8,128)S(1)} %shard_map.86.force_in, f32[11,8,256]{2,1,0:T(8,128)S(1)} %collective-permute-done.got_a.col_a, ...), custom_call_target="tpu_custom_call" | custom-call | flops 1048576 | bytes 1048576 | tf_op jit(solution)/shard_map/pallas_call | solution.py:790
  15.0 13.0 %all_to_all.10.got = f32[32,1,128]{2,1,0:T(1,128)S(1)} all-to-all(f32[32,1,128]{2,1,0:T(1,128)S(1)} %get-tuple-element.42), channel_id=1, replica_groups=mesh['slab'=8,'col'=4] {'slab','col'}, dimensions={0} | all-to-all | bytes 32768 | tf_op jit(solution)/shard_map/all_to_all | solution.py:797
  28.0 1.1 %shard_map.88 = (f32[3024,128]{1,0:T(8,128)S(1)}, f32[9,8,256]{2,1,0:T(8,128)S(1)}, f32[9,8,256]{2,1,0:T(8,128)S(1)}) custom-call(f32[32,1,128]{2,1,0:T(1,128)S(1)} %all_to_all.10.got, f32[3536,128]{1,0:T(8,128)S(1)} %get-tuple-element.43.grown), custom_call_target="tpu_custom_call" | custom-call | flops 1048576 | bytes 1048576 | tf_op jit(solution)/shard_map/pallas_call | solution.py:799
  29.1 0.6 %collective-permute-start.6 = (f32[9,8,256]{2,1,0:T(8,128)S(1)}, f32[9,8,256]{2,1,0:T(8,128)S(1)}, u32[]{:S(2)}, u32[]{:S(2)}) collective-permute-start(f32[9,8,256]{2,1,0:T(8,128)S(1)} %get-tuple-element.47), channel_id=1, source_target_pairs={{0,4},{4,0},{8,12},{12,8},{16,20},{20,16},{24,28},{28,24},{1,5},{5... | collective-permute-start | bytes 221192 | tf_op jit(solution)/shard_map/ppermute | solution.py:714
  29.8 0.0 collective-permute-start.7
  29.8 0.1 shard_map.90
  29.9 0.6 %collective-permute-start.4 = (f32[9,8,256]{2,1,0:T(8,128)S(1)}, f32[9,8,256]{2,1,0:T(8,128)S(1)}, u32[]{:S(2)}, u32[]{:S(2)}) collective-permute-start(f32[9,8,256]{2,1,0:T(8,128)S(1)} %get-tuple-element.45), channel_id=1, source_target_pairs={{0,1},{1,0},{2,3},{3,2},{4,5},{5,4},{6,7},{7,6},{8,9},{9,8},{10,11... | collective-permute-start | bytes 221192 | tf_op jit(solution)/shard_map/ppermute | solution.py:702
  30.4 0.3 collective-permute-start.5
  30.7 0.7 %shard_map.89.force_in = f32[2048,128]{1,0:T(8,128)S(1)} custom-call(f32[3024,128]{1,0:T(8,128)S(1)} %get-tuple-element.44.refs_0_.fields.keep), custom_call_target="tpu_custom_call" | custom-call | flops 8388608 | bytes 4194304 | tf_op jit(solution)/shard_map/pallas_call | solution.py:782
  31.4 2.2 %collective-permute-done.6.slab_a = f32[9,8,256]{2,1,0:T(8,128)S(1)} collective-permute-done((f32[9,8,256]{2,1,0:T(8,128)S(1)}, f32[9,8,256]{2,1,0:T(8,128)S(1)}, u32[]{:S(2)}, u32[]{:S(2)}) %collective-permute-start.6) | collective-permute-done | bytes 73760 | tf_op jit(solution)/shard_map/ppermute | solution.py:714
  33.6 0.0 collective-permute-done.7.slab_b
  33.6 0.0 collective-permute-done.4.col_a
  33.6 1.2 %collective-permute-done.5.col_b = f32[9,8,256]{2,1,0:T(8,128)S(1)} collective-permute-done((f32[9,8,256]{2,1,0:T(8,128)S(1)}, f32[9,8,256]{2,1,0:T(8,128)S(1)}, u32[]{:S(2)}, u32[]{:S(2)}) %collective-permute-start.5) | collective-permute-done | bytes 73760 | tf_op jit(solution)/shard_map/ppermute | solution.py:702
  34.8 0.9 %shard_map.91 = (f32[3536,128]{1,0:T(8,128)S(1)}, f32[32,1,128]{2,1,0:T(1,128)S(1)}) custom-call(f32[3024,128]{1,0:T(8,128)S(1)} %get-tuple-element.44.refs_0_.fields.keep, f32[3024,128]{1,0:T(8,128)S(1)} %get-tuple-element.44.refs_0_.fields.keep, f32[2048,128]{1,0:T(8,128)S(1)} %shard_map.89.force_in, f32[9,8,256]{2,1,0:T(8,128)S(1)} %collective-permute-done.4.col_a, ...), custom_call_target="tpu_custom_call" | custom-call | flops 1048576 | bytes 1048576 | tf_op jit(solution)/shard_map/pallas_call | solution.py:790
  35.6 9.6 %all_to_all.11.got = f32[32,1,128]{2,1,0:T(1,128)S(1)} all-to-all(f32[32,1,128]{2,1,0:T(1,128)S(1)} %get-tuple-element.49), channel_id=1, replica_groups=mesh['slab'=8,'col'=4] {'slab','col'}, dimensions={0} | all-to-all | bytes 32768 | tf_op jit(solution)/shard_map/all_to_all | solution.py:797
  45.2 2.2 %shard_map.92 = f32[16,64,256]{2,1,0:T(8,128)} custom-call(f32[32,1,128]{2,1,0:T(1,128)S(1)} %all_to_all.11.got, f32[3536,128]{1,0:T(8,128)S(1)} %get-tuple-element.50.grown), custom_call_target="tpu_custom_call" | custom-call | flops 1048576 | bytes 1048576 | tf_op jit(solution)/shard_map/pallas_call | solution.py:811
  (5 shorter events, 0.0 us)
Async XLA Ops:
  1.7 5.6 %collective-permute-start = (f32[11,8,256]{2,1,0:T(8,128)S(1)}, f32[11,8,256]{2,1,0:T(8,128)S(1)}, u32[]{:S(2)}, u32[]{:S(2)}) collective-permute-start(f32[11,8,256]{2,1,0:T(8,128)S(1)} %get-tuple-element.35), channel_id=1, source_target_pairs={{0,1},{1,0},{2,3},{3,2},{4,5},{5,4},{6,7},{7,6},{8,9},{9,8},{10,11... | collective-permute-start | bytes 270344 | tf_op jit(solution)/shard_map/ppermute | solution.py:702
  2.2 5.5 %collective-permute-start.1 = (f32[11,8,256]{2,1,0:T(8,128)S(1)}, f32[11,8,256]{2,1,0:T(8,128)S(1)}, u32[]{:S(2)}, u32[]{:S(2)}) collective-permute-start(f32[11,8,256]{2,1,0:T(8,128)S(1)} %get-tuple-element.36), channel_id=1, source_target_pairs={{0,3},{1,2},{2,1},{3,0},{4,7},{5,6},{6,5},{7,4},{8,11},{9,10},{10,... | collective-permute-start | bytes 270344 | tf_op jit(solution)/shard_map/ppermute | solution.py:702
  4.8 0.7 %copy-start.1 = (s32[8,4,16]{2,1,0:T(4,128)S(1)}, s32[8,4,16]{2,1,0:T(4,128)}, u32[]{:S(2)}) copy-start(s32[8,4,16]{2,1,0:T(4,128)} %ids_ref.1) | copy-start | bytes 6148
  5.5 0.7 %copy-start.3 = (f32[304]{0:T(512)S(1)}, f32[304]{0:T(512)}, u32[]{:S(2)}) copy-start(f32[304]{0:T(512)} %energy_ref.1) | copy-start | bytes 3652
  6.2 7.3 %copy-start = (f32[128,256]{1,0:T(8,128)S(1)}, f32[128,256]{1,0:T(8,128)}, u32[]{:S(2)}) copy-start(f32[128,256]{1,0:T(8,128)} %constant.5.clone.height) | copy-start | bytes 393220
  6.2 7.3 %copy-start.2 = (f32[96,48]{1,0:T(8,128)S(1)}, f32[96,48]{1,0:T(8,128)}, u32[]{:S(2)}) copy-start(f32[96,48]{1,0:T(8,128)} %constant.4.clone.weights) | copy-start | bytes 55300
  7.7 5.8 %collective-permute-start.2 = (f32[11,8,256]{2,1,0:T(8,128)S(1)}, f32[11,8,256]{2,1,0:T(8,128)S(1)}, u32[]{:S(2)}, u32[]{:S(2)}) collective-permute-start(f32[11,8,256]{2,1,0:T(8,128)S(1)} %get-tuple-element.40), channel_id=1, source_target_pairs={{0,4},{4,0},{8,12},{12,8},{16,20},{20,16},{24,28},{28,24},{1,5},{5... | collective-permute-start | bytes 270344 | tf_op jit(solution)/shard_map/ppermute | solution.py:714
  9.2 4.3 %collective-permute-start.3 = (f32[11,8,256]{2,1,0:T(8,128)S(1)}, f32[11,8,256]{2,1,0:T(8,128)S(1)}, u32[]{:S(2)}, u32[]{:S(2)}) collective-permute-start(f32[11,8,256]{2,1,0:T(8,128)S(1)} %get-tuple-element.41), channel_id=1, source_target_pairs={{0,1},{1,0},{2,3},{3,2},{4,8},{5,9},{6,10},{7,11},{8,4},{9,5},{10,... | collective-permute-start | bytes 270344 | tf_op jit(solution)/shard_map/ppermute | solution.py:714
  29.1 4.4 %collective-permute-start.6 = (f32[9,8,256]{2,1,0:T(8,128)S(1)}, f32[9,8,256]{2,1,0:T(8,128)S(1)}, u32[]{:S(2)}, u32[]{:S(2)}) collective-permute-start(f32[9,8,256]{2,1,0:T(8,128)S(1)} %get-tuple-element.47), channel_id=1, source_target_pairs={{0,4},{4,0},{8,12},{12,8},{16,20},{20,16},{24,28},{28,24},{1,5},{5... | collective-permute-start | bytes 221192 | tf_op jit(solution)/shard_map/ppermute | solution.py:714
  29.8 3.8 %collective-permute-start.7 = (f32[9,8,256]{2,1,0:T(8,128)S(1)}, f32[9,8,256]{2,1,0:T(8,128)S(1)}, u32[]{:S(2)}, u32[]{:S(2)}) collective-permute-start(f32[9,8,256]{2,1,0:T(8,128)S(1)} %get-tuple-element.48), channel_id=1, source_target_pairs={{0,1},{1,0},{2,3},{3,2},{4,8},{5,9},{6,10},{7,11},{8,4},{9,5},{10,... | collective-permute-start | bytes 221192 | tf_op jit(solution)/shard_map/ppermute | solution.py:714
  29.9 3.7 %collective-permute-start.4 = (f32[9,8,256]{2,1,0:T(8,128)S(1)}, f32[9,8,256]{2,1,0:T(8,128)S(1)}, u32[]{:S(2)}, u32[]{:S(2)}) collective-permute-start(f32[9,8,256]{2,1,0:T(8,128)S(1)} %get-tuple-element.45), channel_id=1, source_target_pairs={{0,1},{1,0},{2,3},{3,2},{4,5},{5,4},{6,7},{7,6},{8,9},{9,8},{10,11... | collective-permute-start | bytes 221192 | tf_op jit(solution)/shard_map/ppermute | solution.py:702
  30.4 4.3 %collective-permute-start.5 = (f32[9,8,256]{2,1,0:T(8,128)S(1)}, f32[9,8,256]{2,1,0:T(8,128)S(1)}, u32[]{:S(2)}, u32[]{:S(2)}) collective-permute-start(f32[9,8,256]{2,1,0:T(8,128)S(1)} %get-tuple-element.46), channel_id=1, source_target_pairs={{0,3},{1,2},{2,1},{3,0},{4,7},{5,6},{6,5},{7,4},{8,11},{9,10},{10,... | collective-permute-start | bytes 221192 | tf_op jit(solution)/shard_map/ppermute | solution.py:702

commit v7 on v6

--- a/solution.py
+++ b/solution.py
@@ -14,6 +14,8 @@
 COUPLING = 1.5
 BELOW, ABOVE, LEFT, RIGHT = range(4)
 FACES = 4
+MASK = 2 * SHARE
+THERMAL = MASK + 1
 LANES = 128
 ROWS = 8
 HIGHEST = lax.Precision.HIGHEST
@@ -136,7 +138,8 @@
         return take(self.ref, self.near_base + k * self.cells + x * self.cy, self.cy)
 
     def energy(self, q):
-        return self.ref[self.energy_base + q * ROWS : self.energy_base + (q + 1) * ROWS, :]
+        at = self.energy_base + q * ROWS
+        return self.ref[pl.ds(at if isinstance(at, int) else pl.multiple_of(at, ROWS), ROWS), :]
 
 
 def keep_on(out, out_base, kept, count):
@@ -153,32 +156,38 @@
     return even, (jnp.where(even, high, low), jnp.where(even, low, high))
 
 
-def pack_faces(fields, cx, cy, slots, out_refs, axis, columns, slot_of=lambda place: place[0] * SHARE + place[1]):
+def pack_faces(fields, energy, cx, cy, slots, out_refs, axis, columns):
     low, high = (LEFT, RIGHT) if columns else (BELOW, ABOVE)
+    first, last, top, bottom = edges()
     _, faces = pair_faces(axis, low, high)
     for out, face in zip(out_refs, faces):
-        is_high = face == high
-        for depth in range(2):
+
+        def plane(q, depth):
             if columns:
-                first = jnp.where(is_high, cy - 1 - depth, depth)
-                plane = lambda q: take(fields, q * (cx * cy) + first, cx, cy)
-            else:
-                first = jnp.where(is_high, cx - 1 - depth, depth) * cy
-                plane = lambda q: take(fields, q * (cx * cy) + first, cy)
-            for j in range(SHARE):
-                fill(out, depth * SHARE + j, plane(slot_of((face, j))))
-            if depth == 0:
-                s0 = s1 = None
-                for q in range(slots):
-                    v0, v1 = plane(q)
-                    s0 = v0 * v0 if s0 is None else s0 + v0 * v0
-                    s1 = v1 * v1 if s1 is None else s1 + v1 * v1
-                fill(out, 2 * SHARE, (s0, s1))
+                return take(fields, q * (cx * cy) + jnp.where(face == high, cy - 1 - depth, depth), cx, cy)
+            return take(fields, q * (cx * cy) + jnp.where(face == high, cx - 1 - depth, depth) * cy, cy)
+
+        squares = [None, None]
+        for q in range(slots):
+            for i, v in enumerate(plane(q, 0)):
+                squares[i] = v * v if squares[i] is None else squares[i] + v * v
+        for j in range(SHARE):
+            q = face * SHARE + j
+            centre, inner = plane(q, 0), plane(q, 1)
+            near = along_height(centre[0], centre[1], first, last)
+            e = energy(q)
+            forces = []
+            for i in range(2):
+                n = near[i] + along_rows(centre[i], top, bottom, None, None) + inner[i]
+                forces.append(force_of(centre[i], n, 2.0 * COUPLING * squares[i], e))
+            fill(out, j, centre)
+            fill(out, SHARE + j, forces)
 
 
 def open_body(
-    cx, cy, slots, slabs, cols, ids_hbm, rows_hbm, fields_hbm, mask_hbm, coarse_hbm,
-    raw, mask, slots_ref, bounds, planes, msg_a, msg_b, ids_smem, rows_smem, ids_ref, coarse_ref, mask_ref, sems,
+    cx, cy, slots, slabs, cols, ids_hbm, rows_hbm, energy_hbm, fields_hbm, mask_hbm, coarse_hbm,
+    fields, mask, slots_ref, energy_out, bounds, planes, msg_a, msg_b,
+    ids_smem, rows_smem, energy_smem, ids_ref, coarse_ref, mask_ref, raw, sems,
 ):
     cells = cx * cy
     loads = [
@@ -186,6 +195,7 @@
         pltpu.make_async_copy(ids_hbm, ids_ref, sems.at[1]),
         pltpu.make_async_copy(rows_hbm, rows_smem, sems.at[2]),
         pltpu.make_async_copy(coarse_hbm, coarse_ref, sems.at[3]),
+        pltpu.make_async_copy(energy_hbm, energy_smem, sems.at[8]),
     ]
     for i in range(2):
         half = pl.ds(i * LANES, LANES)
@@ -198,18 +208,24 @@
         )
     for load in loads:
         load.start()
-    for load in loads[:4]:
+    for load in loads[:5]:
         load.wait()
     place = slot_places(slabs, cols, slots, ids_ref, ids_smem)
     sub = lax.broadcasted_iota(jnp.int32, (slots, LANES), 0).astype(jnp.float32)
     slot_row = jnp.sum(place * sub, axis=0, keepdims=True)
     slots_ref[...] = jnp.broadcast_to(slot_row, (ROWS, LANES))
     lane = lax.broadcasted_iota(jnp.int32, (1, LANES), 1)
-    taken = lambda q: jnp.sum(jnp.where(lane == q, slot_row, 0.0)).astype(jnp.int32)
-    left = [taken(LEFT * SHARE + j) for j in range(SHARE)]
-    right = [taken(RIGHT * SHARE + j) for j in range(SHARE)]
-
-    s = lax.axis_index("slab")
+    taken = [jnp.sum(jnp.where(lane == q, slot_row, 0.0)).astype(jnp.int32) for q in range(slots)]
+    at_rows = lax.broadcasted_iota(jnp.int32, (slots, LANES), 0)
+    own_energy = jnp.zeros((slots, LANES), jnp.float32)
+    s, c = lax.axis_index("slab"), lax.axis_index("col")
+    for q in range(slots):
+        own_energy = jnp.where(at_rows == q, energy_smem[ids_smem[s, c, q]], own_energy)
+    energy_row = jnp.sum(place * own_energy, axis=0, keepdims=True)
+    for q in range(slots):
+        value = jnp.sum(jnp.where(lane == q, energy_row, 0.0), axis=1, keepdims=True)
+        energy_out[q * ROWS : (q + 1) * ROWS, :] = jnp.broadcast_to(value, (ROWS, LANES))
+
     start = jnp.int32(0)
     for t in range(slabs):
         start = start + jnp.where(t < s, rows_smem[t], 0)
@@ -222,27 +238,27 @@
     ] + [jnp.int32(0), jnp.int32(1), live - 2, live - 1]
     _, faces = pair_faces("col", LEFT, RIGHT)
     for out in (msg_a, msg_b):
-        out[2 * SHARE + 2] = jnp.zeros((ROWS, out.shape[2]), jnp.float32)
+        out[THERMAL] = jnp.zeros((ROWS, out.shape[2]), jnp.float32)
     planes[...] = jnp.zeros(planes.shape, jnp.float32)
     for i, p in enumerate(chosen):
         planes[i * ROWS + 1 : i * ROWS + 1 + coarse_y, :] = coarse_ref[p]
         for out, face in zip((msg_a, msg_b), faces):
             row = jnp.where(face == RIGHT, coarse_y - 1, 0)
             spot = slice(i // ROWS * LANES, (i // ROWS + 1) * LANES)
-            out[2 * SHARE + 2, i % ROWS : i % ROWS + 1, spot] = coarse_ref[p, pl.ds(row, 1), :]
-
-    for load in loads[4:]:
+            out[THERMAL, i % ROWS : i % ROWS + 1, spot] = coarse_ref[p, pl.ds(row, 1), :]
+
+    for load in loads[5:]:
         load.wait()
     mask[...] = mask_ref[...].astype(jnp.float32)
 
-    def slot_of(place):
-        face, j = place
-        return jnp.where(face == RIGHT, right[j], left[j])
-
-    pack_faces(raw, cx, cy, slots, (msg_a, msg_b), "col", True, slot_of)
+    for q in range(slots):
+        for i, part in enumerate(take(raw, taken[q] * cells, cells)):
+            put(fields, q * cells, i, part)
+    energy_of = lambda q: energy_out[pl.ds(pl.multiple_of(q * ROWS, ROWS), ROWS), :]
+    pack_faces(fields, energy_of, cx, cy, slots, (msg_a, msg_b), "col", True)
     for out, face in zip((msg_a, msg_b), faces):
         first = jnp.where(face == RIGHT, cy - 1, 0)
-        fill(out, 2 * SHARE + 1, take(mask, first, cx, cy))
+        fill(out, MASK, take(mask, first, cx, cy))
 
 
 def near_planes(cx, slabs):
@@ -251,29 +267,19 @@
     return [jnp.clip(s * half - 1 + i, 0, slabs * half - 1) for i in range(half + 2)]
 
 
-def arrange_body(
-    cx, cy, slots, raw, mask, slots_ref, ids_ref, energy_ref, fields, energy_out, pre_a, pre_b
-):
-    cells = cx * cy
-    s, c = lax.axis_index("slab"), lax.axis_index("col")
-    for q in range(slots):
-        slot = slots_ref[0, q].astype(jnp.int32)
-        for i, part in enumerate(take(raw, slot * cells, cells)):
-            put(fields, q * cells, i, part)
-        value = jnp.full((ROWS, LANES), energy_ref[ids_ref[s, c, slot]], jnp.float32)
-        energy_out[q * ROWS : (q + 1) * ROWS, :] = value
-    pack_faces(fields, cx, cy, slots, (pre_a, pre_b), "slab", False)
+def faces_body(cx, cy, slots, fields, energy, mask, msg_a, msg_b):
+    energy_of = lambda q: energy[pl.ds(pl.multiple_of(q * ROWS, ROWS), ROWS), :]
+    pack_faces(fields, energy_of, cx, cy, slots, (msg_a, msg_b), "slab", False)
     _, faces = pair_faces("slab", BELOW, ABOVE)
-    for out, face in zip((pre_a, pre_b), faces):
+    for out, face in zip((msg_a, msg_b), faces):
         first = jnp.where(face == ABOVE, cx - 1, 0) * cy
-        fill(out, 2 * SHARE + 1, take(mask, first, cy))
-
-
-def slab_body(cx, slabs, cols, coarse_y, own, pre_a, pre_b, got_a, got_b, msg_a, msg_b, planes):
+        fill(out, MASK, take(mask, first, cy))
+
+
+def slab_body(cx, slabs, cols, coarse_y, own, got_a, got_b, msg_a, msg_b, planes):
     have = present(slabs, cols)
     even, _ = pair_faces("col", LEFT, RIGHT)
-    thermal = 2 * SHARE + 2
-    from_a, from_b = got_a[thermal], got_b[thermal]
+    from_a, from_b = got_a[THERMAL], got_b[THERMAL]
     lower = jnp.where(even, from_b, from_a)
     upper = jnp.where(even, from_a, from_b)
     sub = lax.broadcasted_iota(jnp.int32, (ROWS, LANES), 0)
@@ -290,11 +296,10 @@
             planes[i * ROWS : (i + 1) * ROWS, :] = plane
     first = cx // 2 + 2
     _, faces = pair_faces("slab", BELOW, ABOVE)
-    for out, pre, face in zip((msg_a, msg_b), (pre_a, pre_b), faces):
-        out[:thermal] = pre[...]
+    for out, face in zip((msg_a, msg_b), faces):
         for i in range(2):
             plane = jnp.where(face == ABOVE, widened[first + 2 + i], widened[first + i])
-            out[thermal, :, i * LANES : (i + 1) * LANES] = plane
+            out[:, i * LANES : (i + 1) * LANES] = plane
 
 
 def axis_weights(cells):
@@ -330,14 +335,14 @@
 
 def mobility_body(
     cx, cy, slots, slabs, cols, planes, bounds, mask_ref, weights, height, energy, slots_ref,
-    col_a, col_b, slab_a, slab_b, keep, near,
+    col_a, col_b, slab_a, slab_b, ends_a, ends_b, keep, near,
 ):
     start, end = bounds[0:ROWS, :], bounds[ROWS : 2 * ROWS, :]
     even_s, _ = pair_faces("slab", BELOW, ABOVE)
     even_c, _ = pair_faces("col", LEFT, RIGHT)
-    thermal, mask = 2 * SHARE + 2, 2 * SHARE + 1
-    below = jnp.where(even_s, slab_b[thermal], slab_a[thermal])
-    above = jnp.where(even_s, slab_a[thermal], slab_b[thermal])
+    mask = MASK
+    below = jnp.where(even_s, ends_b[...], ends_a[...])
+    above = jnp.where(even_s, ends_a[...], ends_b[...])
     for i, p in enumerate(near_planes(cx, slabs)):
         p = jnp.full((ROWS, LANES), p, jnp.int32)
         own = planes[i * ROWS : (i + 1) * ROWS, :]
@@ -515,35 +520,27 @@
     grown, sums_ref, halos,
 ):
     cells = cx * cy
-    marks = edges()
-    first, last, top, bottom = marks
+    _, _, top, bottom = edges()
     have = present(slabs, cols)
     kept = Kept(keep, base, cx, cy, slots)
     layout = Grown(cx, cy, slots)
     keep_on(grown, layout.kept, kept, layout.count)
     for k, pick in enumerate(arrivals(col_a, col_b, slab_a, slab_b)):
-        s0, s1 = split(2.0 * COUPLING * pick(2 * SHARE))
-        h0, h1 = kept.rate_beside(k)
+        rate = kept.rate_beside(k)
         for j in range(SHARE):
             q = k * SHARE + j
-            v0, v1 = split(jnp.where(have[k], pick(j), 0.0))
-            put(halos, q * ROWS, 0, v0)
-            put(halos, q * ROWS, 1, v1)
-            o0, o1 = split(pick(SHARE + j))
             if k == BELOW:
-                i0, i1 = take(fields, q * cells, cy)
+                own = take(fields, q * cells, cy)
             elif k == ABOVE:
-                i0, i1 = take(fields, (q + 1) * cells - cy, cy)
+                own = take(fields, (q + 1) * cells - cy, cy)
             elif k == LEFT:
-                i0, i1 = take(fields, q * cells, cx, cy)
+                own = take(fields, q * cells, cx, cy)
             else:
-                i0, i1 = take(fields, q * cells + cy - 1, cx, cy)
-            n0, n1 = along_height(v0, v1, first, last)
-            n0 = n0 + along_rows(v0, top, bottom, None, None) + o0 + i0
-            n1 = n1 + along_rows(v1, top, bottom, None, None) + o1 + i1
-            e = kept.energy(q)
-            put(grown, layout.halos + q * ROWS, 0, v0 - h0 * force_of(v0, n0, s0, e))
-            put(grown, layout.halos + q * ROWS, 1, v1 - h1 * force_of(v1, n1, s1, e))
+                own = take(fields, q * cells + cy - 1, cx, cy)
+            beside, force = split(jnp.where(have[k], pick(j), 0.0)), split(pick(SHARE + j))
+            for i in range(2):
+                put(halos, q * ROWS, i, beside[i])
+                put(grown, layout.halos + q * ROWS, i, beside[i] - rate[i] * (force[i] - own[i]))
 
     energy_sum = None
     for q in range(slots):
@@ -663,13 +660,15 @@
         put(fields, q * cx * cy + x * cy, i, value)
 
     settle(cx, cy, slots, got, grown, store)
-    pack_faces(fields, cx, cy, slots, (slab_a, slab_b), "slab", False)
     layout = Grown(cx, cy, slots)
     keep_on(fields, slots * cx * cy, Kept(grown, layout.kept, cx, cy, slots), layout.count)
+    energy = Kept(fields, slots * cx * cy, cx, cy, slots).energy
+    pack_faces(fields, energy, cx, cy, slots, (slab_a, slab_b), "slab", False)
 
 
 def cols_body(cx, cy, slots, fields, col_a, col_b):
-    pack_faces(fields, cx, cy, slots, (col_a, col_b), "col", True)
+    energy = Kept(fields, slots * cx * cy, cx, cy, slots).energy
+    pack_faces(fields, energy, cx, cy, slots, (col_a, col_b), "col", True)
 
 
 def last_body(cx, cy, slots, got, grown, out, result, order, sems, order_sem):
@@ -722,59 +721,62 @@
     capacity, _, coarse_z = coarse_temp.shape
     raw = order_params.reshape(slots * cells, cz)
     mask = layer_mask.reshape(cells, cz)
-    message = f32(2 * SHARE + 3, ROWS, cz)
-    short = f32(2 * SHARE + 1, ROWS, cz)
+    message = f32(THERMAL + 1, ROWS, cz)
+    short = f32(2 * SHARE, ROWS, cz)
     state = f32(2 * slots * cells, cz // 2)
 
     hbm = lambda x: pltpu.with_memory_space_constraint(x, pltpu.HBM)
     near = cx // 2 + 2
-    raw, mask, slot_order, bounds, planes, col_a, col_b = call(
+    fields, mask, slot_order, slot_energy, bounds, planes, col_a, col_b = call(
         functools.partial(open_body, cx, cy, slots, slabs, cols),
         (
             state,
             f32(2 * cells, LANES),
             f32(ROWS, LANES),
+            f32(slots * ROWS, LANES),
             jax.ShapeDtypeStruct((2 * ROWS, LANES), jnp.int32),
             f32((near + 4) * ROWS, LANES),
             message,
             message,
         ),
-        [HBM] * 5,
-        (VMEM,) * 7,
+        [HBM] * 6,
+        (VMEM,) * 8,
         [
             pltpu.SMEM(grain_ids.shape, jnp.int32),
             pltpu.SMEM(coarse_rows.shape, jnp.int32),
+            pltpu.SMEM(energy.shape, jnp.float32),
             pltpu.VMEM(grain_ids.shape, jnp.int32),
             pltpu.VMEM(coarse_temp.shape, jnp.float32),
             pltpu.VMEM((2 * cells, LANES), jnp.int32),
-            pltpu.SemaphoreType.DMA((8,)),
+            pltpu.VMEM(state.shape, jnp.float32),
+            pltpu.SemaphoreType.DMA((9,)),
         ],
-    )(hbm(grain_ids), hbm(coarse_rows), hbm(raw), hbm(mask), hbm(coarse_temp))
+    )(hbm(grain_ids), hbm(coarse_rows), hbm(energy), hbm(raw), hbm(mask), hbm(coarse_temp))
     col_a, col_b = exchange_cols(col_a, col_b)
-    packed = f32(2 * SHARE + 2, ROWS, cz)
-    fields, slot_energy, pre_a, pre_b = call(
-        functools.partial(arrange_body, cx, cy, slots),
-        (state, f32(slots * ROWS, LANES), packed, packed),
-        [VMEM, VMEM, SMEM, SMEM, SMEM],
-        (VMEM,) * 4,
-    )(raw, mask, slot_order, grain_ids, energy)
-    slab_a, slab_b, planes = call(
+    slab_a, slab_b = call(
+        functools.partial(faces_body, cx, cy, slots),
+        (f32(THERMAL, ROWS, cz),) * 2,
+        [VMEM] * 3,
+        (VMEM,) * 2,
+    )(fields, slot_energy, mask)
+    slab_b, slab_a = exchange_slabs(slab_a, slab_b)
+    ends_a, ends_b, planes = call(
         functools.partial(slab_body, cx, slabs, cols, coarse_temp.shape[1]),
-        (message, message, f32(near * ROWS, LANES)),
-        [VMEM] * 5,
+        (f32(ROWS, cz), f32(ROWS, cz), f32(near * ROWS, LANES)),
+        [VMEM] * 3,
         (VMEM,) * 3,
-    )(planes, pre_a, pre_b, col_a, col_b)
-    slab_b, slab_a = exchange_slabs(slab_a, slab_b)
+    )(planes, col_a, col_b)
+    ends_b, ends_a = exchange_slabs(ends_a, ends_b)
     weights = jnp.asarray(plane_weights(cx, cy))
     height = jnp.asarray(height_weights(cz, coarse_z))
     count = Kept.rows(cells, slots)
     keep = call(
         functools.partial(mobility_body, cx, cy, slots, slabs, cols),
         f32(2 * count, LANES),
-        [VMEM] * 11,
+        [VMEM] * 13,
         VMEM,
         [pltpu.VMEM((near * ROWS, LANES), jnp.float32)],
-    )(planes, bounds, mask, weights, height, slot_energy, slot_order, col_a, col_b, slab_a, slab_b)
+    )(planes, bounds, mask, weights, height, slot_energy, slot_order, col_a, col_b, slab_a, slab_b, ends_a, ends_b)
 
     for pair in range(STEPS // 2):
         base = None if pair == 0 else slots * cells

time: 47.7 us -> 46.4 us (0.973)
  waiting for transfers between devices: 7.33 us -> 5.15 us
  starting transfers between devices: 6.19 us -> 8.27 us
  local copies, waits for them, and re-layouts: 1.41 us -> 0.01 us
  blocking collectives: 22.6 us -> 23.7 us
  Pallas kernels: 9.72 us -> 8.91 us
    ppermute x2 -> x3, waiting for transfers between devices: 5.7 us -> 2.96 us  [exchange_slabs(): lax.ppermute(first, 'slab', one)]
    ppermute x2 -> x3, starting transfers between devices: 2.08 us -> 4.25 us  [exchange_slabs(): lax.ppermute(first, 'slab', one)]
    unnamed x8 -> x4, local copies, waits for them, and re-layouts: 1.41 us -> 0.01 us
    all_to_all x2, blocking collectives: 22.6 us -> 23.7 us  [per_device(): got = lax.all_to_all(sums, ('slab', 'col'), 0, 0)]
    pallas_call x1, Pallas kernels: 1.03 us -> 0.11 us  [per_device(): call(functools.partial(faces_body, cx, cy, slots), (f32(THERMAL, ROWS, cz...]
    ppermute x4, waiting for transfers between devices: 1.63 us -> 2.18 us  [exchange_cols(): return (lax.ppermute(first, 'col', one), lax.ppermute(second, 'col', two))]
  transfers between devices with their start and end apart: 8 -> 10, of which waited for: 4 -> 4; matrix products, arithmetic and copies ran while one was open for 0% -> 0% of each run, Pallas kernels for 5% -> 4%
where the time goes in v7:
time: 46.4 us; the launch traced here: 46.1 us
  blocking collectives  23.7 us (51%)
  Pallas kernels  8.91 us (19%)
  starting transfers between devices  8.27 us (18%)
  waiting for transfers between devices  5.15 us (11%)
    all_to_all x2, blocking collectives, per_device(): got = lax.all_to_all(sums, ('slab', 'col'), 0, 0)  23.7 us
    ppermute x3, starting transfers between devices, exchange_slabs(): lax.ppermute(first, 'slab', one)  4.25 us
    ppermute x4, starting transfers between devices, exchange_cols(): return (lax.ppermute(first, 'col', one), lax.ppermute(second, 'col', two))  4.02 us
    ppermute x3, waiting for transfers between devices, exchange_slabs(): lax.ppermute(first, 'slab', one)  2.96 us
    ppermute x4, waiting for transfers between devices, exchange_cols(): return (lax.ppermute(first, 'col', one), lax.ppermute(second, 'col', two))  2.18 us
    pallas_call x1, Pallas kernels, per_device(): call(functools.partial(last_body, cx, cy, slots), f32(slots, cells, cz),...  2.15 us
    pallas_call x1, Pallas kernels, per_device(): call(functools.partial(open_body, cx, cy, slots, slabs, cols), (state, f3...  1.82 us
    pallas_call x2, Pallas kernels, per_device(): call(functools.partial(sums_body, cx, cy, slots, slabs, cols, devices, ba...  1.62 us
  transfers between devices with their start and end apart: 10, of which 4 were waited for; matrix products, arithmetic and copies ran while one was open for 0% of the time, Pallas kernels for 4%

profile of v7, /device:TPU:0, one launch (start us, length us, event | category | flops | bytes accessed | tf_op | source)
XLA Modules:
  0.0 46.1 jit_solution(2425807989178823940)
XLA Ops:
  0.0 1.8 %shard_map.82 = (f32[2048,128]{1,0:T(8,128)S(1)}, f32[128,128]{1,0:T(8,128)S(1)}, f32[8,128]{1,0:T(8,128)S(1)}, f32[128,128]{1,0:T(8,128)S(1)}, s32[16,128]{1,0:...) custom-call(s32[8,4,16]{2,1,0:T(4,128)} %ids_hbm.1, s32[8]{0:T(128)} %rows_hbm.1, ...), custom_call_target="tpu_custom_call" | custom-call | flops 1048576 | bytes 1048576 | tf_op jit(solution)/shard_map/pallas_call | solution.py:730
  1.8 0.0 copy-start
  1.8 0.0 copy-start.1
  1.9 0.5 %collective-permute-start = (f32[10,8,256]{2,1,0:T(8,128)S(1)}, f32[10,8,256]{2,1,0:T(8,128)S(1)}, u32[]{:S(2)}, u32[]{:S(2)}) collective-permute-start(f32[10,8,256]{2,1,0:T(8,128)S(1)} %get-tuple-element.29), channel_id=1, source_target_pairs={{0,1},{1,0},{2,3},{3,2},{4,5},{5,4},{6,7},{7,6},{8,9},{9,8},{10,11... | collective-permute-start | bytes 245768 | tf_op jit(solution)/shard_map/ppermute | solution.py:701
  2.4 2.6 %collective-permute-start.1 = (f32[10,8,256]{2,1,0:T(8,128)S(1)}, f32[10,8,256]{2,1,0:T(8,128)S(1)}, u32[]{:S(2)}, u32[]{:S(2)}) collective-permute-start(f32[10,8,256]{2,1,0:T(8,128)S(1)} %get-tuple-element.30), channel_id=1, source_target_pairs={{0,3},{1,2},{2,1},{3,0},{4,7},{5,6},{6,5},{7,4},{8,11},{9,10},{10,... | collective-permute-start | bytes 245768 | tf_op jit(solution)/shard_map/ppermute | solution.py:701
  5.0 0.1 shard_map.84
  5.1 1.6 %collective-permute-start.2 = (f32[9,8,256]{2,1,0:T(8,128)S(1)}, f32[9,8,256]{2,1,0:T(8,128)S(1)}, u32[]{:S(2)}, u32[]{:S(2)}) collective-permute-start(f32[9,8,256]{2,1,0:T(8,128)S(1)} %get-tuple-element.36), channel_id=1, source_target_pairs={{0,4},{4,0},{8,12},{12,8},{16,20},{20,16},{24,28},{28,24},{1,5},{5... | collective-permute-start | bytes 221192 | tf_op jit(solution)/shard_map/ppermute | solution.py:713
  6.7 0.0 collective-permute-start.3
  6.7 0.0 collective-permute-done.got_a.col_a
  6.7 1.0 %collective-permute-done.1.got_b.col_b = f32[10,8,256]{2,1,0:T(8,128)S(1)} collective-permute-done((f32[10,8,256]{2,1,0:T(8,128)S(1)}, f32[10,8,256]{2,1,0:T(8,128)S(1)}, u32[]{:S(2)}, u32[]{:S(2)}) %collective-permute-start.1) | collective-permute-done | bytes 81952 | tf_op jit(solution)/shard_map/ppermute | solution.py:701
  7.8 2.1 %collective-permute-start.4 = (f32[8,256]{1,0:T(8,128)S(1)}, f32[8,256]{1,0:T(8,128)S(1)}, u32[]{:S(2)}, u32[]{:S(2)}) collective-permute-start(f32[8,256]{1,0:T(8,128)S(1)} %get-tuple-element.38), channel_id=1, source_target_pairs={{0,4},{4,0},{8,12},{12,8},{16,20},{20,16},{24,28},{28,24},{1,5},{5... | collective-permute-start | bytes 24584 | tf_op jit(solution)/shard_map/ppermute | solution.py:713
  9.8 0.0 collective-permute-start.5
  9.8 0.7 %shard_map.86.force_in = f32[2048,128]{1,0:T(8,128)S(1)} custom-call(f32[2048,128]{1,0:T(8,128)S(1)} %get-tuple-element.27.fields.refs_0_, f32[128,128]{1,0:T(8,128)S(1)} %get-tuple-element.34.energy.refs_1_), custom_call_target="tpu_custom_call" | custom-call | flops 8388608 | bytes 4194304 | tf_op jit(solution)/shard_map/pallas_call | solution.py:784
  10.5 0.0 collective-permute-done.3.slab_b
  10.6 0.9 %collective-permute-done.4.ends_a = f32[8,256]{1,0:T(8,128)S(1)} collective-permute-done((f32[8,256]{1,0:T(8,128)S(1)}, f32[8,256]{1,0:T(8,128)S(1)}, u32[]{:S(2)}, u32[]{:S(2)}) %collective-permute-start.4) | collective-permute-done | bytes 8224 | tf_op jit(solution)/shard_map/ppermute | solution.py:713
  11.5 0.5 %shard_map.85.keep = f32[976,128]{1,0:T(8,128)S(1)} custom-call(f32[48,128]{1,0:T(8,128)S(1)} %get-tuple-element.31.planes, s32[16,128]{1,0:T(8,128)S(1)} %get-tuple-element.32.bounds, f32[128,128]{1,0:T(8,128)S(1)} %get-tuple-element.33.mask.mask_ref, f32[96,48]{1,0:T(8,128)S(1)} %copy-done.1, f32[128,256]{1,0:T(8,128)S(1)} %copy-done, ...), custom_call_target="tpu_custom_call" | custom-call | flops 1048576 | bytes 1048576 | tf_op jit(solution)/shard_map/pallas_call | solution.py:773
  12.0 0.8 %shard_map.87 = (f32[3536,128]{1,0:T(8,128)S(1)}, f32[32,1,128]{2,1,0:T(1,128)S(1)}) custom-call(f32[2048,128]{1,0:T(8,128)S(1)} %get-tuple-element.27.fields.refs_0_, f32[976,128]{1,0:T(8,128)S(1)} %shard_map.85.keep, f32[2048,128]{1,0:T(8,128)S(1)} %shard_map.86.force_in, f32[10,8,256]{2,1,0:T(8,128)S(1)} %collective-permute-done.got_a.col_a, ...), custom_call_target="tpu_custom_call" | custom-call | flops 1048576 | bytes 1048576 | tf_op jit(solution)/shard_map/pallas_call | solution.py:792
  12.9 14.1 %all_to_all.10.got = f32[32,1,128]{2,1,0:T(1,128)S(1)} all-to-all(f32[32,1,128]{2,1,0:T(1,128)S(1)} %get-tuple-element.40), channel_id=1, replica_groups=mesh['slab'=8,'col'=4] {'slab','col'}, dimensions={0} | all-to-all | bytes 32768 | tf_op jit(solution)/shard_map/all_to_all | solution.py:799
  27.0 1.2 %shard_map.88 = (f32[3024,128]{1,0:T(8,128)S(1)}, f32[8,8,256]{2,1,0:T(8,128)S(1)}, f32[8,8,256]{2,1,0:T(8,128)S(1)}) custom-call(f32[32,1,128]{2,1,0:T(1,128)S(1)} %all_to_all.10.got, f32[3536,128]{1,0:T(8,128)S(1)} %get-tuple-element.41.grown), custom_call_target="tpu_custom_call" | custom-call | flops 1048576 | bytes 1048576 | tf_op jit(solution)/shard_map/pallas_call | solution.py:801
  28.2 0.6 %collective-permute-start.8 = (f32[8,8,256]{2,1,0:T(8,128)S(1)}, f32[8,8,256]{2,1,0:T(8,128)S(1)}, u32[]{:S(2)}, u32[]{:S(2)}) collective-permute-start(f32[8,8,256]{2,1,0:T(8,128)S(1)} %get-tuple-element.45), channel_id=1, source_target_pairs={{0,4},{4,0},{8,12},{12,8},{16,20},{20,16},{24,28},{28,24},{1,5},{5... | collective-permute-start | bytes 196616 | tf_op jit(solution)/shard_map/ppermute | solution.py:713
  28.8 0.0 collective-permute-start.9
  28.8 0.1 shard_map.90
  28.9 0.6 %collective-permute-start.6 = (f32[8,8,256]{2,1,0:T(8,128)S(1)}, f32[8,8,256]{2,1,0:T(8,128)S(1)}, u32[]{:S(2)}, u32[]{:S(2)}) collective-permute-start(f32[8,8,256]{2,1,0:T(8,128)S(1)} %get-tuple-element.43), channel_id=1, source_target_pairs={{0,1},{1,0},{2,3},{3,2},{4,5},{5,4},{6,7},{7,6},{8,9},{9,8},{10,11... | collective-permute-start | bytes 196616 | tf_op jit(solution)/shard_map/ppermute | solution.py:701
  29.5 0.3 collective-permute-start.7
  29.8 0.7 %shard_map.89.force_in = f32[2048,128]{1,0:T(8,128)S(1)} custom-call(f32[3024,128]{1,0:T(8,128)S(1)} %get-tuple-element.42.refs_0_.fields.keep), custom_call_target="tpu_custom_call" | custom-call | flops 8388608 | bytes 4194304 | tf_op jit(solution)/shard_map/pallas_call | solution.py:784
  30.5 2.0 %collective-permute-done.8.slab_a = f32[8,8,256]{2,1,0:T(8,128)S(1)} collective-permute-done((f32[8,8,256]{2,1,0:T(8,128)S(1)}, f32[8,8,256]{2,1,0:T(8,128)S(1)}, u32[]{:S(2)}, u32[]{:S(2)}) %collective-permute-start.8) | collective-permute-done | bytes 65568 | tf_op jit(solution)/shard_map/ppermute | solution.py:713
  32.5 0.0 collective-permute-done.9.slab_b
  32.5 0.0 collective-permute-done.6.col_a
  32.5 1.1 %collective-permute-done.7.col_b = f32[8,8,256]{2,1,0:T(8,128)S(1)} collective-permute-done((f32[8,8,256]{2,1,0:T(8,128)S(1)}, f32[8,8,256]{2,1,0:T(8,128)S(1)}, u32[]{:S(2)}, u32[]{:S(2)}) %collective-permute-start.7) | collective-permute-done | bytes 65568 | tf_op jit(solution)/shard_map/ppermute | solution.py:701
  33.6 0.8 %shard_map.91 = (f32[3536,128]{1,0:T(8,128)S(1)}, f32[32,1,128]{2,1,0:T(1,128)S(1)}) custom-call(f32[3024,128]{1,0:T(8,128)S(1)} %get-tuple-element.42.refs_0_.fields.keep, f32[3024,128]{1,0:T(8,128)S(1)} %get-tuple-element.42.refs_0_.fields.keep, f32[2048,128]{1,0:T(8,128)S(1)} %shard_map.89.force_in, f32[8,8,256]{2,1,0:T(8,128)S(1)} %collective-permute-done.6.col_a, ...), custom_call_target="tpu_custom_call" | custom-call | flops 1048576 | bytes 1048576 | tf_op jit(solution)/shard_map/pallas_call | solution.py:792
  34.4 9.6 %all_to_all.11.got = f32[32,1,128]{2,1,0:T(1,128)S(1)} all-to-all(f32[32,1,128]{2,1,0:T(1,128)S(1)} %get-tuple-element.47), channel_id=1, replica_groups=mesh['slab'=8,'col'=4] {'slab','col'}, dimensions={0} | all-to-all | bytes 32768 | tf_op jit(solution)/shard_map/all_to_all | solution.py:799
  44.0 2.2 %shard_map.92 = f32[16,64,256]{2,1,0:T(8,128)} custom-call(f32[32,1,128]{2,1,0:T(1,128)S(1)} %all_to_all.11.got, f32[3536,128]{1,0:T(8,128)S(1)} %get-tuple-element.48.grown), custom_call_target="tpu_custom_call" | custom-call | flops 1048576 | bytes 1048576 | tf_op jit(solution)/shard_map/pallas_call | solution.py:813
  (5 shorter events, 0.0 us)
Async XLA Ops:
  1.8 9.7 %copy-start = (f32[128,256]{1,0:T(8,128)S(1)}, f32[128,256]{1,0:T(8,128)}, u32[]{:S(2)}) copy-start(f32[128,256]{1,0:T(8,128)} %constant.5.clone.height) | copy-start | bytes 393220
  1.8 9.6 %copy-start.1 = (f32[96,48]{1,0:T(8,128)S(1)}, f32[96,48]{1,0:T(8,128)}, u32[]{:S(2)}) copy-start(f32[96,48]{1,0:T(8,128)} %constant.4.clone.weights) | copy-start | bytes 55300
  1.9 4.8 %collective-permute-start = (f32[10,8,256]{2,1,0:T(8,128)S(1)}, f32[10,8,256]{2,1,0:T(8,128)S(1)}, u32[]{:S(2)}, u32[]{:S(2)}) collective-permute-start(f32[10,8,256]{2,1,0:T(8,128)S(1)} %get-tuple-element.29), channel_id=1, source_target_pairs={{0,1},{1,0},{2,3},{3,2},{4,5},{5,4},{6,7},{7,6},{8,9},{9,8},{10,11... | collective-permute-start | bytes 245768 | tf_op jit(solution)/shard_map/ppermute | solution.py:701
  2.4 5.4 %collective-permute-start.1 = (f32[10,8,256]{2,1,0:T(8,128)S(1)}, f32[10,8,256]{2,1,0:T(8,128)S(1)}, u32[]{:S(2)}, u32[]{:S(2)}) collective-permute-start(f32[10,8,256]{2,1,0:T(8,128)S(1)} %get-tuple-element.30), channel_id=1, source_target_pairs={{0,3},{1,2},{2,1},{3,0},{4,7},{5,6},{6,5},{7,4},{8,11},{9,10},{10,... | collective-permute-start | bytes 245768 | tf_op jit(solution)/shard_map/ppermute | solution.py:701
  5.1 5.4 %collective-permute-start.2 = (f32[9,8,256]{2,1,0:T(8,128)S(1)}, f32[9,8,256]{2,1,0:T(8,128)S(1)}, u32[]{:S(2)}, u32[]{:S(2)}) collective-permute-start(f32[9,8,256]{2,1,0:T(8,128)S(1)} %get-tuple-element.36), channel_id=1, source_target_pairs={{0,4},{4,0},{8,12},{12,8},{16,20},{20,16},{24,28},{28,24},{1,5},{5... | collective-permute-start | bytes 221192 | tf_op jit(solution)/shard_map/ppermute | solution.py:713
  6.7 3.9 %collective-permute-start.3 = (f32[9,8,256]{2,1,0:T(8,128)S(1)}, f32[9,8,256]{2,1,0:T(8,128)S(1)}, u32[]{:S(2)}, u32[]{:S(2)}) collective-permute-start(f32[9,8,256]{2,1,0:T(8,128)S(1)} %get-tuple-element.37), channel_id=1, source_target_pairs={{0,1},{1,0},{2,3},{3,2},{4,8},{5,9},{6,10},{7,11},{8,4},{9,5},{10,... | collective-permute-start | bytes 221192 | tf_op jit(solution)/shard_map/ppermute | solution.py:713
  7.8 3.7 %collective-permute-start.4 = (f32[8,256]{1,0:T(8,128)S(1)}, f32[8,256]{1,0:T(8,128)S(1)}, u32[]{:S(2)}, u32[]{:S(2)}) collective-permute-start(f32[8,256]{1,0:T(8,128)S(1)} %get-tuple-element.38), channel_id=1, source_target_pairs={{0,4},{4,0},{8,12},{12,8},{16,20},{20,16},{24,28},{28,24},{1,5},{5... | collective-permute-start | bytes 24584 | tf_op jit(solution)/shard_map/ppermute | solution.py:713
  9.8 1.7 %collective-permute-start.5 = (f32[8,256]{1,0:T(8,128)S(1)}, f32[8,256]{1,0:T(8,128)S(1)}, u32[]{:S(2)}, u32[]{:S(2)}) collective-permute-start(f32[8,256]{1,0:T(8,128)S(1)} %get-tuple-element.39), channel_id=1, source_target_pairs={{0,1},{1,0},{2,3},{3,2},{4,8},{5,9},{6,10},{7,11},{8,4},{9,5},{10,... | collective-permute-start | bytes 24584 | tf_op jit(solution)/shard_map/ppermute | solution.py:713
  28.2 4.3 %collective-permute-start.8 = (f32[8,8,256]{2,1,0:T(8,128)S(1)}, f32[8,8,256]{2,1,0:T(8,128)S(1)}, u32[]{:S(2)}, u32[]{:S(2)}) collective-permute-start(f32[8,8,256]{2,1,0:T(8,128)S(1)} %get-tuple-element.45), channel_id=1, source_target_pairs={{0,4},{4,0},{8,12},{12,8},{16,20},{20,16},{24,28},{28,24},{1,5},{5... | collective-permute-start | bytes 196616 | tf_op jit(solution)/shard_map/ppermute | solution.py:713
  28.8 3.7 %collective-permute-start.9 = (f32[8,8,256]{2,1,0:T(8,128)S(1)}, f32[8,8,256]{2,1,0:T(8,128)S(1)}, u32[]{:S(2)}, u32[]{:S(2)}) collective-permute-start(f32[8,8,256]{2,1,0:T(8,128)S(1)} %get-tuple-element.46), channel_id=1, source_target_pairs={{0,1},{1,0},{2,3},{3,2},{4,8},{5,9},{6,10},{7,11},{8,4},{9,5},{10,... | collective-permute-start | bytes 196616 | tf_op jit(solution)/shard_map/ppermute | solution.py:713
  28.9 3.6 %collective-permute-start.6 = (f32[8,8,256]{2,1,0:T(8,128)S(1)}, f32[8,8,256]{2,1,0:T(8,128)S(1)}, u32[]{:S(2)}, u32[]{:S(2)}) collective-permute-start(f32[8,8,256]{2,1,0:T(8,128)S(1)} %get-tuple-element.43), channel_id=1, source_target_pairs={{0,1},{1,0},{2,3},{3,2},{4,5},{5,4},{6,7},{7,6},{8,9},{9,8},{10,11... | collective-permute-start | bytes 196616 | tf_op jit(solution)/shard_map/ppermute | solution.py:701
  29.5 4.1 %collective-permute-start.7 = (f32[8,8,256]{2,1,0:T(8,128)S(1)}, f32[8,8,256]{2,1,0:T(8,128)S(1)}, u32[]{:S(2)}, u32[]{:S(2)}) collective-permute-start(f32[8,8,256]{2,1,0:T(8,128)S(1)} %get-tuple-element.44), channel_id=1, source_target_pairs={{0,3},{1,2},{2,1},{3,0},{4,7},{5,6},{6,5},{7,4},{8,11},{9,10},{10,... | collective-permute-start | bytes 196616 | tf_op jit(solution)/shard_map/ppermute | solution.py:701

commit v8 on v7

--- a/solution.py
+++ b/solution.py
@@ -335,7 +335,7 @@
 
 def mobility_body(
     cx, cy, slots, slabs, cols, planes, bounds, mask_ref, weights, height, energy, slots_ref,
-    col_a, col_b, slab_a, slab_b, ends_a, ends_b, keep, near,
+    col_a, col_b, slab_a, slab_b, ends_b, ends_a, keep, near,
 ):
     start, end = bounds[0:ROWS, :], bounds[ROWS : 2 * ROWS, :]
     even_s, _ = pair_faces("slab", BELOW, ABOVE)
@@ -776,7 +776,7 @@
         [VMEM] * 13,
         VMEM,
         [pltpu.VMEM((near * ROWS, LANES), jnp.float32)],
-    )(planes, bounds, mask, weights, height, slot_energy, slot_order, col_a, col_b, slab_a, slab_b, ends_a, ends_b)
+    )(planes, bounds, mask, weights, height, slot_energy, slot_order, col_a, col_b, slab_a, slab_b, ends_b, ends_a)
 
     for pair in range(STEPS // 2):
         base = None if pair == 0 else slots * cells

time: 46.4 us -> 45.6 us (0.983)
  blocking collectives: 23.7 us -> 22 us
  starting transfers between devices: 8.27 us -> 9.22 us
    all_to_all x2, blocking collectives: 23.7 us -> 22 us  [per_device(): got = lax.all_to_all(sums, ('slab', 'col'), 0, 0)]
    ppermute x3, starting transfers between devices: 4.25 us -> 5.02 us  [exchange_slabs(): lax.ppermute(first, 'slab', one)]
where the time goes in v8:
time: 45.6 us; the launch traced here: 45.4 us
  blocking collectives  22 us (48%)
  starting transfers between devices  9.22 us (20%)
  Pallas kernels  8.9 us (20%)
  waiting for transfers between devices  5.12 us (11%)
    all_to_all x2, blocking collectives, per_device(): got = lax.all_to_all(sums, ('slab', 'col'), 0, 0)  22 us
    ppermute x3, starting transfers between devices, exchange_slabs(): lax.ppermute(first, 'slab', one)  5.02 us
    ppermute x4, starting transfers between devices, exchange_cols(): return (lax.ppermute(first, 'col', one), lax.ppermute(second, 'col', two))  4.02 us
    ppermute x3, waiting for transfers between devices, exchange_slabs(): lax.ppermute(first, 'slab', one)  2.93 us
    ppermute x4, waiting for transfers between devices, exchange_cols(): return (lax.ppermute(first, 'col', one), lax.ppermute(second, 'col', two))  2.18 us
    pallas_call x1, Pallas kernels, per_device(): call(functools.partial(last_body, cx, cy, slots), f32(slots, cells, cz),...  2.15 us
    pallas_call x1, Pallas kernels, per_device(): call(functools.partial(open_body, cx, cy, slots, slabs, cols), (state, f3...  1.82 us
    pallas_call x2, Pallas kernels, per_device(): call(functools.partial(sums_body, cx, cy, slots, slabs, cols, devices, ba...  1.62 us
  transfers between devices with their start and end apart: 10, of which 4 were waited for; matrix products, arithmetic and copies ran while one was open for 0% of the time, Pallas kernels for 4%

profile of v8, /device:TPU:0, one launch (start us, length us, event | category | flops | bytes accessed | tf_op | source)
XLA Modules:
  0.0 45.4 jit_solution(14897162653372062291)
XLA Ops:
  0.0 1.8 %shard_map.82 = (f32[2048,128]{1,0:T(8,128)S(1)}, f32[128,128]{1,0:T(8,128)S(1)}, f32[8,128]{1,0:T(8,128)S(1)}, f32[128,128]{1,0:T(8,128)S(1)}, s32[16,128]{1,0:...) custom-call(s32[8,4,16]{2,1,0:T(4,128)} %ids_hbm.1, s32[8]{0:T(128)} %rows_hbm.1, ...), custom_call_target="tpu_custom_call" | custom-call | flops 1048576 | bytes 1048576 | tf_op jit(solution)/shard_map/pallas_call | solution.py:730
  1.8 0.0 copy-start
  1.8 0.0 copy-start.1
  1.9 0.5 %collective-permute-start = (f32[10,8,256]{2,1,0:T(8,128)S(1)}, f32[10,8,256]{2,1,0:T(8,128)S(1)}, u32[]{:S(2)}, u32[]{:S(2)}) collective-permute-start(f32[10,8,256]{2,1,0:T(8,128)S(1)} %get-tuple-element.29), channel_id=1, source_target_pairs={{0,1},{1,0},{2,3},{3,2},{4,5},{5,4},{6,7},{7,6},{8,9},{9,8},{10,11... | collective-permute-start | bytes 245768 | tf_op jit(solution)/shard_map/ppermute | solution.py:701
  2.4 2.6 %collective-permute-start.1 = (f32[10,8,256]{2,1,0:T(8,128)S(1)}, f32[10,8,256]{2,1,0:T(8,128)S(1)}, u32[]{:S(2)}, u32[]{:S(2)}) collective-permute-start(f32[10,8,256]{2,1,0:T(8,128)S(1)} %get-tuple-element.30), channel_id=1, source_target_pairs={{0,3},{1,2},{2,1},{3,0},{4,7},{5,6},{6,5},{7,4},{8,11},{9,10},{10,... | collective-permute-start | bytes 245768 | tf_op jit(solution)/shard_map/ppermute | solution.py:701
  5.0 0.1 shard_map.84
  5.1 1.6 %collective-permute-start.2 = (f32[9,8,256]{2,1,0:T(8,128)S(1)}, f32[9,8,256]{2,1,0:T(8,128)S(1)}, u32[]{:S(2)}, u32[]{:S(2)}) collective-permute-start(f32[9,8,256]{2,1,0:T(8,128)S(1)} %get-tuple-element.36), channel_id=1, source_target_pairs={{0,4},{4,0},{8,12},{12,8},{16,20},{20,16},{24,28},{28,24},{1,5},{5... | collective-permute-start | bytes 221192 | tf_op jit(solution)/shard_map/ppermute | solution.py:713
  6.7 0.0 collective-permute-start.3
  6.7 0.0 collective-permute-done.got_a.col_a
  6.7 1.0 %collective-permute-done.1.got_b.col_b = f32[10,8,256]{2,1,0:T(8,128)S(1)} collective-permute-done((f32[10,8,256]{2,1,0:T(8,128)S(1)}, f32[10,8,256]{2,1,0:T(8,128)S(1)}, u32[]{:S(2)}, u32[]{:S(2)}) %collective-permute-start.1) | collective-permute-done | bytes 81952 | tf_op jit(solution)/shard_map/ppermute | solution.py:701
  7.8 0.2 collective-permute-start.4
  7.9 2.8 %collective-permute-start.5 = (f32[8,256]{1,0:T(8,128)S(1)}, f32[8,256]{1,0:T(8,128)S(1)}, u32[]{:S(2)}, u32[]{:S(2)}) collective-permute-start(f32[8,256]{1,0:T(8,128)S(1)} %get-tuple-element.39), channel_id=1, source_target_pairs={{0,4},{4,0},{8,12},{12,8},{16,20},{20,16},{24,28},{28,24},{1,5},{5... | collective-permute-start | bytes 24584 | tf_op jit(solution)/shard_map/ppermute | solution.py:713
  10.8 0.7 %shard_map.86.force_in = f32[2048,128]{1,0:T(8,128)S(1)} custom-call(f32[2048,128]{1,0:T(8,128)S(1)} %get-tuple-element.27.fields.refs_0_, f32[128,128]{1,0:T(8,128)S(1)} %get-tuple-element.34.energy.refs_1_), custom_call_target="tpu_custom_call" | custom-call | flops 8388608 | bytes 4194304 | tf_op jit(solution)/shard_map/pallas_call | solution.py:784
  11.5 0.0 collective-permute-done.2.slab_a
  11.5 0.0 collective-permute-done.3.slab_b
  11.5 0.9 %collective-permute-done.5.ends_a = f32[8,256]{1,0:T(8,128)S(1)} collective-permute-done((f32[8,256]{1,0:T(8,128)S(1)}, f32[8,256]{1,0:T(8,128)S(1)}, u32[]{:S(2)}, u32[]{:S(2)}) %collective-permute-start.5) | collective-permute-done | bytes 8224 | tf_op jit(solution)/shard_map/ppermute | solution.py:713
  12.4 0.5 %shard_map.85.keep = f32[976,128]{1,0:T(8,128)S(1)} custom-call(f32[48,128]{1,0:T(8,128)S(1)} %get-tuple-element.31.planes, s32[16,128]{1,0:T(8,128)S(1)} %get-tuple-element.32.bounds, f32[128,128]{1,0:T(8,128)S(1)} %get-tuple-element.33.mask.mask_ref, f32[96,48]{1,0:T(8,128)S(1)} %copy-done.1, f32[128,256]{1,0:T(8,128)S(1)} %copy-done, ...), custom_call_target="tpu_custom_call" | custom-call | flops 1048576 | bytes 1048576 | tf_op jit(solution)/shard_map/pallas_call | solution.py:773
  12.9 0.8 %shard_map.87 = (f32[3536,128]{1,0:T(8,128)S(1)}, f32[32,1,128]{2,1,0:T(1,128)S(1)}) custom-call(f32[2048,128]{1,0:T(8,128)S(1)} %get-tuple-element.27.fields.refs_0_, f32[976,128]{1,0:T(8,128)S(1)} %shard_map.85.keep, f32[2048,128]{1,0:T(8,128)S(1)} %shard_map.86.force_in, f32[10,8,256]{2,1,0:T(8,128)S(1)} %collective-permute-done.got_a.col_a, ...), custom_call_target="tpu_custom_call" | custom-call | flops 1048576 | bytes 1048576 | tf_op jit(solution)/shard_map/pallas_call | solution.py:792
  13.8 12.4 %all_to_all.10.got = f32[32,1,128]{2,1,0:T(1,128)S(1)} all-to-all(f32[32,1,128]{2,1,0:T(1,128)S(1)} %get-tuple-element.40), channel_id=1, replica_groups=mesh['slab'=8,'col'=4] {'slab','col'}, dimensions={0} | all-to-all | bytes 32768 | tf_op jit(solution)/shard_map/all_to_all | solution.py:799
  26.2 1.2 %shard_map.88 = (f32[3024,128]{1,0:T(8,128)S(1)}, f32[8,8,256]{2,1,0:T(8,128)S(1)}, f32[8,8,256]{2,1,0:T(8,128)S(1)}) custom-call(f32[32,1,128]{2,1,0:T(1,128)S(1)} %all_to_all.10.got, f32[3536,128]{1,0:T(8,128)S(1)} %get-tuple-element.41.grown), custom_call_target="tpu_custom_call" | custom-call | flops 1048576 | bytes 1048576 | tf_op jit(solution)/shard_map/pallas_call | solution.py:801
  27.4 0.6 %collective-permute-start.8 = (f32[8,8,256]{2,1,0:T(8,128)S(1)}, f32[8,8,256]{2,1,0:T(8,128)S(1)}, u32[]{:S(2)}, u32[]{:S(2)}) collective-permute-start(f32[8,8,256]{2,1,0:T(8,128)S(1)} %get-tuple-element.45), channel_id=1, source_target_pairs={{0,4},{4,0},{8,12},{12,8},{16,20},{20,16},{24,28},{28,24},{1,5},{5... | collective-permute-start | bytes 196616 | tf_op jit(solution)/shard_map/ppermute | solution.py:713
  28.0 0.0 collective-permute-start.9
  28.0 0.1 shard_map.90
  28.1 0.6 %collective-permute-start.6 = (f32[8,8,256]{2,1,0:T(8,128)S(1)}, f32[8,8,256]{2,1,0:T(8,128)S(1)}, u32[]{:S(2)}, u32[]{:S(2)}) collective-permute-start(f32[8,8,256]{2,1,0:T(8,128)S(1)} %get-tuple-element.43), channel_id=1, source_target_pairs={{0,1},{1,0},{2,3},{3,2},{4,5},{5,4},{6,7},{7,6},{8,9},{9,8},{10,11... | collective-permute-start | bytes 196616 | tf_op jit(solution)/shard_map/ppermute | solution.py:701
  28.7 0.3 collective-permute-start.7
  29.0 0.7 %shard_map.89.force_in = f32[2048,128]{1,0:T(8,128)S(1)} custom-call(f32[3024,128]{1,0:T(8,128)S(1)} %get-tuple-element.42.refs_0_.fields.keep), custom_call_target="tpu_custom_call" | custom-call | flops 8388608 | bytes 4194304 | tf_op jit(solution)/shard_map/pallas_call | solution.py:784
  29.7 2.0 %collective-permute-done.8.slab_a = f32[8,8,256]{2,1,0:T(8,128)S(1)} collective-permute-done((f32[8,8,256]{2,1,0:T(8,128)S(1)}, f32[8,8,256]{2,1,0:T(8,128)S(1)}, u32[]{:S(2)}, u32[]{:S(2)}) %collective-permute-start.8) | collective-permute-done | bytes 65568 | tf_op jit(solution)/shard_map/ppermute | solution.py:713
  31.7 0.0 collective-permute-done.9.slab_b
  31.7 1.1 %collective-permute-done.7.col_b = f32[8,8,256]{2,1,0:T(8,128)S(1)} collective-permute-done((f32[8,8,256]{2,1,0:T(8,128)S(1)}, f32[8,8,256]{2,1,0:T(8,128)S(1)}, u32[]{:S(2)}, u32[]{:S(2)}) %collective-permute-start.7) | collective-permute-done | bytes 65568 | tf_op jit(solution)/shard_map/ppermute | solution.py:701
  32.8 0.8 %shard_map.91 = (f32[3536,128]{1,0:T(8,128)S(1)}, f32[32,1,128]{2,1,0:T(1,128)S(1)}) custom-call(f32[3024,128]{1,0:T(8,128)S(1)} %get-tuple-element.42.refs_0_.fields.keep, f32[3024,128]{1,0:T(8,128)S(1)} %get-tuple-element.42.refs_0_.fields.keep, f32[2048,128]{1,0:T(8,128)S(1)} %shard_map.89.force_in, f32[8,8,256]{2,1,0:T(8,128)S(1)} %collective-permute-done.6.col_a, ...), custom_call_target="tpu_custom_call" | custom-call | flops 1048576 | bytes 1048576 | tf_op jit(solution)/shard_map/pallas_call | solution.py:792
  33.6 9.6 %all_to_all.11.got = f32[32,1,128]{2,1,0:T(1,128)S(1)} all-to-all(f32[32,1,128]{2,1,0:T(1,128)S(1)} %get-tuple-element.47), channel_id=1, replica_groups=mesh['slab'=8,'col'=4] {'slab','col'}, dimensions={0} | all-to-all | bytes 32768 | tf_op jit(solution)/shard_map/all_to_all | solution.py:799
  43.2 2.2 %shard_map.92 = f32[16,64,256]{2,1,0:T(8,128)} custom-call(f32[32,1,128]{2,1,0:T(1,128)S(1)} %all_to_all.11.got, f32[3536,128]{1,0:T(8,128)S(1)} %get-tuple-element.48.grown), custom_call_target="tpu_custom_call" | custom-call | flops 1048576 | bytes 1048576 | tf_op jit(solution)/shard_map/pallas_call | solution.py:813
  (5 shorter events, 0.0 us)
Async XLA Ops:
  1.8 10.6 %copy-start = (f32[128,256]{1,0:T(8,128)S(1)}, f32[128,256]{1,0:T(8,128)}, u32[]{:S(2)}) copy-start(f32[128,256]{1,0:T(8,128)} %constant.5.clone.height) | copy-start | bytes 393220
  1.8 10.6 %copy-start.1 = (f32[96,48]{1,0:T(8,128)S(1)}, f32[96,48]{1,0:T(8,128)}, u32[]{:S(2)}) copy-start(f32[96,48]{1,0:T(8,128)} %constant.4.clone.weights) | copy-start | bytes 55300
  1.9 4.8 %collective-permute-start = (f32[10,8,256]{2,1,0:T(8,128)S(1)}, f32[10,8,256]{2,1,0:T(8,128)S(1)}, u32[]{:S(2)}, u32[]{:S(2)}) collective-permute-start(f32[10,8,256]{2,1,0:T(8,128)S(1)} %get-tuple-element.29), channel_id=1, source_target_pairs={{0,1},{1,0},{2,3},{3,2},{4,5},{5,4},{6,7},{7,6},{8,9},{9,8},{10,11... | collective-permute-start | bytes 245768 | tf_op jit(solution)/shard_map/ppermute | solution.py:701
  2.4 5.4 %collective-permute-start.1 = (f32[10,8,256]{2,1,0:T(8,128)S(1)}, f32[10,8,256]{2,1,0:T(8,128)S(1)}, u32[]{:S(2)}, u32[]{:S(2)}) collective-permute-start(f32[10,8,256]{2,1,0:T(8,128)S(1)} %get-tuple-element.30), channel_id=1, source_target_pairs={{0,3},{1,2},{2,1},{3,0},{4,7},{5,6},{6,5},{7,4},{8,11},{9,10},{10,... | collective-permute-start | bytes 245768 | tf_op jit(solution)/shard_map/ppermute | solution.py:701
  5.1 6.4 %collective-permute-start.2 = (f32[9,8,256]{2,1,0:T(8,128)S(1)}, f32[9,8,256]{2,1,0:T(8,128)S(1)}, u32[]{:S(2)}, u32[]{:S(2)}) collective-permute-start(f32[9,8,256]{2,1,0:T(8,128)S(1)} %get-tuple-element.36), channel_id=1, source_target_pairs={{0,4},{4,0},{8,12},{12,8},{16,20},{20,16},{24,28},{28,24},{1,5},{5... | collective-permute-start | bytes 221192 | tf_op jit(solution)/shard_map/ppermute | solution.py:713
  6.7 4.8 %collective-permute-start.3 = (f32[9,8,256]{2,1,0:T(8,128)S(1)}, f32[9,8,256]{2,1,0:T(8,128)S(1)}, u32[]{:S(2)}, u32[]{:S(2)}) collective-permute-start(f32[9,8,256]{2,1,0:T(8,128)S(1)} %get-tuple-element.37), channel_id=1, source_target_pairs={{0,1},{1,0},{2,3},{3,2},{4,8},{5,9},{6,10},{7,11},{8,4},{9,5},{10,... | collective-permute-start | bytes 221192 | tf_op jit(solution)/shard_map/ppermute | solution.py:713
  7.8 3.7 %collective-permute-start.4 = (f32[8,256]{1,0:T(8,128)S(1)}, f32[8,256]{1,0:T(8,128)S(1)}, u32[]{:S(2)}, u32[]{:S(2)}) collective-permute-start(f32[8,256]{1,0:T(8,128)S(1)} %get-tuple-element.38), channel_id=1, source_target_pairs={{0,1},{1,0},{2,3},{3,2},{4,8},{5,9},{6,10},{7,11},{8,4},{9,5},{10,... | collective-permute-start | bytes 24584 | tf_op jit(solution)/shard_map/ppermute | solution.py:713
  7.9 4.5 %collective-permute-start.5 = (f32[8,256]{1,0:T(8,128)S(1)}, f32[8,256]{1,0:T(8,128)S(1)}, u32[]{:S(2)}, u32[]{:S(2)}) collective-permute-start(f32[8,256]{1,0:T(8,128)S(1)} %get-tuple-element.39), channel_id=1, source_target_pairs={{0,4},{4,0},{8,12},{12,8},{16,20},{20,16},{24,28},{28,24},{1,5},{5... | collective-permute-start | bytes 24584 | tf_op jit(solution)/shard_map/ppermute | solution.py:713
  27.4 4.3 %collective-permute-start.8 = (f32[8,8,256]{2,1,0:T(8,128)S(1)}, f32[8,8,256]{2,1,0:T(8,128)S(1)}, u32[]{:S(2)}, u32[]{:S(2)}) collective-permute-start(f32[8,8,256]{2,1,0:T(8,128)S(1)} %get-tuple-element.45), channel_id=1, source_target_pairs={{0,4},{4,0},{8,12},{12,8},{16,20},{20,16},{24,28},{28,24},{1,5},{5... | collective-permute-start | bytes 196616 | tf_op jit(solution)/shard_map/ppermute | solution.py:713
  28.0 3.7 %collective-permute-start.9 = (f32[8,8,256]{2,1,0:T(8,128)S(1)}, f32[8,8,256]{2,1,0:T(8,128)S(1)}, u32[]{:S(2)}, u32[]{:S(2)}) collective-permute-start(f32[8,8,256]{2,1,0:T(8,128)S(1)} %get-tuple-element.46), channel_id=1, source_target_pairs={{0,1},{1,0},{2,3},{3,2},{4,8},{5,9},{6,10},{7,11},{8,4},{9,5},{10,... | collective-permute-start | bytes 196616 | tf_op jit(solution)/shard_map/ppermute | solution.py:713
  28.1 3.6 %collective-permute-start.6 = (f32[8,8,256]{2,1,0:T(8,128)S(1)}, f32[8,8,256]{2,1,0:T(8,128)S(1)}, u32[]{:S(2)}, u32[]{:S(2)}) collective-permute-start(f32[8,8,256]{2,1,0:T(8,128)S(1)} %get-tuple-element.43), channel_id=1, source_target_pairs={{0,1},{1,0},{2,3},{3,2},{4,5},{5,4},{6,7},{7,6},{8,9},{9,8},{10,11... | collective-permute-start | bytes 196616 | tf_op jit(solution)/shard_map/ppermute | solution.py:701
  28.7 4.1 %collective-permute-start.7 = (f32[8,8,256]{2,1,0:T(8,128)S(1)}, f32[8,8,256]{2,1,0:T(8,128)S(1)}, u32[]{:S(2)}, u32[]{:S(2)}) collective-permute-start(f32[8,8,256]{2,1,0:T(8,128)S(1)} %get-tuple-element.44), channel_id=1, source_target_pairs={{0,3},{1,2},{2,1},{3,0},{4,7},{5,6},{6,5},{7,4},{8,11},{9,10},{10,... | collective-permute-start | bytes 196616 | tf_op jit(solution)/shard_map/ppermute | solution.py:701

commit v9 on v8

--- a/solution.py
+++ b/solution.py
@@ -333,9 +333,17 @@
     return out
 
 
+def parts_of(value):
+    parts = []
+    for _ in range(3):
+        parts.append(value.astype(jnp.bfloat16))
+        value = value - parts[-1].astype(jnp.float32)
+    return parts
+
+
 def mobility_body(
     cx, cy, slots, slabs, cols, planes, bounds, mask_ref, weights, height, energy, slots_ref,
-    col_a, col_b, slab_a, slab_b, ends_b, ends_a, keep, near,
+    ends_b, ends_a, col_a, col_b, slab_a, slab_b, keep, near,
 ):
     start, end = bounds[0:ROWS, :], bounds[ROWS : 2 * ROWS, :]
     even_s, _ = pair_faces("slab", BELOW, ABOVE)
@@ -349,8 +357,9 @@
         lower = jnp.where(p == start - 2, below[:, :LANES], below[:, LANES:])
         upper = jnp.where(p == end, above[:, :LANES], above[:, LANES:])
         near[i * ROWS : (i + 1) * ROWS, :] = jnp.where(p < start, lower, jnp.where(p < end, own, upper))
-    flat = jnp.dot(weights[...], near[...], precision=HIGHEST, preferred_element_type=jnp.float32)
-    profile = jnp.dot(flat, height[...], precision=HIGHEST, preferred_element_type=jnp.float32)
+    dot = functools.partial(jnp.dot, preferred_element_type=jnp.float32)
+    flat = sum(dot(weights[...], part) for part in parts_of(near[...]))
+    profile = sum(dot(part, height[...]) for part in parts_of(flat))
     mobility = jnp.exp(2.0 * (profile - 1.0)) * TIME_STEP
     cells = cx * cy
     kept = Kept(keep, 0, cx, cy, slots)
@@ -767,8 +776,8 @@
         (VMEM,) * 3,
     )(planes, col_a, col_b)
     ends_b, ends_a = exchange_slabs(ends_a, ends_b)
-    weights = jnp.asarray(plane_weights(cx, cy))
-    height = jnp.asarray(height_weights(cz, coarse_z))
+    weights = jnp.asarray(plane_weights(cx, cy), jnp.bfloat16)
+    height = jnp.asarray(height_weights(cz, coarse_z), jnp.bfloat16)
     count = Kept.rows(cells, slots)
     keep = call(
         functools.partial(mobility_body, cx, cy, slots, slabs, cols),
@@ -776,7 +785,7 @@
         [VMEM] * 13,
         VMEM,
         [pltpu.VMEM((near * ROWS, LANES), jnp.float32)],
-    )(planes, bounds, mask, weights, height, slot_energy, slot_order, col_a, col_b, slab_a, slab_b, ends_b, ends_a)
+    )(planes, bounds, mask, weights, height, slot_energy, slot_order, ends_b, ends_a, col_a, col_b, slab_a, slab_b)
 
     for pair in range(STEPS // 2):
         base = None if pair == 0 else slots * cells

time: 45.6 us -> 45.5 us (level)
  no operation moved by 1% of the time
where the time goes in v9:
time: 45.5 us; the launch traced here: 45.3 us
  blocking collectives  22 us (48%)
  starting transfers between devices  9.22 us (20%)
  Pallas kernels  8.82 us (19%)
  waiting for transfers between devices  5.11 us (11%)
    all_to_all x2, blocking collectives, per_device(): got = lax.all_to_all(sums, ('slab', 'col'), 0, 0)  22 us
    ppermute x3, starting transfers between devices, exchange_slabs(): lax.ppermute(first, 'slab', one)  5.02 us
    ppermute x4, starting transfers between devices, exchange_cols(): return (lax.ppermute(first, 'col', one), lax.ppermute(second, 'col', two))  4.02 us
    ppermute x3, waiting for transfers between devices, exchange_slabs(): lax.ppermute(first, 'slab', one)  2.93 us
    ppermute x4, waiting for transfers between devices, exchange_cols(): return (lax.ppermute(first, 'col', one), lax.ppermute(second, 'col', two))  2.18 us
    pallas_call x1, Pallas kernels, per_device(): call(functools.partial(last_body, cx, cy, slots), f32(slots, cells, cz),...  2.15 us
    pallas_call x1, Pallas kernels, per_device(): call(functools.partial(open_body, cx, cy, slots, slabs, cols), (state, f3...  1.82 us
    pallas_call x2, Pallas kernels, per_device(): call(functools.partial(sums_body, cx, cy, slots, slabs, cols, devices, ba...  1.62 us
  transfers between devices with their start and end apart: 10, of which 4 were waited for; matrix products, arithmetic and copies ran while one was open for 0% of the time, Pallas kernels for 4%

profile of v9, /device:TPU:0, one launch (start us, length us, event | category | flops | bytes accessed | tf_op | source)
XLA Modules:
  0.0 45.3 jit_solution(16621279830579815031)
XLA Ops:
  0.0 1.8 %shard_map.82 = (f32[2048,128]{1,0:T(8,128)S(1)}, f32[128,128]{1,0:T(8,128)S(1)}, f32[8,128]{1,0:T(8,128)S(1)}, f32[128,128]{1,0:T(8,128)S(1)}, s32[16,128]{1,0:...) custom-call(s32[8,4,16]{2,1,0:T(4,128)} %ids_hbm.1, s32[8]{0:T(128)} %rows_hbm.1, ...), custom_call_target="tpu_custom_call" | custom-call | flops 1048576 | bytes 1048576 | tf_op jit(solution)/shard_map/pallas_call | solution.py:739
  1.8 0.0 copy-start
  1.8 0.0 copy-start.1
  1.8 0.5 %collective-permute-start = (f32[10,8,256]{2,1,0:T(8,128)S(1)}, f32[10,8,256]{2,1,0:T(8,128)S(1)}, u32[]{:S(2)}, u32[]{:S(2)}) collective-permute-start(f32[10,8,256]{2,1,0:T(8,128)S(1)} %get-tuple-element.29), channel_id=1, source_target_pairs={{0,1},{1,0},{2,3},{3,2},{4,5},{5,4},{6,7},{7,6},{8,9},{9,8},{10,11... | collective-permute-start | bytes 245768 | tf_op jit(solution)/shard_map/ppermute | solution.py:710
  2.4 2.6 %collective-permute-start.1 = (f32[10,8,256]{2,1,0:T(8,128)S(1)}, f32[10,8,256]{2,1,0:T(8,128)S(1)}, u32[]{:S(2)}, u32[]{:S(2)}) collective-permute-start(f32[10,8,256]{2,1,0:T(8,128)S(1)} %get-tuple-element.30), channel_id=1, source_target_pairs={{0,3},{1,2},{2,1},{3,0},{4,7},{5,6},{6,5},{7,4},{8,11},{9,10},{10,... | collective-permute-start | bytes 245768 | tf_op jit(solution)/shard_map/ppermute | solution.py:710
  5.0 0.1 shard_map.84
  5.1 1.6 %collective-permute-start.4 = (f32[9,8,256]{2,1,0:T(8,128)S(1)}, f32[9,8,256]{2,1,0:T(8,128)S(1)}, u32[]{:S(2)}, u32[]{:S(2)}) collective-permute-start(f32[9,8,256]{2,1,0:T(8,128)S(1)} %get-tuple-element.38), channel_id=1, source_target_pairs={{0,4},{4,0},{8,12},{12,8},{16,20},{20,16},{24,28},{28,24},{1,5},{5... | collective-permute-start | bytes 221192 | tf_op jit(solution)/shard_map/ppermute | solution.py:722
  6.7 0.0 collective-permute-start.5
  6.7 0.0 collective-permute-done.got_a.col_a
  6.7 1.1 %collective-permute-done.1.got_b.col_b = f32[10,8,256]{2,1,0:T(8,128)S(1)} collective-permute-done((f32[10,8,256]{2,1,0:T(8,128)S(1)}, f32[10,8,256]{2,1,0:T(8,128)S(1)}, u32[]{:S(2)}, u32[]{:S(2)}) %collective-permute-start.1) | collective-permute-done | bytes 81952 | tf_op jit(solution)/shard_map/ppermute | solution.py:710
  7.8 0.2 collective-permute-start.2
  7.9 2.8 %collective-permute-start.3 = (f32[8,256]{1,0:T(8,128)S(1)}, f32[8,256]{1,0:T(8,128)S(1)}, u32[]{:S(2)}, u32[]{:S(2)}) collective-permute-start(f32[8,256]{1,0:T(8,128)S(1)} %get-tuple-element.37), channel_id=1, source_target_pairs={{0,4},{4,0},{8,12},{12,8},{16,20},{20,16},{24,28},{28,24},{1,5},{5... | collective-permute-start | bytes 24584 | tf_op jit(solution)/shard_map/ppermute | solution.py:722
  10.8 0.7 %shard_map.86.force_in = f32[2048,128]{1,0:T(8,128)S(1)} custom-call(f32[2048,128]{1,0:T(8,128)S(1)} %get-tuple-element.27.fields.refs_0_, f32[128,128]{1,0:T(8,128)S(1)} %get-tuple-element.34.energy.refs_1_), custom_call_target="tpu_custom_call" | custom-call | flops 8388608 | bytes 4194304 | tf_op jit(solution)/shard_map/pallas_call | solution.py:793
  11.5 0.0 collective-permute-done.5.slab_b
  11.5 0.0 collective-permute-done.2.ends_b
  11.5 0.9 %collective-permute-done.3.ends_a = f32[8,256]{1,0:T(8,128)S(1)} collective-permute-done((f32[8,256]{1,0:T(8,128)S(1)}, f32[8,256]{1,0:T(8,128)S(1)}, u32[]{:S(2)}, u32[]{:S(2)}) %collective-permute-start.3) | collective-permute-done | bytes 8224 | tf_op jit(solution)/shard_map/ppermute | solution.py:722
  12.4 0.4 shard_map.85.keep
  12.9 0.8 %shard_map.87 = (f32[3536,128]{1,0:T(8,128)S(1)}, f32[32,1,128]{2,1,0:T(1,128)S(1)}) custom-call(f32[2048,128]{1,0:T(8,128)S(1)} %get-tuple-element.27.fields.refs_0_, f32[976,128]{1,0:T(8,128)S(1)} %shard_map.85.keep, f32[2048,128]{1,0:T(8,128)S(1)} %shard_map.86.force_in, f32[10,8,256]{2,1,0:T(8,128)S(1)} %collective-permute-done.got_a.col_a, ...), custom_call_target="tpu_custom_call" | custom-call | flops 1048576 | bytes 1048576 | tf_op jit(solution)/shard_map/pallas_call | solution.py:801
  13.7 12.4 %all_to_all.10.got = f32[32,1,128]{2,1,0:T(1,128)S(1)} all-to-all(f32[32,1,128]{2,1,0:T(1,128)S(1)} %get-tuple-element.40), channel_id=1, replica_groups=mesh['slab'=8,'col'=4] {'slab','col'}, dimensions={0} | all-to-all | bytes 32768 | tf_op jit(solution)/shard_map/all_to_all | solution.py:808
  26.1 1.2 %shard_map.88 = (f32[3024,128]{1,0:T(8,128)S(1)}, f32[8,8,256]{2,1,0:T(8,128)S(1)}, f32[8,8,256]{2,1,0:T(8,128)S(1)}) custom-call(f32[32,1,128]{2,1,0:T(1,128)S(1)} %all_to_all.10.got, f32[3536,128]{1,0:T(8,128)S(1)} %get-tuple-element.41.grown), custom_call_target="tpu_custom_call" | custom-call | flops 1048576 | bytes 1048576 | tf_op jit(solution)/shard_map/pallas_call | solution.py:810
  27.3 0.6 %collective-permute-start.8 = (f32[8,8,256]{2,1,0:T(8,128)S(1)}, f32[8,8,256]{2,1,0:T(8,128)S(1)}, u32[]{:S(2)}, u32[]{:S(2)}) collective-permute-start(f32[8,8,256]{2,1,0:T(8,128)S(1)} %get-tuple-element.45), channel_id=1, source_target_pairs={{0,4},{4,0},{8,12},{12,8},{16,20},{20,16},{24,28},{28,24},{1,5},{5... | collective-permute-start | bytes 196616 | tf_op jit(solution)/shard_map/ppermute | solution.py:722
  27.9 0.1 shard_map.90
  28.1 0.6 %collective-permute-start.6 = (f32[8,8,256]{2,1,0:T(8,128)S(1)}, f32[8,8,256]{2,1,0:T(8,128)S(1)}, u32[]{:S(2)}, u32[]{:S(2)}) collective-permute-start(f32[8,8,256]{2,1,0:T(8,128)S(1)} %get-tuple-element.43), channel_id=1, source_target_pairs={{0,1},{1,0},{2,3},{3,2},{4,5},{5,4},{6,7},{7,6},{8,9},{9,8},{10,11... | collective-permute-start | bytes 196616 | tf_op jit(solution)/shard_map/ppermute | solution.py:710
  28.6 0.3 collective-permute-start.7
  28.9 0.7 %shard_map.89.force_in = f32[2048,128]{1,0:T(8,128)S(1)} custom-call(f32[3024,128]{1,0:T(8,128)S(1)} %get-tuple-element.42.refs_0_.fields.keep), custom_call_target="tpu_custom_call" | custom-call | flops 8388608 | bytes 4194304 | tf_op jit(solution)/shard_map/pallas_call | solution.py:793
  29.6 2.0 %collective-permute-done.8.slab_a = f32[8,8,256]{2,1,0:T(8,128)S(1)} collective-permute-done((f32[8,8,256]{2,1,0:T(8,128)S(1)}, f32[8,8,256]{2,1,0:T(8,128)S(1)}, u32[]{:S(2)}, u32[]{:S(2)}) %collective-permute-start.8) | collective-permute-done | bytes 65568 | tf_op jit(solution)/shard_map/ppermute | solution.py:722
  31.6 0.0 collective-permute-done.9.slab_b
  31.6 0.0 collective-permute-done.6.col_a
  31.6 1.1 %collective-permute-done.7.col_b = f32[8,8,256]{2,1,0:T(8,128)S(1)} collective-permute-done((f32[8,8,256]{2,1,0:T(8,128)S(1)}, f32[8,8,256]{2,1,0:T(8,128)S(1)}, u32[]{:S(2)}, u32[]{:S(2)}) %collective-permute-start.7) | collective-permute-done | bytes 65568 | tf_op jit(solution)/shard_map/ppermute | solution.py:710
  32.8 0.8 %shard_map.91 = (f32[3536,128]{1,0:T(8,128)S(1)}, f32[32,1,128]{2,1,0:T(1,128)S(1)}) custom-call(f32[3024,128]{1,0:T(8,128)S(1)} %get-tuple-element.42.refs_0_.fields.keep, f32[3024,128]{1,0:T(8,128)S(1)} %get-tuple-element.42.refs_0_.fields.keep, f32[2048,128]{1,0:T(8,128)S(1)} %shard_map.89.force_in, f32[8,8,256]{2,1,0:T(8,128)S(1)} %collective-permute-done.6.col_a, ...), custom_call_target="tpu_custom_call" | custom-call | flops 1048576 | bytes 1048576 | tf_op jit(solution)/shard_map/pallas_call | solution.py:801
  33.6 9.6 %all_to_all.11.got = f32[32,1,128]{2,1,0:T(1,128)S(1)} all-to-all(f32[32,1,128]{2,1,0:T(1,128)S(1)} %get-tuple-element.47), channel_id=1, replica_groups=mesh['slab'=8,'col'=4] {'slab','col'}, dimensions={0} | all-to-all | bytes 32768 | tf_op jit(solution)/shard_map/all_to_all | solution.py:808
  43.1 2.2 %shard_map.92 = f32[16,64,256]{2,1,0:T(8,128)} custom-call(f32[32,1,128]{2,1,0:T(1,128)S(1)} %all_to_all.11.got, f32[3536,128]{1,0:T(8,128)S(1)} %get-tuple-element.48.grown), custom_call_target="tpu_custom_call" | custom-call | flops 1048576 | bytes 1048576 | tf_op jit(solution)/shard_map/pallas_call | solution.py:822
  (5 shorter events, 0.0 us)
Async XLA Ops:
  1.8 10.6 %copy-start = (bf16[128,256]{1,0:T(8,128)(2,1)S(1)}, bf16[128,256]{1,0:T(8,128)(2,1)}, u32[]{:S(2)}) copy-start(bf16[128,256]{1,0:T(8,128)(2,1)} %constant.5.clone.height) | copy-start | bytes 196612
  1.8 10.6 %copy-start.1 = (bf16[96,48]{1,0:T(8,128)(2,1)S(1)}, bf16[96,48]{1,0:T(8,128)(2,1)}, u32[]{:S(2)}) copy-start(bf16[96,48]{1,0:T(8,128)(2,1)} %constant.4.clone.weights) | copy-start | bytes 27652
  1.8 4.8 %collective-permute-start = (f32[10,8,256]{2,1,0:T(8,128)S(1)}, f32[10,8,256]{2,1,0:T(8,128)S(1)}, u32[]{:S(2)}, u32[]{:S(2)}) collective-permute-start(f32[10,8,256]{2,1,0:T(8,128)S(1)} %get-tuple-element.29), channel_id=1, source_target_pairs={{0,1},{1,0},{2,3},{3,2},{4,5},{5,4},{6,7},{7,6},{8,9},{9,8},{10,11... | collective-permute-start | bytes 245768 | tf_op jit(solution)/shard_map/ppermute | solution.py:710
  2.4 5.4 %collective-permute-start.1 = (f32[10,8,256]{2,1,0:T(8,128)S(1)}, f32[10,8,256]{2,1,0:T(8,128)S(1)}, u32[]{:S(2)}, u32[]{:S(2)}) collective-permute-start(f32[10,8,256]{2,1,0:T(8,128)S(1)} %get-tuple-element.30), channel_id=1, source_target_pairs={{0,3},{1,2},{2,1},{3,0},{4,7},{5,6},{6,5},{7,4},{8,11},{9,10},{10,... | collective-permute-start | bytes 245768 | tf_op jit(solution)/shard_map/ppermute | solution.py:710
  5.1 6.4 %collective-permute-start.4 = (f32[9,8,256]{2,1,0:T(8,128)S(1)}, f32[9,8,256]{2,1,0:T(8,128)S(1)}, u32[]{:S(2)}, u32[]{:S(2)}) collective-permute-start(f32[9,8,256]{2,1,0:T(8,128)S(1)} %get-tuple-element.38), channel_id=1, source_target_pairs={{0,4},{4,0},{8,12},{12,8},{16,20},{20,16},{24,28},{28,24},{1,5},{5... | collective-permute-start | bytes 221192 | tf_op jit(solution)/shard_map/ppermute | solution.py:722
  6.7 4.8 %collective-permute-start.5 = (f32[9,8,256]{2,1,0:T(8,128)S(1)}, f32[9,8,256]{2,1,0:T(8,128)S(1)}, u32[]{:S(2)}, u32[]{:S(2)}) collective-permute-start(f32[9,8,256]{2,1,0:T(8,128)S(1)} %get-tuple-element.39), channel_id=1, source_target_pairs={{0,1},{1,0},{2,3},{3,2},{4,8},{5,9},{6,10},{7,11},{8,4},{9,5},{10,... | collective-permute-start | bytes 221192 | tf_op jit(solution)/shard_map/ppermute | solution.py:722
  7.8 3.7 %collective-permute-start.2 = (f32[8,256]{1,0:T(8,128)S(1)}, f32[8,256]{1,0:T(8,128)S(1)}, u32[]{:S(2)}, u32[]{:S(2)}) collective-permute-start(f32[8,256]{1,0:T(8,128)S(1)} %get-tuple-element.36), channel_id=1, source_target_pairs={{0,1},{1,0},{2,3},{3,2},{4,8},{5,9},{6,10},{7,11},{8,4},{9,5},{10,... | collective-permute-start | bytes 24584 | tf_op jit(solution)/shard_map/ppermute | solution.py:722
  7.9 4.5 %collective-permute-start.3 = (f32[8,256]{1,0:T(8,128)S(1)}, f32[8,256]{1,0:T(8,128)S(1)}, u32[]{:S(2)}, u32[]{:S(2)}) collective-permute-start(f32[8,256]{1,0:T(8,128)S(1)} %get-tuple-element.37), channel_id=1, source_target_pairs={{0,4},{4,0},{8,12},{12,8},{16,20},{20,16},{24,28},{28,24},{1,5},{5... | collective-permute-start | bytes 24584 | tf_op jit(solution)/shard_map/ppermute | solution.py:722
  27.3 4.3 %collective-permute-start.8 = (f32[8,8,256]{2,1,0:T(8,128)S(1)}, f32[8,8,256]{2,1,0:T(8,128)S(1)}, u32[]{:S(2)}, u32[]{:S(2)}) collective-permute-start(f32[8,8,256]{2,1,0:T(8,128)S(1)} %get-tuple-element.45), channel_id=1, source_target_pairs={{0,4},{4,0},{8,12},{12,8},{16,20},{20,16},{24,28},{28,24},{1,5},{5... | collective-permute-start | bytes 196616 | tf_op jit(solution)/shard_map/ppermute | solution.py:722
  27.9 3.7 %collective-permute-start.9 = (f32[8,8,256]{2,1,0:T(8,128)S(1)}, f32[8,8,256]{2,1,0:T(8,128)S(1)}, u32[]{:S(2)}, u32[]{:S(2)}) collective-permute-start(f32[8,8,256]{2,1,0:T(8,128)S(1)} %get-tuple-element.46), channel_id=1, source_target_pairs={{0,1},{1,0},{2,3},{3,2},{4,8},{5,9},{6,10},{7,11},{8,4},{9,5},{10,... | collective-permute-start | bytes 196616 | tf_op jit(solution)/shard_map/ppermute | solution.py:722
  28.1 3.6 %collective-permute-start.6 = (f32[8,8,256]{2,1,0:T(8,128)S(1)}, f32[8,8,256]{2,1,0:T(8,128)S(1)}, u32[]{:S(2)}, u32[]{:S(2)}) collective-permute-start(f32[8,8,256]{2,1,0:T(8,128)S(1)} %get-tuple-element.43), channel_id=1, source_target_pairs={{0,1},{1,0},{2,3},{3,2},{4,5},{5,4},{6,7},{7,6},{8,9},{9,8},{10,11... | collective-permute-start | bytes 196616 | tf_op jit(solution)/shard_map/ppermute | solution.py:710
  28.6 4.1 %collective-permute-start.7 = (f32[8,8,256]{2,1,0:T(8,128)S(1)}, f32[8,8,256]{2,1,0:T(8,128)S(1)}, u32[]{:S(2)}, u32[]{:S(2)}) collective-permute-start(f32[8,8,256]{2,1,0:T(8,128)S(1)} %get-tuple-element.44), channel_id=1, source_target_pairs={{0,3},{1,2},{2,1},{3,0},{4,7},{5,6},{6,5},{7,4},{8,11},{9,10},{10,... | collective-permute-start | bytes 196616 | tf_op jit(solution)/shard_map/ppermute | solution.py:710

commit v10 on v9

--- a/solution.py
+++ b/solution.py
@@ -76,7 +76,16 @@
         ranks.append(jnp.sum(jnp.where(row < own, shared, zero), axis=1, keepdims=True))
     free = one - (matches[0] + matches[1] + matches[2] + matches[3])
     lanef = lane.astype(jnp.float32)
-    free_row = jnp.sum(jnp.where(sub == lane, free, zero), axis=0, keepdims=True)
+    own_row = ids_ref[s, pl.ds(c, 1), :]
+    own_row = jnp.concatenate([own_row, jnp.full((1, LANES - slots), -2, jnp.int32)], axis=1)
+    own_row = jnp.broadcast_to(own_row, (slots, LANES))
+    held = jnp.zeros((slots, LANES), jnp.float32)
+    for k, (ns, nc) in enumerate(beside(slabs, cols)):
+        theirs = jnp.zeros((slots, LANES), jnp.int32)
+        for r in range(slots):
+            theirs = jnp.where(sub == r, ids_smem[ns, nc, r], theirs)
+        held = jnp.where((theirs == own_row) & have[k], one, held)
+    free_row = one - jnp.max(held, axis=0, keepdims=True)
     free_rank = jnp.sum(jnp.where(lane < sub, free_row, zero), axis=1, keepdims=True)
     place = jnp.zeros((slots, LANES), jnp.float32)
     skipped = jnp.int32(0)

time: 45.5 us -> 45.5 us (level)
  no operation moved by 1% of the time
where the time goes in v10:
time: 45.5 us; the launch traced here: 45.2 us
  blocking collectives  22 us (48%)
  starting transfers between devices  9.22 us (20%)
  Pallas kernels  8.77 us (19%)
  waiting for transfers between devices  5.11 us (11%)
    all_to_all x2, blocking collectives, per_device(): got = lax.all_to_all(sums, ('slab', 'col'), 0, 0)  22 us
    ppermute x3, starting transfers between devices, exchange_slabs(): lax.ppermute(first, 'slab', one)  5.02 us
    ppermute x4, starting transfers between devices, exchange_cols(): return (lax.ppermute(first, 'col', one), lax.ppermute(second, 'col', two))  4.02 us
    ppermute x3, waiting for transfers between devices, exchange_slabs(): lax.ppermute(first, 'slab', one)  2.93 us
    ppermute x4, waiting for transfers between devices, exchange_cols(): return (lax.ppermute(first, 'col', one), lax.ppermute(second, 'col', two))  2.18 us
    pallas_call x1, Pallas kernels, per_device(): call(functools.partial(last_body, cx, cy, slots), f32(slots, cells, cz),...  2.15 us
    pallas_call x1, Pallas kernels, per_device(): call(functools.partial(open_body, cx, cy, slots, slabs, cols), (state, f3...  1.77 us
    pallas_call x2, Pallas kernels, per_device(): call(functools.partial(sums_body, cx, cy, slots, slabs, cols, devices, ba...  1.62 us
  transfers between devices with their start and end apart: 10, of which 4 were waited for; matrix products, arithmetic and copies ran while one was open for 0% of the time, Pallas kernels for 4%

profile of v10, /device:TPU:0, one launch (start us, length us, event | category | flops | bytes accessed | tf_op | source)
XLA Modules:
  0.0 45.2 jit_solution(5717744341404905494)
XLA Ops:
  0.0 1.8 %shard_map.82 = (f32[2048,128]{1,0:T(8,128)S(1)}, f32[128,128]{1,0:T(8,128)S(1)}, f32[8,128]{1,0:T(8,128)S(1)}, f32[128,128]{1,0:T(8,128)S(1)}, s32[16,128]{1,0:...) custom-call(s32[8,4,16]{2,1,0:T(4,128)} %ids_hbm.1, s32[8]{0:T(128)} %rows_hbm.1, ...), custom_call_target="tpu_custom_call" | custom-call | flops 1048576 | bytes 1048576 | tf_op jit(solution)/shard_map/pallas_call | solution.py:748
  1.8 0.0 copy-start
  1.8 0.0 copy-start.1
  1.8 0.5 %collective-permute-start = (f32[10,8,256]{2,1,0:T(8,128)S(1)}, f32[10,8,256]{2,1,0:T(8,128)S(1)}, u32[]{:S(2)}, u32[]{:S(2)}) collective-permute-start(f32[10,8,256]{2,1,0:T(8,128)S(1)} %get-tuple-element.29), channel_id=1, source_target_pairs={{0,1},{1,0},{2,3},{3,2},{4,5},{5,4},{6,7},{7,6},{8,9},{9,8},{10,11... | collective-permute-start | bytes 245768 | tf_op jit(solution)/shard_map/ppermute | solution.py:719
  2.3 2.6 %collective-permute-start.1 = (f32[10,8,256]{2,1,0:T(8,128)S(1)}, f32[10,8,256]{2,1,0:T(8,128)S(1)}, u32[]{:S(2)}, u32[]{:S(2)}) collective-permute-start(f32[10,8,256]{2,1,0:T(8,128)S(1)} %get-tuple-element.30), channel_id=1, source_target_pairs={{0,3},{1,2},{2,1},{3,0},{4,7},{5,6},{6,5},{7,4},{8,11},{9,10},{10,... | collective-permute-start | bytes 245768 | tf_op jit(solution)/shard_map/ppermute | solution.py:719
  5.0 0.1 shard_map.84
  5.1 1.6 %collective-permute-start.4 = (f32[9,8,256]{2,1,0:T(8,128)S(1)}, f32[9,8,256]{2,1,0:T(8,128)S(1)}, u32[]{:S(2)}, u32[]{:S(2)}) collective-permute-start(f32[9,8,256]{2,1,0:T(8,128)S(1)} %get-tuple-element.38), channel_id=1, source_target_pairs={{0,4},{4,0},{8,12},{12,8},{16,20},{20,16},{24,28},{28,24},{1,5},{5... | collective-permute-start | bytes 221192 | tf_op jit(solution)/shard_map/ppermute | solution.py:731
  6.6 0.0 collective-permute-start.5
  6.6 0.0 collective-permute-done.got_a.col_a
  6.6 1.1 %collective-permute-done.1.got_b.col_b = f32[10,8,256]{2,1,0:T(8,128)S(1)} collective-permute-done((f32[10,8,256]{2,1,0:T(8,128)S(1)}, f32[10,8,256]{2,1,0:T(8,128)S(1)}, u32[]{:S(2)}, u32[]{:S(2)}) %collective-permute-start.1) | collective-permute-done | bytes 81952 | tf_op jit(solution)/shard_map/ppermute | solution.py:719
  7.7 0.2 collective-permute-start.2
  7.9 2.8 %collective-permute-start.3 = (f32[8,256]{1,0:T(8,128)S(1)}, f32[8,256]{1,0:T(8,128)S(1)}, u32[]{:S(2)}, u32[]{:S(2)}) collective-permute-start(f32[8,256]{1,0:T(8,128)S(1)} %get-tuple-element.37), channel_id=1, source_target_pairs={{0,4},{4,0},{8,12},{12,8},{16,20},{20,16},{24,28},{28,24},{1,5},{5... | collective-permute-start | bytes 24584 | tf_op jit(solution)/shard_map/ppermute | solution.py:731
  10.7 0.7 %shard_map.86.force_in = f32[2048,128]{1,0:T(8,128)S(1)} custom-call(f32[2048,128]{1,0:T(8,128)S(1)} %get-tuple-element.27.fields.refs_0_, f32[128,128]{1,0:T(8,128)S(1)} %get-tuple-element.34.energy.refs_1_), custom_call_target="tpu_custom_call" | custom-call | flops 8388608 | bytes 4194304 | tf_op jit(solution)/shard_map/pallas_call | solution.py:802
  11.4 0.0 collective-permute-done.4.slab_a
  11.5 0.0 collective-permute-done.2.ends_b
  11.5 0.9 %collective-permute-done.3.ends_a = f32[8,256]{1,0:T(8,128)S(1)} collective-permute-done((f32[8,256]{1,0:T(8,128)S(1)}, f32[8,256]{1,0:T(8,128)S(1)}, u32[]{:S(2)}, u32[]{:S(2)}) %collective-permute-start.3) | collective-permute-done | bytes 8224 | tf_op jit(solution)/shard_map/ppermute | solution.py:731
  12.4 0.4 shard_map.85.keep
  12.8 0.8 %shard_map.87 = (f32[3536,128]{1,0:T(8,128)S(1)}, f32[32,1,128]{2,1,0:T(1,128)S(1)}) custom-call(f32[2048,128]{1,0:T(8,128)S(1)} %get-tuple-element.27.fields.refs_0_, f32[976,128]{1,0:T(8,128)S(1)} %shard_map.85.keep, f32[2048,128]{1,0:T(8,128)S(1)} %shard_map.86.force_in, f32[10,8,256]{2,1,0:T(8,128)S(1)} %collective-permute-done.got_a.col_a, ...), custom_call_target="tpu_custom_call" | custom-call | flops 1048576 | bytes 1048576 | tf_op jit(solution)/shard_map/pallas_call | solution.py:810
  13.6 12.4 %all_to_all.10.got = f32[32,1,128]{2,1,0:T(1,128)S(1)} all-to-all(f32[32,1,128]{2,1,0:T(1,128)S(1)} %get-tuple-element.40), channel_id=1, replica_groups=mesh['slab'=8,'col'=4] {'slab','col'}, dimensions={0} | all-to-all | bytes 32768 | tf_op jit(solution)/shard_map/all_to_all | solution.py:817
  26.1 1.2 %shard_map.88 = (f32[3024,128]{1,0:T(8,128)S(1)}, f32[8,8,256]{2,1,0:T(8,128)S(1)}, f32[8,8,256]{2,1,0:T(8,128)S(1)}) custom-call(f32[32,1,128]{2,1,0:T(1,128)S(1)} %all_to_all.10.got, f32[3536,128]{1,0:T(8,128)S(1)} %get-tuple-element.41.grown), custom_call_target="tpu_custom_call" | custom-call | flops 1048576 | bytes 1048576 | tf_op jit(solution)/shard_map/pallas_call | solution.py:819
  27.3 0.6 %collective-permute-start.8 = (f32[8,8,256]{2,1,0:T(8,128)S(1)}, f32[8,8,256]{2,1,0:T(8,128)S(1)}, u32[]{:S(2)}, u32[]{:S(2)}) collective-permute-start(f32[8,8,256]{2,1,0:T(8,128)S(1)} %get-tuple-element.45), channel_id=1, source_target_pairs={{0,4},{4,0},{8,12},{12,8},{16,20},{20,16},{24,28},{28,24},{1,5},{5... | collective-permute-start | bytes 196616 | tf_op jit(solution)/shard_map/ppermute | solution.py:731
  27.9 0.0 collective-permute-start.9
  27.9 0.1 shard_map.90
  28.0 0.6 %collective-permute-start.6 = (f32[8,8,256]{2,1,0:T(8,128)S(1)}, f32[8,8,256]{2,1,0:T(8,128)S(1)}, u32[]{:S(2)}, u32[]{:S(2)}) collective-permute-start(f32[8,8,256]{2,1,0:T(8,128)S(1)} %get-tuple-element.43), channel_id=1, source_target_pairs={{0,1},{1,0},{2,3},{3,2},{4,5},{5,4},{6,7},{7,6},{8,9},{9,8},{10,11... | collective-permute-start | bytes 196616 | tf_op jit(solution)/shard_map/ppermute | solution.py:719
  28.6 0.3 collective-permute-start.7
  28.9 0.7 %shard_map.89.force_in = f32[2048,128]{1,0:T(8,128)S(1)} custom-call(f32[3024,128]{1,0:T(8,128)S(1)} %get-tuple-element.42.refs_0_.fields.keep), custom_call_target="tpu_custom_call" | custom-call | flops 8388608 | bytes 4194304 | tf_op jit(solution)/shard_map/pallas_call | solution.py:802
  29.6 2.0 %collective-permute-done.8.slab_a = f32[8,8,256]{2,1,0:T(8,128)S(1)} collective-permute-done((f32[8,8,256]{2,1,0:T(8,128)S(1)}, f32[8,8,256]{2,1,0:T(8,128)S(1)}, u32[]{:S(2)}, u32[]{:S(2)}) %collective-permute-start.8) | collective-permute-done | bytes 65568 | tf_op jit(solution)/shard_map/ppermute | solution.py:731
  31.6 0.0 collective-permute-done.9.slab_b
  31.6 1.1 %collective-permute-done.7.col_b = f32[8,8,256]{2,1,0:T(8,128)S(1)} collective-permute-done((f32[8,8,256]{2,1,0:T(8,128)S(1)}, f32[8,8,256]{2,1,0:T(8,128)S(1)}, u32[]{:S(2)}, u32[]{:S(2)}) %collective-permute-start.7) | collective-permute-done | bytes 65568 | tf_op jit(solution)/shard_map/ppermute | solution.py:719
  32.7 0.8 %shard_map.91 = (f32[3536,128]{1,0:T(8,128)S(1)}, f32[32,1,128]{2,1,0:T(1,128)S(1)}) custom-call(f32[3024,128]{1,0:T(8,128)S(1)} %get-tuple-element.42.refs_0_.fields.keep, f32[3024,128]{1,0:T(8,128)S(1)} %get-tuple-element.42.refs_0_.fields.keep, f32[2048,128]{1,0:T(8,128)S(1)} %shard_map.89.force_in, f32[8,8,256]{2,1,0:T(8,128)S(1)} %collective-permute-done.6.col_a, ...), custom_call_target="tpu_custom_call" | custom-call | flops 1048576 | bytes 1048576 | tf_op jit(solution)/shard_map/pallas_call | solution.py:810
  33.5 9.6 %all_to_all.11.got = f32[32,1,128]{2,1,0:T(1,128)S(1)} all-to-all(f32[32,1,128]{2,1,0:T(1,128)S(1)} %get-tuple-element.47), channel_id=1, replica_groups=mesh['slab'=8,'col'=4] {'slab','col'}, dimensions={0} | all-to-all | bytes 32768 | tf_op jit(solution)/shard_map/all_to_all | solution.py:817
  43.1 2.2 %shard_map.92 = f32[16,64,256]{2,1,0:T(8,128)} custom-call(f32[32,1,128]{2,1,0:T(1,128)S(1)} %all_to_all.11.got, f32[3536,128]{1,0:T(8,128)S(1)} %get-tuple-element.48.grown), custom_call_target="tpu_custom_call" | custom-call | flops 1048576 | bytes 1048576 | tf_op jit(solution)/shard_map/pallas_call | solution.py:831
  (5 shorter events, 0.0 us)
Async XLA Ops:
  1.8 10.6 %copy-start = (bf16[128,256]{1,0:T(8,128)(2,1)S(1)}, bf16[128,256]{1,0:T(8,128)(2,1)}, u32[]{:S(2)}) copy-start(bf16[128,256]{1,0:T(8,128)(2,1)} %constant.5.clone.height) | copy-start | bytes 196612
  1.8 10.6 %copy-start.1 = (bf16[96,48]{1,0:T(8,128)(2,1)S(1)}, bf16[96,48]{1,0:T(8,128)(2,1)}, u32[]{:S(2)}) copy-start(bf16[96,48]{1,0:T(8,128)(2,1)} %constant.4.clone.weights) | copy-start | bytes 27652
  1.8 4.8 %collective-permute-start = (f32[10,8,256]{2,1,0:T(8,128)S(1)}, f32[10,8,256]{2,1,0:T(8,128)S(1)}, u32[]{:S(2)}, u32[]{:S(2)}) collective-permute-start(f32[10,8,256]{2,1,0:T(8,128)S(1)} %get-tuple-element.29), channel_id=1, source_target_pairs={{0,1},{1,0},{2,3},{3,2},{4,5},{5,4},{6,7},{7,6},{8,9},{9,8},{10,11... | collective-permute-start | bytes 245768 | tf_op jit(solution)/shard_map/ppermute | solution.py:719
  2.3 5.4 %collective-permute-start.1 = (f32[10,8,256]{2,1,0:T(8,128)S(1)}, f32[10,8,256]{2,1,0:T(8,128)S(1)}, u32[]{:S(2)}, u32[]{:S(2)}) collective-permute-start(f32[10,8,256]{2,1,0:T(8,128)S(1)} %get-tuple-element.30), channel_id=1, source_target_pairs={{0,3},{1,2},{2,1},{3,0},{4,7},{5,6},{6,5},{7,4},{8,11},{9,10},{10,... | collective-permute-start | bytes 245768 | tf_op jit(solution)/shard_map/ppermute | solution.py:719
  5.1 6.4 %collective-permute-start.4 = (f32[9,8,256]{2,1,0:T(8,128)S(1)}, f32[9,8,256]{2,1,0:T(8,128)S(1)}, u32[]{:S(2)}, u32[]{:S(2)}) collective-permute-start(f32[9,8,256]{2,1,0:T(8,128)S(1)} %get-tuple-element.38), channel_id=1, source_target_pairs={{0,4},{4,0},{8,12},{12,8},{16,20},{20,16},{24,28},{28,24},{1,5},{5... | collective-permute-start | bytes 221192 | tf_op jit(solution)/shard_map/ppermute | solution.py:731
  6.6 4.8 %collective-permute-start.5 = (f32[9,8,256]{2,1,0:T(8,128)S(1)}, f32[9,8,256]{2,1,0:T(8,128)S(1)}, u32[]{:S(2)}, u32[]{:S(2)}) collective-permute-start(f32[9,8,256]{2,1,0:T(8,128)S(1)} %get-tuple-element.39), channel_id=1, source_target_pairs={{0,1},{1,0},{2,3},{3,2},{4,8},{5,9},{6,10},{7,11},{8,4},{9,5},{10,... | collective-permute-start | bytes 221192 | tf_op jit(solution)/shard_map/ppermute | solution.py:731
  7.7 3.7 %collective-permute-start.2 = (f32[8,256]{1,0:T(8,128)S(1)}, f32[8,256]{1,0:T(8,128)S(1)}, u32[]{:S(2)}, u32[]{:S(2)}) collective-permute-start(f32[8,256]{1,0:T(8,128)S(1)} %get-tuple-element.36), channel_id=1, source_target_pairs={{0,1},{1,0},{2,3},{3,2},{4,8},{5,9},{6,10},{7,11},{8,4},{9,5},{10,... | collective-permute-start | bytes 24584 | tf_op jit(solution)/shard_map/ppermute | solution.py:731
  7.9 4.5 %collective-permute-start.3 = (f32[8,256]{1,0:T(8,128)S(1)}, f32[8,256]{1,0:T(8,128)S(1)}, u32[]{:S(2)}, u32[]{:S(2)}) collective-permute-start(f32[8,256]{1,0:T(8,128)S(1)} %get-tuple-element.37), channel_id=1, source_target_pairs={{0,4},{4,0},{8,12},{12,8},{16,20},{20,16},{24,28},{28,24},{1,5},{5... | collective-permute-start | bytes 24584 | tf_op jit(solution)/shard_map/ppermute | solution.py:731
  27.3 4.3 %collective-permute-start.8 = (f32[8,8,256]{2,1,0:T(8,128)S(1)}, f32[8,8,256]{2,1,0:T(8,128)S(1)}, u32[]{:S(2)}, u32[]{:S(2)}) collective-permute-start(f32[8,8,256]{2,1,0:T(8,128)S(1)} %get-tuple-element.45), channel_id=1, source_target_pairs={{0,4},{4,0},{8,12},{12,8},{16,20},{20,16},{24,28},{28,24},{1,5},{5... | collective-permute-start | bytes 196616 | tf_op jit(solution)/shard_map/ppermute | solution.py:731
  27.9 3.7 %collective-permute-start.9 = (f32[8,8,256]{2,1,0:T(8,128)S(1)}, f32[8,8,256]{2,1,0:T(8,128)S(1)}, u32[]{:S(2)}, u32[]{:S(2)}) collective-permute-start(f32[8,8,256]{2,1,0:T(8,128)S(1)} %get-tuple-element.46), channel_id=1, source_target_pairs={{0,1},{1,0},{2,3},{3,2},{4,8},{5,9},{6,10},{7,11},{8,4},{9,5},{10,... | collective-permute-start | bytes 196616 | tf_op jit(solution)/shard_map/ppermute | solution.py:731
  28.0 3.6 %collective-permute-start.6 = (f32[8,8,256]{2,1,0:T(8,128)S(1)}, f32[8,8,256]{2,1,0:T(8,128)S(1)}, u32[]{:S(2)}, u32[]{:S(2)}) collective-permute-start(f32[8,8,256]{2,1,0:T(8,128)S(1)} %get-tuple-element.43), channel_id=1, source_target_pairs={{0,1},{1,0},{2,3},{3,2},{4,5},{5,4},{6,7},{7,6},{8,9},{9,8},{10,11... | collective-permute-start | bytes 196616 | tf_op jit(solution)/shard_map/ppermute | solution.py:719
  28.6 4.1 %collective-permute-start.7 = (f32[8,8,256]{2,1,0:T(8,128)S(1)}, f32[8,8,256]{2,1,0:T(8,128)S(1)}, u32[]{:S(2)}, u32[]{:S(2)}) collective-permute-start(f32[8,8,256]{2,1,0:T(8,128)S(1)} %get-tuple-element.44), channel_id=1, source_target_pairs={{0,3},{1,2},{2,1},{3,0},{4,7},{5,6},{6,5},{7,4},{8,11},{9,10},{10,... | collective-permute-start | bytes 196616 | tf_op jit(solution)/shard_map/ppermute | solution.py:719
